TPU v7x, 32 devices: a whole 2x2x4 slice. The times are simulated.
32 devices in a mesh: row: 4 (over y, core), col: 8 (over z, x).
Axes of the slice: x: 2, y: 2, z: 4, core: 2. Of those that a mesh axis runs over, the one named last changes fastest.
Arguments:
- inputs: bfloat16 [1024, 8192], P('col', 'row'), may hold values from -6 to 6
- grad_out: bfloat16 [1024, 8192], P('col', 'row'), may hold values from -0.59765625 to 0.59765625
- gate_pre: bfloat16 [1024, 14336], P('row', 'col'), may hold values from -9 to 9
- up_pre: bfloat16 [1024, 14336], P('row', 'col'), may hold values from -6 to 6
- w_gate: bfloat16 [8192, 14336], P('row', 'col'), may hold values from -0.125 to 0.125
- w_up: bfloat16 [8192, 14336], P('row', 'col'), may hold values from -0.125 to 0.125
- w_down: bfloat16 [14336, 8192], P('col', 'row'), may hold values from -0.09375 to 0.09375
- mask_gate: int32 [64, 112], P('row', 'col'), may hold values 0 or 1
- mask_up: int32 [64, 112], P('row', 'col'), may hold values 0 or 1
- mask_down: int32 [112, 64], P('col', 'row'), may hold values 0 or 1
Outputs:
- grad_inputs: bfloat16 [1024, 8192], P('col', 'row')
- grad_gate: bfloat16 [8192, 14336], P('row', 'col')
- grad_up: bfloat16 [8192, 14336], P('row', 'col')
- grad_down: bfloat16 [14336, 8192], P('col', 'row')
All inputs are finite; a program needn't handle non-finite values. No bound on the sum of `mask_gate` or of `mask_up` or of `mask_down` on one device may be relied on, other than what follows from the above.
Results may differ from a plain program's by a relative error of at most 0.005.
Values may be sent and summed in bfloat16 or wider, within the bound.
No kernel may reach another device: no remote copies, remote signals or barrier semaphores. Data moves between devices by JAX's collectives and lax.ppermute only.
A program may use at most 128 MiB of HBM per device.

v0:
```python
import jax
import jax.numpy as jnp
from jax import lax
from jax.sharding import PartitionSpec as P


def expand(mask, block):
    return jnp.repeat(jnp.repeat(mask, block, 0), block, 1).astype(jnp.bfloat16)


def swiglu_grads(hidden_grad, gate_pre, up_pre):
    gated = gate_pre.astype(jnp.float32)
    upper = up_pre.astype(jnp.float32)
    sigma = jax.nn.sigmoid(gated)
    act = (gated * sigma * upper).astype(jnp.bfloat16)
    grad_g = (hidden_grad * upper * sigma * (1.0 + gated * (1.0 - sigma))).astype(jnp.bfloat16)
    grad_u = (hidden_grad * gated * sigma).astype(jnp.bfloat16)
    return (act, grad_g, grad_u)


def per_device(
    inputs, grad_out, gate_pre, up_pre, w_gate, w_up, w_down, mask_gate, mask_up, mask_down
):
    block = w_gate.shape[0] // mask_gate.shape[0]
    keep_gate = expand(mask_gate, block)
    keep_up = expand(mask_up, block)
    keep_down = expand(mask_down, block)
    gate_eff = w_gate * keep_gate
    up_eff = w_up * keep_up
    down_eff = w_down * keep_down
    contract = (((1,), (1,)), ((), ()))
    tokens_dim = (((0,), (0,)), ((), ()))
    grad_all = lax.all_gather(grad_out, "col", axis=0, tiled=True)
    hidden_grad = lax.psum_scatter(
        lax.dot_general(grad_all, down_eff, contract, preferred_element_type=jnp.float32),
        "row",
        scatter_dimension=0,
        tiled=True,
    )
    act, grad_g, grad_u = swiglu_grads(hidden_grad, gate_pre, up_pre)
    act_all, grad_g_all, grad_u_all = (
        lax.all_gather(act, "row", axis=0, tiled=True),
        lax.all_gather(grad_g, "row", axis=0, tiled=True),
        lax.all_gather(grad_u, "row", axis=0, tiled=True),
    )
    first = lax.dot_general(grad_g_all, gate_eff, contract, preferred_element_type=jnp.float32)
    grad_inputs = lax.psum_scatter(
        first + lax.dot_general(grad_u_all, up_eff, contract, preferred_element_type=jnp.float32),
        "col",
        scatter_dimension=0,
        tiled=True,
    ).astype(jnp.bfloat16)
    grad_down = lax.dot_general(act_all, grad_all, tokens_dim, preferred_element_type=jnp.float32)
    grad_down = (grad_down * keep_down.astype(jnp.float32)).astype(jnp.bfloat16)
    input_all = lax.all_gather(inputs, "col", axis=0, tiled=True)
    grad_gate = lax.dot_general(
        input_all, grad_g_all, tokens_dim, preferred_element_type=jnp.float32
    )
    grad_gate = (grad_gate * keep_gate.astype(jnp.float32)).astype(jnp.bfloat16)
    grad_up = lax.dot_general(input_all, grad_u_all, tokens_dim, preferred_element_type=jnp.float32)
    grad_up = (grad_up * keep_up.astype(jnp.float32)).astype(jnp.bfloat16)
    return (grad_inputs, grad_gate, grad_up, grad_down)


def solution(mesh):
    placed = (
        P("col", "row"),
        P("col", "row"),
        P("row", "col"),
        P("row", "col"),
        P("row", "col"),
        P("row", "col"),
        P("col", "row"),
        P("row", "col"),
        P("row", "col"),
        P("col", "row"),
    )
    return jax.shard_map(
        per_device,
        mesh=mesh,
        in_specs=placed,
        out_specs=(P("col", "row"), P("row", "col"), P("row", "col"), P("col", "row")),
        check_vma=False,
    )
```

profile of v0, /device:TPU:0, one launch (start us, length us, event | category | flops | bytes accessed | tf_op | source)
XLA Modules:
  0.0 516.3 jit_solution(15862770175255840883)
XLA Ops:
  7.2 0.7 all-gather.6.cloned.1.call-update
  7.9 0.7 convert_element_type.69
  8.6 77.6 %all-gather.6.cloned.1.call-done = bf16[1024,2048]{1,0:T(8,128)(2,1)} async-done(((bf16[128,2048]{1,0:T(8,128)(2,1)}), bf16[1024,2048]{1,0:T(8,128)(2,1)}) %all-gather.6.cloned.1.call-update) | async-done | bytes 4194320 | tf_op jit(solution)/shard_map/all_gather | solution.py:33
  86.3 11.2 %broadcast_in_dim.19 = bf16[1792,16,128]{2,1,0:T(8,128)(2,1)S(1)} broadcast(bf16[1792,16]{1,0:T(8,128)(2,1)S(1)} %bitcast.49), dimensions={0,1} | broadcast | bytes 7397376 | tf_op jit(solution)/shard_map/broadcast_in_dim | solution.py:8
  97.5 3.0 copy-done.1
  100.5 12.1 %fusion.4 = f32[1024,1792]{0,1:T(8,128)} fusion(bf16[1024,2048]{1,0:T(8,128)(2,1)} %all-gather.6.cloned.1.call-done, bf16[1792,2048]{1,0:T(8,128)(2,1)S(1)} %copy-done.6, bf16[224,8,16,128]{3,2,1,0:T(8,128)(2,1)S(1)} %bitcast.47), kind=kOutput, calls=%fused_computation.10 | convolution fusion | flops 7519862784 | bytes 26214400 | tf_op jit(solution)/shard_map/dot_general | solution.py:35
  112.6 1.1 copy-done.2
  113.7 0.5 copy.14
  114.3 0.5 copy.15
  114.8 61.7 %reduce-scatter.3.cloned.1.call-done = f32[256,1792]{0,1:T(8,128)} async-done(((f32[1024,1792]{0,1:T(8,128)}), f32[256,1792]{0,1:T(8,128)}) %reduce-scatter.3.cloned.1.call-update) | async-done | bytes 1835024 | tf_op jit(solution)/shard_map/reduce_scatter | solution.py:34
  176.5 4.2 fusion.14
  180.7 0.5 all-gather.10.cloned.1.call-update
  181.3 0.5 all-gather.12.cloned.1.call-update
  181.9 0.5 all-gather.14.cloned.1.call-update
  182.4 0.2 reduce-scatter.5.cloned.1.call-start
  182.8 0.1 broadcast_bitcast_fusion.1
  182.9 10.6 %copy.17 = bf16[2048,1792]{0,1:T(8,128)(2,1)} copy(bf16[2048,1792]{1,0:T(8,128)(2,1)} %param.14) | data formatting | bytes 14680064 | tf_op args[4]
  193.6 0.1 broadcast_bitcast_fusion
  193.7 10.5 %copy.19 = bf16[2048,1792]{0,1:T(8,128)(2,1)} copy(bf16[2048,1792]{1,0:T(8,128)(2,1)} %param.15) | data formatting | bytes 14680064 | tf_op args[5]
  204.2 6.8 %bitcast_multiply_fusion.3 = bf16[2048,1792]{0,1:T(8,128)(2,1)} fusion(bf16[2048,1792]{0,1:T(8,128)(2,1)} %copy.17, bf16[2048,14]{0,1:T(8,128)(2,1)S(1)} %bitcast.50), kind=kLoop, calls=%fused_computation.6 | loop fusion | flops 3670016 | bytes 14737408 | tf_op jit(solution)/shard_map/mul | solution.py:28
  211.0 3.6 bitcast_multiply_fusion.2
  214.6 13.2 %fusion.15 = f32[1024,2048]{1,0:T(8,128)} fusion(bf16[1024,1792]{0,1:T(8,128)(2,1)} %all-gather.8.cloned.1.call-done, bf16[2048,1792]{0,1:T(8,128)(2,1)} %bitcast_multiply_fusion.3), kind=kOutput, calls=%fused_computation.30 | convolution fusion | flops 7516192768 | bytes 19398656 | tf_op jit(solution)/shard_map/dot_general | solution.py:46
  227.8 19.1 %all-gather.10.cloned.1.call-done = bf16[1024,1792]{0,1:T(8,128)(2,1)} async-done(((bf16[256,1792]{0,1:T(8,128)(2,1)}), bf16[1024,1792]{0,1:T(8,128)(2,1)}) %all-gather.10.cloned.1.call-update) | async-done | bytes 3670032 | tf_op jit(solution)/shard_map/all_gather | solution.py:44
  246.9 14.4 %convolution_add_fusion = f32[1024,2048]{1,0:T(8,128)} fusion(f32[1024,2048]{1,0:T(8,128)} %fusion.15, bf16[1024,1792]{0,1:T(8,128)(2,1)} %all-gather.10.cloned.1.call-done, bf16[2048,1792]{0,1:T(8,128)(2,1)} %bitcast_multiply_fusion.2), kind=kOutput, calls=%fused_computation.11 | convolution fusion | flops 7518289920 | bytes 27787264 | tf_op jit(solution)/shard_map/dot_general | solution.py:48
  261.3 61.2 %all-gather.12.cloned.1.call-done = bf16[1024,2048]{1,0:T(8,128)(2,1)} async-done(((bf16[128,2048]{1,0:T(8,128)(2,1)}), bf16[1024,2048]{1,0:T(8,128)(2,1)}) %all-gather.12.cloned.1.call-update) | async-done | bytes 4194320 | tf_op jit(solution)/shard_map/all_gather | solution.py:55
  322.5 12.5 %fusion.1 = bf16[2048,1792]{0,1:T(8,128)(2,1)} fusion(bf16[1024,1792]{0,1:T(8,128)(2,1)} %all-gather.8.cloned.1.call-done, bf16[1024,2048]{1,0:T(8,128)(2,1)} %all-gather.12.cloned.1.call-done, bf16[2048,14]{0,1:T(8,128)(2,1)S(1)} %bitcast.51), kind=kOutput, calls=%fused_computation.3 | convolution fusion | flops 7527202816 | bytes 15261696 | tf_op jit(solution)/shard_map/dot_general | solution.py:56
  335.0 9.9 %copy.20 = bf16[2048,1792]{1,0:T(8,128)(2,1)} copy(bf16[2048,1792]{0,1:T(8,128)(2,1)} %fusion.1) | data formatting | bytes 14680064
  344.9 12.5 %fusion = bf16[2048,1792]{0,1:T(8,128)(2,1)} fusion(bf16[1024,1792]{0,1:T(8,128)(2,1)} %all-gather.10.cloned.1.call-done, bf16[1024,2048]{1,0:T(8,128)(2,1)} %all-gather.12.cloned.1.call-done, bf16[2048,14]{0,1:T(8,128)(2,1)S(1)} %bitcast.53), kind=kOutput, calls=%fused_computation.1 | convolution fusion | flops 7527202816 | bytes 15261696 | tf_op jit(solution)/shard_map/dot_general | solution.py:60
  357.4 10.1 %copy.21 = bf16[2048,1792]{1,0:T(8,128)(2,1)} copy(bf16[2048,1792]{0,1:T(8,128)(2,1)} %fusion) | data formatting | bytes 14680064
  367.5 14.0 %multiply_convert_fusion = bf16[1792,2048]{1,0:T(8,128)(2,1)} fusion(bf16[1024,1792]{0,1:T(8,128)(2,1)} %all-gather.14.cloned.1.call-done, bf16[1024,2048]{1,0:T(8,128)(2,1)} %all-gather.6.cloned.1.call-done, bf16[224,8,16,128]{3,2,1,0:T(8,128)(2,1)} %bitcast.48), kind=kOutput, calls=%fused_computation.4 | convolution fusion | flops 7527202816 | bytes 22544384 | tf_op jit(solution)/shard_map/dot_general | solution.py:53
  381.6 125.8 %reduce-scatter.5.cloned.1.call-done = f32[128,2048]{1,0:T(8,128)} async-done(((f32[1024,2048]{1,0:T(8,128)}), f32[128,2048]{1,0:T(8,128)}) %reduce-scatter.5.cloned.1.call-update) | async-done | bytes 1048592 | tf_op jit(solution)/shard_map/reduce_scatter | solution.py:47
  507.4 2.1 convert_element_type.82
  (32 shorter events, 0.6 us)
Async XLA Ops:
  7.2 79.1 %all-gather.6.cloned.1.call-start = ((), (), s32[]{:S(2)}) async-start(), calls=%async_computation.2 | async-start | bytes 4718592 | tf_op jit(solution)/shard_map/all_gather | solution.py:33
  7.9 168.6 %reduce-scatter.3.cloned.1.call-start = ((), (), s32[]{:S(2)}) async-start(), calls=%async_computation.3 | async-start | bytes 9175040 | tf_op jit(solution)/shard_map/reduce_scatter | solution.py:34
  86.3 14.2 %copy-start.6 = (bf16[1792,2048]{1,0:T(8,128)(2,1)S(1)}, bf16[1792,2048]{1,0:T(8,128)(2,1)}, u32[]{:S(2)}) copy-start(bf16[1792,2048]{1,0:T(8,128)(2,1)} %param.16) | copy-start | bytes 22020100
  97.5 3.0 copy-start.1
  112.6 1.2 copy-start.2
  112.6 1.7 copy-start.3
  112.6 70.1 %copy-start.4 = (s32[16,14]{1,0:T(8,128)S(1)}, s32[16,14]{1,0:T(8,128)}, u32[]{:S(2)}) copy-start(s32[16,14]{1,0:T(8,128)} %param.17) | copy-start | bytes 2692
  112.6 102.0 %all-gather.8.cloned.1.call-start = ((), (), s32[]{:S(2)}) async-start(), calls=%async_computation.4 | async-start | bytes 4587520 | tf_op jit(solution)/shard_map/all_gather | solution.py:43
  180.7 66.2 %all-gather.10.cloned.1.call-start = ((), (), s32[]{:S(2)}) async-start(), calls=%async_computation.5 | async-start | bytes 4587520 | tf_op jit(solution)/shard_map/all_gather | solution.py:44
  181.3 141.2 %all-gather.12.cloned.1.call-start = ((), (), s32[]{:S(2)}) async-start(), calls=%async_computation.7 | async-start | bytes 4718592 | tf_op jit(solution)/shard_map/all_gather | solution.py:55
  181.9 185.7 %all-gather.14.cloned.1.call-start = ((), (), s32[]{:S(2)}) async-start(), calls=%async_computation.8 | async-start | bytes 4587520 | tf_op jit(solution)/shard_map/all_gather | solution.py:42
  182.4 325.0 %reduce-scatter.5.cloned.1.call-start = ((), (), s32[]{:S(2)}) async-start(), calls=%async_computation.6 | async-start | bytes 9437184 | tf_op jit(solution)/shard_map/reduce_scatter | solution.py:47
  182.9 10.6 %copy-start.5 = (s32[16,14]{1,0:T(8,128)S(1)}, s32[16,14]{1,0:T(8,128)}, u32[]{:S(2)}) copy-start(s32[16,14]{1,0:T(8,128)} %param.18) | copy-start | bytes 2692
  204.2 6.8 %copy-start = (bf16[2048,1792]{0,1:T(8,128)(2,1)S(1)}, bf16[2048,1792]{0,1:T(8,128)(2,1)}, u32[]{:S(2)}) copy-start(bf16[2048,1792]{0,1:T(8,128)(2,1)} %copy.19) | copy-start | bytes 22020100
Sparse Core Ops, SparseCore 0:
  10.1 76.0 all-gather.5
  112.7 63.7 reduce-scatter.2
  180.8 31.9 all-gather.7
  214.9 31.9 all-gather.9
  249.1 73.3 all-gather.11
  324.0 30.2 all-gather.13
  358.3 149.0 reduce-scatter.4
where the time goes:
time: 517 us; the launch traced here: 516 us
  waiting for transfers between devices  348 us (67%)
  matrix products  78.7 us (15%)
  local copies, waits for them, and re-layouts  57.9 us (11%)
  other arithmetic  17.3 us (3%)
  between operations  14.3 us (3%)
    reduce_scatter x1, waiting for transfers between devices, per_device(): lax.psum_scatter(first + lax.dot_general(grad_u_all, up_eff, contract, pr...  126 us
    all_gather x1, waiting for transfers between devices, per_device(): grad_all = lax.all_gather(grad_out, 'col', axis=0, tiled=True)  77.6 us
    reduce_scatter x1, waiting for transfers between devices, per_device(): lax.psum_scatter(lax.dot_general(grad_all, down_eff, contract, preferred_...  61.7 us
    all_gather x1, waiting for transfers between devices, per_device(): input_all = lax.all_gather(inputs, 'col', axis=0, tiled=True)  61.2 us
    unnamed x26, local copies, waits for them, and re-layouts  46.5 us
    all_gather x1, waiting for transfers between devices, per_device(): lax.all_gather(grad_u, 'row', axis=0, tiled=True)  19.1 us
    dot_general x1, matrix products, per_device(): lax.dot_general(grad_u_all, up_eff, contract, preferred_element_type=jnp....  14.4 us
    dot_general x1, matrix products, per_device(): lax.dot_general(act_all, grad_all, tokens_dim, preferred_element_type=jnp...  14 us
  transfers between devices with their start and end apart: 7, of which 5 were waited for; matrix products, arithmetic and copies ran while one was open for 23% of the time, Pallas kernels for 0%

commit v1 on v0

v1 whole, which is shorter than its diff:
```python
import functools

import jax
import jax.numpy as jnp
from jax import lax
from jax.experimental import pallas as pl
from jax.experimental.pallas import tpu as pltpu
from jax.sharding import PartitionSpec as P

F32 = jnp.float32
BF16 = jnp.bfloat16
MIB = 1024 * 1024
NT = (((1,), (1,)), ((), ()))
NN = (((1,), (0,)), ((), ()))


def params(mib):
    return pltpu.CompilerParams(vmem_limit_bytes=mib * MIB)


def cost(flops, nbytes):
    return pl.CostEstimate(flops=flops // 4096, bytes_accessed=nbytes // 4096, transcendentals=0)


def smem_spec():
    return pl.BlockSpec(memory_space=pltpu.SMEM)


def whole_spec(x):
    return pl.BlockSpec(x.shape, lambda *_: (0,) * x.ndim, pipeline_mode=pl.Buffered(1))


def in_hbm(x):
    return pltpu.with_memory_space_constraint(x, pltpu.HBM)


def stack_rows(dst_ref, refs):
    at = 0
    for r in refs:
        dst_ref[at : at + r.shape[0]] = r[...]
        at += r.shape[0]


def tile_copy(w_ref, dst_ref, sem_ref, t):
    rows = dst_ref.shape[1]
    at = pl.ds(pl.multiple_of(t * rows, rows), rows)
    return pltpu.make_async_copy(w_ref.at[at], dst_ref.at[t], sem_ref.at[t])


def apply_mask(dst_ref, w_ref, m_ref, i, blk):
    for a in range(2):
        for j in range(w_ref.shape[1] // blk):
            keep = m_ref[2 * i + a, j].astype(F32).astype(BF16)
            ra, cj = slice(a * blk, (a + 1) * blk), slice(j * blk, (j + 1) * blk)
            dst_ref[ra, cj] = w_ref[ra, cj] * keep


def hidden_part(where, first, second, w, mask, swap):
    h, d = w.shape
    blk = h // mask.shape[0]
    m = first.shape[0]
    tile = 2 * blk

    def body(at_ref, m_ref, w_ref, a_ref, b_ref, keep_ref, send_ref, rows_ref, eff_ref, all_ref, sem_ref, row_sem):
        j = pl.program_id(0)

        @pl.when(j == 0)
        def _():
            rows = [
                pltpu.make_async_copy(x, rows_ref.at[pl.ds(i * m, m)], row_sem.at[i])
                for i, x in enumerate((a_ref, b_ref))
            ]
            for copy in rows:
                copy.start()
            for t in range(h // tile):
                tile_copy(w_ref, all_ref, sem_ref, t).start()
            for copy in rows:
                copy.wait()

        tile_copy(w_ref, all_ref, sem_ref, j).wait()
        apply_mask(eff_ref, all_ref.at[j], m_ref, j, blk)
        out = lax.dot_general(rows_ref[...], eff_ref[...], NT, preferred_element_type=F32)
        one, two = out[:m], out[m:]
        if swap:
            here = at_ref[where.shape[0] - 1] == 0
            one, two = jnp.where(here, one, two), jnp.where(here, two, one)
        keep_ref[...] = one
        send_ref[...] = two.astype(BF16)

    out_spec = pl.BlockSpec((m, tile), lambda j: (0, j))
    return pl.pallas_call(
        body,
        grid=(h // tile,),
        in_specs=[
            smem_spec(),
            smem_spec(),
        ]
        + [pl.BlockSpec(memory_space=pl.ANY)] * 3,
        out_specs=[out_spec, out_spec],
        out_shape=[jax.ShapeDtypeStruct((m, h), F32), jax.ShapeDtypeStruct((m, h), BF16)],
        scratch_shapes=[
            pltpu.VMEM((2 * m, d), BF16),
            pltpu.VMEM((tile, d), BF16),
            pltpu.VMEM((h // tile, tile, d), BF16),
            pltpu.SemaphoreType.DMA((h // tile,)),
            pltpu.SemaphoreType.DMA((2,)),
        ],
        compiler_params=params(16),
        cost_estimate=cost(4 * m * d * h, 2 * d * (m + h) + 6 * m * h),
        name="hidden_part",
    )(where, mask, in_hbm(w), first, second)


def activation(saved, where):
    m, h = saved[0][0].shape
    n = len(saved)
    wide = 256 if h % 256 == 0 else 128

    def body(at_ref, *refs):
        o_ref, buf_ref, sem_ref = refs[2 * n :]
        k = pl.program_id(0)

        def copy(src, i, p):
            return pltpu.make_async_copy(refs[2 * src + p], buf_ref.at[i, p], sem_ref.at[i, p])

        @pl.when(k == 0)
        def _():
            for i in range(n):
                for p in range(2):
                    copy(i, i, p).start()

        for p in range(2):
            copy(0, k, p).wait()
        for c in range(h // wide):
            at = slice(c * wide, (c + 1) * wide)
            g = buf_ref[k, 0, :, at].astype(F32)
            u = buf_ref[k, 1, :, at].astype(F32)
            act = g * (1.0 / (1.0 + jnp.exp(-g))) * u
            o_ref[at, :] = act.astype(BF16).T

    return pl.pallas_call(
        body,
        grid=(n,),
        in_specs=[smem_spec()] + [pl.BlockSpec(memory_space=pl.ANY)] * (2 * n),
        out_specs=pl.BlockSpec((h, m), lambda k: (0, k)),
        out_shape=jax.ShapeDtypeStruct((h, n * m), BF16),
        scratch_shapes=[pltpu.VMEM((n, 2, m, h), BF16), pltpu.SemaphoreType.DMA((n, 2))],
        compiler_params=params(16),
        cost_estimate=cost(10 * h * n * m, 6 * h * n * m),
        name="activation",
    )(where, *[in_hbm(x) for pair in saved for x in pair])


def swiglu_grads(sums, saved, where, n, q):
    m, h = sums[0].shape
    cuts = 2 if (h // 2) % 128 == 0 else 1
    wide = h // cuts
    ns, nt = len(saved), len(sums)

    def body(i_ref, *refs):
        s_refs, t_refs = refs[: 2 * ns], refs[2 * ns : 2 * ns + nt]
        o_ref, s_buf = refs[2 * ns + nt], refs[2 * ns + nt + 1]
        t_bufs = refs[2 * ns + nt + 2 : 2 * ns + 2 * nt + 2]
        o_buf, s_sem, t_sem, o_sem = refs[2 * ns + 2 * nt + 2 :]
        src = i_ref[n] // q
        rows = pl.ds(pl.multiple_of(i_ref[n] % q * m, m), m)

        def saved_copy(c, k, p):
            cols = slice(c * wide, (c + 1) * wide)
            return pltpu.make_async_copy(
                s_refs[2 * k + p].at[rows, cols], s_buf.at[c, p], s_sem.at[c, p]
            )

        def term_copy(c, t):
            cols = slice(c * wide, (c + 1) * wide)
            return pltpu.make_async_copy(t_refs[t].at[:, cols], t_bufs[t].at[c], t_sem.at[c, t])

        def out_copy(c):
            cols = slice(c * wide, (c + 1) * wide)
            return pltpu.make_async_copy(o_buf.at[c], o_ref.at[:, :, cols], o_sem.at[c])

        for c in range(cuts):
            for k in range(ns):

                @pl.when(src == k)
                def _():
                    for p in range(2):
                        saved_copy(c, k, p).start()

            for t in range(nt):
                term_copy(c, t).start()
        for c in range(cuts):
            for p in range(2):
                saved_copy(c, 0, p).wait()
            for t in range(nt):
                term_copy(c, t).wait()
            hg = t_bufs[0][c].astype(F32)
            for t in range(1, nt):
                hg = hg + t_bufs[t][c].astype(F32)
            g = s_buf[c, 0].astype(F32)
            u = s_buf[c, 1].astype(F32)
            sig = 1.0 / (1.0 + jnp.exp(-g))
            hs = hg * sig
            o_buf[c, 0] = (hs * u * (1.0 + g * (1.0 - sig))).astype(BF16)
            o_buf[c, 1] = (hs * g).astype(BF16)
            out_copy(c).start()
        for c in range(cuts):
            out_copy(c).wait()

    anywhere = pl.BlockSpec(memory_space=pl.ANY)
    return pl.pallas_call(
        body,
        in_specs=[smem_spec()] + [anywhere] * (2 * ns + nt),
        out_specs=anywhere,
        out_shape=jax.ShapeDtypeStruct((2, m, h), BF16),
        scratch_shapes=[pltpu.VMEM((cuts, 2, m, wide), BF16)]
        + [pltpu.VMEM((cuts, m, wide), x.dtype) for x in sums]
        + [
            pltpu.VMEM((cuts, 2, m, wide), BF16),
            pltpu.SemaphoreType.DMA((cuts, 2)),
            pltpu.SemaphoreType.DMA((cuts, nt)),
            pltpu.SemaphoreType.DMA((cuts,)),
        ],
        compiler_params=params(8),
        cost_estimate=cost(20 * h * m, 14 * h * m),
        name="swiglu_grads",
    )(where, *[in_hbm(x) for pair in saved for x in pair], *sums)


def turned_weight(w, mask, where):
    d, h = w.shape
    nr, nc = mask.shape
    blk = d // nr
    tile = 2 * blk

    def body(at_ref, m_ref, w_ref, o_ref):
        i = pl.program_id(0)
        for j in range(nc):
            cols = slice(j * blk, (j + 1) * blk)
            halves = []
            for a in range(2):
                keep = m_ref[2 * i + a, j].astype(F32).astype(BF16)
                halves.append(w_ref[a * blk : (a + 1) * blk, cols] * keep)
            o_ref[0, cols, :] = jnp.concatenate(halves, 0).T

    return pl.pallas_call(
        body,
        grid=(d // tile,),
        in_specs=[smem_spec(), smem_spec(), pl.BlockSpec((tile, h), lambda i: (i, 0))],
        out_specs=pl.BlockSpec((1, h, tile), lambda i: (i, 0, 0)),
        out_shape=pltpu.HBM((d // tile, h, tile), BF16),
        compiler_params=params(8),
        cost_estimate=cost(d * h, 4 * d * h),
        name="turned_weight",
    )(where, mask, in_hbm(w))


def input_part(grads, gate_t, up_t, where):
    _, m, h = grads[0].shape
    n = len(grads)
    tiles, _, tile = gate_t.shape
    d = tiles * tile

    def body(at_ref, wg_ref, wu_ref, *refs):
        o_ref, g_ref, u_ref, wg_all, wu_all, g_sem, u_sem, row_sem = refs[n:]
        i = pl.program_id(0)

        def copies(t):
            return (
                pltpu.make_async_copy(wg_ref.at[t], wg_all.at[t], g_sem.at[t]),
                pltpu.make_async_copy(wu_ref.at[t], wu_all.at[t], u_sem.at[t]),
            )

        @pl.when(i == 0)
        def _():
            rows = [
                pltpu.make_async_copy(r.at[p], dst.at[pl.ds(k * m, m)], row_sem.at[p, k])
                for p, dst in enumerate((g_ref, u_ref))
                for k, r in enumerate(refs[:n])
            ]
            for copy in rows:
                copy.start()
            for t in range(tiles):
                for copy in copies(t):
                    copy.start()
            for copy in rows:
                copy.wait()

        for copy in copies(i):
            copy.wait()
        out = lax.dot_general(g_ref[...], wg_all[i], NN, preferred_element_type=F32)
        out = out + lax.dot_general(u_ref[...], wu_all[i], NN, preferred_element_type=F32)
        for k in range(n):
            o_ref[k] = out[k * m : (k + 1) * m]

    anywhere = pl.BlockSpec(memory_space=pl.ANY)
    return pl.pallas_call(
        body,
        grid=(tiles,),
        in_specs=[smem_spec()] + [anywhere] * (2 + n),
        out_specs=pl.BlockSpec((n, m, tile), lambda j: (0, 0, j)),
        out_shape=jax.ShapeDtypeStruct((n, m, d), F32),
        scratch_shapes=[pltpu.VMEM((n * m, h), BF16)] * 2
        + [pltpu.VMEM((tiles, h, tile), BF16)] * 2
        + [pltpu.SemaphoreType.DMA((tiles,))] * 2
        + [pltpu.SemaphoreType.DMA((2, n))],
        compiler_params=params(28),
        cost_estimate=cost(4 * n * m * d * h, 4 * n * m * h + 4 * d * h + 4 * n * m * d),
        name="input_part",
    )(where, in_hbm(gate_t), in_hbm(up_t), *grads)


def weight_grad(lhs, rhs, mask, where, pick=None, places=None):
    lhs = lhs if isinstance(lhs, list) else [lhs]
    rows = lhs[0].shape[0]
    k = sum(x.shape[1] for x in lhs)
    cols = rhs[0].shape[-1]
    nr, nc = mask.shape
    blk = rows // nr
    per = 4 if nr % 4 == 0 else 2
    tile = per * blk
    wide = 2 * blk
    nl, n = len(lhs), len(rhs)

    def body(m_ref, p_ref, *refs):
        lefts, rights = refs[:nl], refs[nl : nl + n]
        o_ref, r_ref, l_ref = refs[nl + n :]
        i = pl.program_id(0)

        @pl.when(i == 0)
        def _():
            if places is None:
                stack_rows(r_ref, [r if pick is None else r.at[0] for r in rights])
            else:
                for t, r in enumerate(rights):
                    m = r.shape[0]
                    r_ref[pl.ds(pl.multiple_of(p_ref[places + t] * m, m), m)] = r[...]

        if nl > 1:
            at = 0
            for r in lefts:
                l_ref[:, at : at + r.shape[1]] = r[...]
                at += r.shape[1]
        left = l_ref if nl > 1 else lefts[0]
        for c in range(cols // wide):
            out = lax.dot_general(
                left[...], r_ref[:, c * wide : (c + 1) * wide], NN, preferred_element_type=F32
            )
            for a in range(per):
                for s in range(2):
                    keep = m_ref[i * per + a, 2 * c + s].astype(F32)
                    ra, cs = slice(a * blk, (a + 1) * blk), slice(s * blk, (s + 1) * blk)
                    at = slice((2 * c + s) * blk, (2 * c + s + 1) * blk)
                    o_ref[ra, at] = (out[ra, cs] * keep).astype(BF16)

    specs = [pl.BlockSpec((tile, x.shape[1]), lambda i: (i, 0)) for x in lhs]
    for r in rhs:
        if pick is None:
            specs.append(whole_spec(r))
        else:
            specs.append(
                pl.BlockSpec(
                    (1,) + r.shape[1:], lambda i: (pick, 0, 0), pipeline_mode=pl.Buffered(1)
                )
            )
    return pl.pallas_call(
        body,
        grid=(rows // tile,),
        in_specs=[smem_spec(), smem_spec()] + specs,
        out_specs=pl.BlockSpec((tile, cols), lambda i: (i, 0)),
        out_shape=jax.ShapeDtypeStruct((rows, cols), BF16),
        scratch_shapes=[
            pltpu.VMEM((k, cols), BF16),
            pltpu.VMEM((tile, k) if nl > 1 else (16, 128), BF16),
        ],
        compiler_params=params(20),
        cost_estimate=cost(2 * rows * cols * k, 2 * (rows * k + cols * k + rows * cols)),
        name="weight_grad",
    )(mask, where, *lhs, *rhs)


def join(*xs):
    return lax.optimization_barrier(xs)


def ring_order(n):
    a = 4 if n % 4 == 0 and n > 4 else 2
    b = n // a
    walk = [(0, j) for j in range(b)]
    for i in range(1, a):
        js = range(b - 1, 0, -1) if i % 2 else range(1, b)
        walk += [(i, j) for j in js]
    walk += [(i, 0) for i in range(a - 1, 0, -1)]
    return [i * b + j for i, j in walk]


def per_device(
    n_row, n_col, inputs, grad_out, gate_pre, up_pre, w_gate, w_up, w_down, mask_gate, mask_up, mask_down
):
    order = ring_order(n_col)
    half = n_col // 2
    ny = n_row // 2
    tpc = inputs.shape[0]
    q = gate_pre.shape[0] // tpc
    row = lax.axis_index("row")
    core = row % 2
    first = core == 0

    def ring_perm(step):
        pairs = []
        for r in range(n_row):
            s = step if r % 2 == 0 else -step
            for p in range(n_col):
                pairs.append((r * n_col + order[p], r * n_col + order[(p + s) % n_col]))
        return pairs

    back, ahead = ring_perm(-1), ring_perm(1)

    def from_ahead(x):
        return lax.ppermute(x, ("row", "col"), back)

    def from_behind(x):
        return lax.ppermute(x, ("row", "col"), ahead)

    def swap_core(x):
        return lax.ppermute(x, "row", [(r, r ^ 1) for r in range(n_row)])

    def shift_y(x, s):
        return lax.ppermute(
            x, "row", [(r, (r // 2 + s) % ny * 2 + r % 2) for r in range(n_row)]
        )

    last = half - 1
    dists = list(range(1, half)) + [0] + [s * d for d in range(1, half) for s in (1, -1)] + [0, half]
    at = lax.iota(jnp.int32, len(dists) + 1)
    dist = jnp.zeros_like(at)
    for i, d in enumerate(dists):
        if d:
            dist = jnp.where(at == i, d, dist)
    dist = jnp.where(at == last, core * half, dist)
    col = lax.axis_index("col")
    pos = sum(jnp.where(col == c, p, 0) for p, c in enumerate(order))
    near = (pos + (1 - 2 * core) * dist + 2 * n_col) % n_col
    block = sum(jnp.where(near == p, c, 0) for p, c in enumerate(order))
    owner = block // q
    s = (row // 2 - owner // 2 + ny) % ny
    e = (owner % 2 + core) % 2
    where = jnp.where(at == len(dists), core, (s * 2 + e) * q + block % q).astype(jnp.int32)

    def spread_y(x):
        return [shift_y(x, s) for s in range(1, ny)]

    go_rows, terms = [], []
    others, own, got, parts = [None] * half, [None] * half, [None] * half, [None] * half

    def hidden(n, x, y, after):
        kept, sent = hidden_part(after, x, y, w_down, mask_down, n == last)
        go_rows.extend([x, y])
        terms.append([kept, swap_core(sent)])

    def chip_sum(n):
        chip = (terms[n][0] + terms[n][1].astype(F32)).astype(BF16)
        return jnp.pad(chip, ((0, 0), (0, 128)))

    def grads(n, after):
        sums = terms[n] + others[n]
        if n == half - 2:
            sums = [in_hbm(x) for x in sums]
        own[n] = swiglu_grads(sums, saved, after, n, q)

    def following(x):
        return join(where, x)[0]

    a, b = from_ahead(grad_out), from_behind(grad_out)
    gate_y, up_y, in_t = spread_y(gate_pre), spread_y(up_pre), inputs.T
    by_core = []
    gate_t = turned_weight(w_gate, mask_gate, where)
    a, b, where, in_t, gate_t, *by_core = join(a, b, where, in_t, gate_t, *by_core)

    up_t, y_core = None, []
    for k in range(2, half + 1):
        na = from_ahead(a)
        nb = from_behind(b) if k < half else b
        after = where
        if k > 2:
            chip = chip_sum(k - 3)
            after = following(chip)
        hidden(k - 2, a, b, after)
        over, more = [], []
        if k > 2:
            over = others[k - 3] = spread_y(chip)
        if k == 2:
            up_t = turned_weight(w_up, mask_up, following(terms[0][0]))
            more = gate_y + up_y + [up_t]
        elif k == 3:
            by_core = [swap_core(gate_pre)]
            more = by_core
        elif k == 4:
            by_core = by_core + [swap_core(up_pre)]
            y_core = [swap_core(x) for x in gate_y + up_y]
            saved = [(gate_pre, up_pre), tuple(by_core)]
            for s in range(ny - 1):
                saved += [(gate_y[s], up_y[s]), (y_core[s], y_core[ny - 1 + s])]
            act_t = activation(saved, following(terms[2][0]))
            more = [act_t]
        out = join(*over, na, nb, where, *more, *terms[k - 2])
        others[k - 3] = list(out[: len(over)]) if over else others[k - 3]
        a, b, where = out[len(over) : len(over) + 3]
        terms[k - 2], more = list(out[-2:]), list(out[len(over) + 3 : -2])
        if k == 2:
            gate_y, up_y, up_t = more[: ny - 1], more[ny - 1 : -1], more[-1]
        elif k == 3:
            by_core = more
        elif k == 4:
            act_t = more[0]
    far, in_t = join(a, in_t)
    ia, ib = from_ahead(in_t), from_behind(in_t)
    chip = chip_sum(half - 2)
    others[half - 2] = spread_y(chip)
    hidden(last, grad_out, far, following(chip))
    after = following(terms[last][0])
    for n in range(half - 2):
        grads(n, after)
        after = following(own[n])
    ia, ib, where, own[half - 3], *rest = join(ia, ib, where, own[half - 3], *others[half - 2])
    others[half - 2] = rest
    in_pairs = [(ia, ib)]

    ia, ib = from_ahead(ia), from_behind(ib)
    chip = chip_sum(last)
    others[last], after = spread_y(chip), following(chip)
    for n in range(half - 2):
        got[n] = swap_core(own[n])
    grad_down = weight_grad(act_t, go_rows, mask_down, after, places=half)
    ia, ib, where, grad_down, *rest = join(ia, ib, where, grad_down, *others[last])
    others[last] = rest
    in_pairs.append((ia, ib))

    for _ in range(2, half - 1):
        ia, ib = from_ahead(ia), from_behind(ib)
        in_pairs.append((ia, ib))
    grads(last, where)
    got[last] = swap_core(own[last])
    grads(half - 2, following(own[last]))
    got[half - 2] = swap_core(own[half - 2])

    def part(ns, after):
        rows = [x for n in ns for x in (own[n], got[n])]
        return input_part(rows, gate_t, up_t, after)

    both = part([last], following(own[half - 2]))
    to_self = jnp.where(first, both[0], both[1])
    to_far = jnp.where(first, both[1], both[0]).astype(BF16)
    to_far, ia, where = join(to_far, ia, where)

    run_a, run_b, in_far = from_behind(to_far), None, from_ahead(ia)
    parts[half - 2] = part([half - 2], where)
    run_a, where, parts[half - 2] = join(run_a, where, parts[half - 2])

    def send_sums(d):
        add_a = parts[d - 1][0] + run_a.astype(F32)
        add_b = parts[d - 1][1] + run_b.astype(F32) if run_b is not None else parts[d - 1][1]
        return from_behind(add_a.astype(BF16)), from_ahead(add_b.astype(BF16))

    run_a, run_b = send_sums(half - 1)
    both = part(list(range(half - 2)), where)
    lefts = [x for pair in in_pairs for x in pair]
    lefts += [jnp.where(first, in_t, in_far), jnp.where(first, in_far, in_t)]
    rights = [x for n in range(half) for x in (own[n], got[n])]
    run_a, run_b, where, both, *lefts = join(run_a, run_b, where, both, *lefts)
    for n in range(half - 2):
        parts[n] = both[2 * n : 2 * n + 2]

    grad_gate = grad_up = None
    for d in range(half - 2, 0, -1):
        run_a, run_b = send_sums(d)
        if d == half - 2:
            grad_gate = weight_grad(lefts, rights, mask_gate, where, 0)
            run_a, run_b, where, grad_gate = join(run_a, run_b, where, grad_gate)
        elif d == half - 3:
            grad_up = weight_grad(lefts, rights, mask_up, where, 1)
    grad_inputs = (to_self + run_a.astype(F32) + run_b.astype(F32)).astype(BF16)
    return (grad_inputs, grad_gate, grad_up, grad_down)


def solution(mesh):
    placed = (
        P("col", "row"),
        P("col", "row"),
        P("row", "col"),
        P("row", "col"),
        P("row", "col"),
        P("row", "col"),
        P("col", "row"),
        P("row", "col"),
        P("row", "col"),
        P("col", "row"),
    )
    return jax.shard_map(
        functools.partial(per_device, mesh.shape["row"], mesh.shape["col"]),
        mesh=mesh,
        in_specs=placed,
        out_specs=(P("col", "row"), P("row", "col"), P("row", "col"), P("col", "row")),
        check_vma=False,
    )
```

time: 517 us -> 186 us (0.36)
  waiting for transfers between devices: 348 us -> 19.2 us
  Pallas kernels: 0 us -> 125 us
  matrix products: 78.7 us -> 0 us
  local copies, waits for them, and re-layouts: 57.9 us -> 5.09 us
  starting transfers between devices: 0.45 us -> 32.9 us
  other arithmetic: 17.3 us -> 2.43 us
  between operations: 14.3 us -> 1.21 us
    reduce_scatter x2 -> x0, waiting for transfers between devices: 188 us -> none  [the longest x1 126 us: per_device(): lax.psum_scatter(first + lax.dot_general(grad_u_all, up_eff, contract, pr...]
    all_gather x5 -> x0, waiting for transfers between devices: 158 us -> none  [the longest x1 77.6 us: per_device(): grad_all = lax.all_gather(grad_out, 'col', axis=0, tiled=True)]
    pallas_call x0 -> x17, Pallas kernels: none -> 125 us  [the longest x3 33.6 us: input_part(): pl.pallas_call(body, grid=(tiles,), in_specs=[smem_spec()] + [anywhere] *...]
    dot_general x6 -> x0, matrix products: 78.7 us -> none  [the longest x1 14.4 us: per_device(): lax.dot_general(grad_u_all, up_eff, contract, preferred_element_type=jnp....]
    unnamed x26 -> x47, local copies, waits for them, and re-layouts: 46.5 us -> 4.89 us
    ppermute x0 -> x39, starting transfers between devices: none -> 32.9 us  [the longest x11 13.3 us: from_ahead(): return lax.ppermute(x, ('row', 'col'), back)]
    ppermute x0 -> x39, waiting for transfers between devices: none -> 19.2 us  [the longest x6 11.5 us: shift_y(): lax.ppermute(x, 'row', [(r, (r // 2 + s) % ny * 2 + r % 2) for r in range...]
    broadcast_in_dim x2 -> x0, local copies, waits for them, and re-layouts: 11.2 us -> none  [expand(): return jnp.repeat(jnp.repeat(mask, block, 0), block, 1).astype(jnp.bfloat16)]
  transfers between devices with their start and end apart: 7 -> 39, of which waited for: 5 -> 10; matrix products, arithmetic and copies ran while one was open for 23% -> 2% of each run, Pallas kernels for 0% -> 66%
where the time goes in v1:
time: 186 us
  Pallas kernels  125 us (67%)
  starting transfers between devices  32.9 us (18%)
  waiting for transfers between devices  19.2 us (10%)
  local copies, waits for them, and re-layouts  5.09 us (3%)
  other arithmetic  2.43 us (1%)
    pallas_call x3, Pallas kernels, input_part(): pl.pallas_call(body, grid=(tiles,), in_specs=[smem_spec()] + [anywhere] *...  33.6 us
    pallas_call x3, Pallas kernels, weight_grad(): pl.pallas_call(body, grid=(rows // tile,), in_specs=[smem_spec(), smem_sp...  33.4 us
    pallas_call x4, Pallas kernels, hidden_part(): pl.pallas_call(body, grid=(h // tile,), in_specs=[smem_spec(), smem_spec(...  24.2 us
    pallas_call x2, Pallas kernels, turned_weight(): pl.pallas_call(body, grid=(d // tile,), in_specs=[smem_spec(), smem_spec(...  18.5 us
    ppermute x11, starting transfers between devices, from_ahead(): return lax.ppermute(x, ('row', 'col'), back)  13.3 us
    ppermute x6, waiting for transfers between devices, shift_y(): lax.ppermute(x, 'row', [(r, (r // 2 + s) % ny * 2 + r % 2) for r in range...  11.5 us
    pallas_call x4, Pallas kernels, swiglu_grads(): pl.pallas_call(body, in_specs=[smem_spec()] + [anywhere] * (2 * ns + nt),...  9.95 us
    ppermute x10, starting transfers between devices, from_behind(): return lax.ppermute(x, ('row', 'col'), ahead)  9.63 us
  transfers between devices with their start and end apart: 39, of which 10 were waited for; matrix products, arithmetic and copies ran while one was open for 2% of the time, Pallas kernels for 66%

profile of v1, /device:TPU:0, one launch (start us, length us, event | category | flops | bytes accessed | tf_op | source)
XLA Modules:
  0.0 185.7 jit_solution(9223089167660916224)
XLA Ops:
  0.6 3.0 %collective-permute-start.4 = (bf16[256,1792]{1,0:T(8,128)(2,1)}, bf16[256,1792]{1,0:T(8,128)(2,1)S(1)}, u32[]{:S(2)}, u32[]{:S(2)}) collective-permute-start(bf16[256,1792]{1,0:T(8,128)(2,1)} %refs_0_.9), channel_id=1, source_target_pairs={{0,16},{8,24},{16,0},{24,8},{1,17},{9,25},{17,1},{25,9},{2,18},{10... | collective-permute-start | bytes 2752520 | tf_op jit(solution)/shard_map/ppermute | solution.py:429
  6.5 9.2 %turned_weight.2.wg_ref = bf16[8,1792,256]{2,1,0:T(8,128)(2,1)} custom-call(s32[13]{0:T(128)S(1)} %compare_select_fusion.14.at_ref.i_ref.p_ref, s32[16,14]{1,0:T(8,128)S(1)} %copy-done.7, bf16[2048,1792]{1,0:T(8,128)(2,1)} %w_ref.6), custom_call_target="tpu_custom_call" | custom-call | flops 896 | bytes 3584 | tf_op jit(solution)/shard_map/turned_weight/pallas_call | solution.py:246
  15.8 2.0 %copy.14 = bf16[128,2048]{0,1:T(8,128)(2,1)} copy(bf16[128,2048]{1,0:T(8,128)(2,1)} %param.10) | data formatting | bytes 1048576 | tf_op args[0]
  20.6 6.0 %hidden_part.4 = (f32[128,1792]{1,0:T(8,128)S(1)}, bf16[128,1792]{1,0:T(8,128)(2,1)S(1)}) custom-call(s32[13]{0:T(128)S(1)} %compare_select_fusion.14.at_ref.i_ref.p_ref, s32[14,16]{1,0:T(8,128)S(1)} %copy-done.6, bf16[1792,2048]{1,0:T(8,128)(2,1)} %w_ref.11, bf16[128,2048]{1,0:T(8,128)(2,1)S(1)} %collective-permute-done.a_ref.refs_1_, ...), custom_call_target="tpu_custom_call" | custom-call | flops 458752 | bytes 2256 | tf_op jit(solution)/shard_map/hidden_part/pallas_call | solution.py:91
  27.2 9.2 %turned_weight.3.wu_ref = bf16[8,1792,256]{2,1,0:T(8,128)(2,1)} custom-call(s32[13]{0:T(128)S(1)} %compare_select_fusion.14.at_ref.i_ref.p_ref, s32[16,14]{1,0:T(8,128)S(1)} %copy-done.9, bf16[2048,1792]{1,0:T(8,128)(2,1)} %w_ref.8), custom_call_target="tpu_custom_call" | custom-call | flops 896 | bytes 3584 | tf_op jit(solution)/shard_map/turned_weight/pallas_call | solution.py:246
  36.5 7.4 %collective-permute-done.5.refs_5_ = bf16[256,1792]{1,0:T(8,128)(2,1)S(1)} collective-permute-done((bf16[256,1792]{1,0:T(8,128)(2,1)}, bf16[256,1792]{1,0:T(8,128)(2,1)S(1)}, u32[]{:S(2)}, u32[]{:S(2)}) %collective-permute-start.5) | collective-permute-done | bytes 917536 | tf_op jit(solution)/shard_map/ppermute | solution.py:429
  43.9 1.8 collective-permute-start.8
  46.2 1.8 collective-permute-start.7
  47.9 6.0 %hidden_part.5 = (f32[128,1792]{1,0:T(8,128)S(1)}, bf16[128,1792]{1,0:T(8,128)(2,1)S(1)}) custom-call(s32[13]{0:T(128)S(1)} %compare_select_fusion.14.at_ref.i_ref.p_ref, s32[14,16]{1,0:T(8,128)S(1)} %copy-done.6, bf16[1792,2048]{1,0:T(8,128)(2,1)} %w_ref.11, bf16[128,2048]{1,0:T(8,128)(2,1)S(1)} %collective-permute-done.2.a_ref.refs_3_, ...), custom_call_target="tpu_custom_call" | custom-call | flops 458752 | bytes 2256 | tf_op jit(solution)/shard_map/hidden_part/pallas_call | solution.py:91
  56.0 2.0 %collective-permute-done.7.refs_10_ = bf16[128,1920]{1,0:T(8,128)(2,1)S(1)} collective-permute-done((bf16[128,1920]{1,0:T(8,128)(2,1)S(1)}, bf16[128,1920]{1,0:T(8,128)(2,1)S(1)}, u32[]{:S(2)}, u32[]{:S(2)}) %collective-permute-start.7) | collective-permute-done | bytes 491552 | tf_op jit(solution)/shard_map/ppermute | solution.py:429
  59.7 1.6 collective-permute-start.12
  61.3 6.0 %hidden_part.6 = (f32[128,1792]{1,0:T(8,128)S(1)}, bf16[128,1792]{1,0:T(8,128)(2,1)S(1)}) custom-call(s32[13]{0:T(128)S(1)} %compare_select_fusion.14.at_ref.i_ref.p_ref, s32[14,16]{1,0:T(8,128)S(1)} %copy-done.6, bf16[1792,2048]{1,0:T(8,128)(2,1)} %w_ref.11, bf16[128,2048]{1,0:T(8,128)(2,1)S(1)} %collective-permute-done.8.a_ref.refs_5_, ...), custom_call_target="tpu_custom_call" | custom-call | flops 458752 | bytes 2256 | tf_op jit(solution)/shard_map/hidden_part/pallas_call | solution.py:91
  69.6 5.2 %activation.1.refs_0_ = bf16[1792,1024]{1,0:T(8,128)(2,1)S(1)} custom-call(s32[13]{0:T(128)S(1)} %compare_select_fusion.14.at_ref.i_ref.p_ref, bf16[256,1792]{1,0:T(8,128)(2,1)} %refs_0_.9, bf16[256,1792]{1,0:T(8,128)(2,1)} %refs_1_.9, bf16[256,1792]{1,0:T(8,128)(2,1)} %copy-done.15, bf16[256,1792]{1,0:T(8,128)(2,1)} %copy-done.16, ...), custom_call_target="tpu_custom_call" | custom-call | flops 4480 | bytes 2688 | tf_op jit(solution)/shard_map/activation/pallas_call | solution.py:141
  74.9 1.6 collective-permute-start.18
  77.6 6.1 %hidden_part.7 = (f32[128,1792]{1,0:T(8,128)S(1)}, bf16[128,1792]{1,0:T(8,128)(2,1)S(1)}) custom-call(s32[13]{0:T(128)S(1)} %compare_select_fusion.14.at_ref.i_ref.p_ref, s32[14,16]{1,0:T(8,128)S(1)} %copy-done.6, bf16[1792,2048]{1,0:T(8,128)(2,1)} %w_ref.11, bf16[128,2048]{1,0:T(8,128)(2,1)S(1)} %copy-done.1, ...), custom_call_target="tpu_custom_call" | custom-call | flops 458752 | bytes 2256 | tf_op jit(solution)/shard_map/hidden_part/pallas_call | solution.py:91
  83.8 2.4 %swiglu_grads.4.refs_0_.refs_8_ = bf16[2,128,1792]{2,1,0:T(8,128)(2,1)S(1)} custom-call(s32[13]{0:T(128)S(1)} %compare_select_fusion.14.at_ref.i_ref.p_ref, bf16[256,1792]{1,0:T(8,128)(2,1)} %refs_0_.9, bf16[256,1792]{1,0:T(8,128)(2,1)} %refs_1_.9, bf16[256,1792]{1,0:T(8,128)(2,1)} %copy-done.15, bf16[256,1792]{1,0:T(8,128)(2,1)} %copy-done.16, ...), custom_call_target="tpu_custom_call" | custom-call | flops 1120 | bytes 784 | tf_op jit(solution)/shard_map/swiglu_grads/pallas_call | solution.py:211
  86.2 2.4 %swiglu_grads.5.refs_2_.refs_10_ = bf16[2,128,1792]{2,1,0:T(8,128)(2,1)S(1)} custom-call(s32[13]{0:T(128)S(1)} %compare_select_fusion.14.at_ref.i_ref.p_ref, bf16[256,1792]{1,0:T(8,128)(2,1)} %refs_0_.9, bf16[256,1792]{1,0:T(8,128)(2,1)} %refs_1_.9, bf16[256,1792]{1,0:T(8,128)(2,1)} %copy-done.15, bf16[256,1792]{1,0:T(8,128)(2,1)} %copy-done.16, ...), custom_call_target="tpu_custom_call" | custom-call | flops 1120 | bytes 784 | tf_op jit(solution)/shard_map/swiglu_grads/pallas_call | solution.py:211
  90.0 1.6 collective-permute-start.21
  92.8 11.1 %weight_grad.3 = bf16[1792,2048]{1,0:T(8,128)(2,1)} custom-call(s32[14,16]{1,0:T(8,128)S(1)} %copy-done.6, s32[13]{0:T(128)S(1)} %compare_select_fusion.14.at_ref.i_ref.p_ref, bf16[1792,1024]{1,0:T(8,128)(2,1)S(1)} %activation.1.refs_0_, bf16[128,2048]{1,0:T(8,128)(2,1)S(1)} %collective-permute-done.a_ref.refs_1_, ...), custom_call_target="tpu_custom_call" | custom-call | flops 1835008 | bytes 3712 | tf_op jit(solution)/shard_map/weight_grad/pallas_call | solution.py:366
  104.6 2.4 %swiglu_grads.6.refs_0_.refs_14_ = bf16[2,128,1792]{2,1,0:T(8,128)(2,1)S(1)} custom-call(s32[13]{0:T(128)S(1)} %compare_select_fusion.14.at_ref.i_ref.p_ref, bf16[256,1792]{1,0:T(8,128)(2,1)} %refs_0_.9, bf16[256,1792]{1,0:T(8,128)(2,1)} %refs_1_.9, bf16[256,1792]{1,0:T(8,128)(2,1)} %copy-done.15, bf16[256,1792]{1,0:T(8,128)(2,1)} %copy-done.16, ...), custom_call_target="tpu_custom_call" | custom-call | flops 1120 | bytes 784 | tf_op jit(solution)/shard_map/swiglu_grads/pallas_call | solution.py:211
  108.3 2.8 %swiglu_grads.7.refs_0_.refs_12_ = bf16[2,128,1792]{2,1,0:T(8,128)(2,1)S(1)} custom-call(s32[13]{0:T(128)S(1)} %compare_select_fusion.14.at_ref.i_ref.p_ref, bf16[256,1792]{1,0:T(8,128)(2,1)} %refs_0_.9, bf16[256,1792]{1,0:T(8,128)(2,1)} %refs_1_.9, bf16[256,1792]{1,0:T(8,128)(2,1)} %copy-done.15, bf16[256,1792]{1,0:T(8,128)(2,1)} %copy-done.16, ...), custom_call_target="tpu_custom_call" | custom-call | flops 1120 | bytes 784 | tf_op jit(solution)/shard_map/swiglu_grads/pallas_call | solution.py:211
  111.5 11.4 %input_part.3 = f32[2,128,2048]{2,1,0:T(8,128)S(1)} custom-call(s32[13]{0:T(128)S(1)} %compare_select_fusion.14.at_ref.i_ref.p_ref, bf16[8,1792,256]{2,1,0:T(8,128)(2,1)} %turned_weight.2.wg_ref, bf16[8,1792,256]{2,1,0:T(8,128)(2,1)} %turned_weight.3.wu_ref, bf16[2,128,1792]{2,1,0:T(8,128)(2,1)S(1)} %swiglu_grads.6.refs_0_.refs_14_, ...), custom_call_target="tpu_custom_call" | custom-call | flops 917504 | bytes 4544 | tf_op jit(solution)/shard_map/input_part/pallas_call | solution.py:297
  123.0 1.6 collective-permute-start.27
  125.1 1.6 collective-permute-start.33
  127.1 8.6 %input_part.4 = f32[2,128,2048]{2,1,0:T(8,128)S(1)} custom-call(s32[13]{0:T(128)S(1)} %compare_select_fusion.14.at_ref.i_ref.p_ref, bf16[8,1792,256]{2,1,0:T(8,128)(2,1)} %turned_weight.2.wg_ref, bf16[8,1792,256]{2,1,0:T(8,128)(2,1)} %turned_weight.3.wu_ref, bf16[2,128,1792]{2,1,0:T(8,128)(2,1)S(1)} %swiglu_grads.7.refs_0_.refs_12_, ...), custom_call_target="tpu_custom_call" | custom-call | flops 917504 | bytes 4544 | tf_op jit(solution)/shard_map/input_part/pallas_call | solution.py:297
  136.0 2.1 %collective-permute-start.29 = (bf16[128,2048]{1,0:T(8,128)(2,1)S(1)}, bf16[128,2048]{1,0:T(8,128)(2,1)S(1)}, u32[]{:S(2)}, u32[]{:S(2)}) collective-permute-start(bf16[128,2048]{1,0:T(8,128)(2,1)S(1)} %fusion.4), channel_id=1, source_target_pairs={{0,1},{1,3},{3,5},{5,7},{7,6},{6,4},{4,2},{2,0},{8,10},{9,8},{11,9... | collective-permute-start | bytes 1572872 | tf_op jit(solution)/shard_map/ppermute | solution.py:423
  138.1 13.6 %input_part.5 = f32[4,128,2048]{2,1,0:T(8,128)S(1)} custom-call(s32[13]{0:T(128)S(1)} %compare_select_fusion.14.at_ref.i_ref.p_ref, bf16[8,1792,256]{2,1,0:T(8,128)(2,1)} %turned_weight.2.wg_ref, bf16[8,1792,256]{2,1,0:T(8,128)(2,1)} %turned_weight.3.wu_ref, bf16[2,128,1792]{2,1,0:T(8,128)(2,1)S(1)} %swiglu_grads.4.refs_0_.refs_8_, ...), custom_call_target="tpu_custom_call" | custom-call | flops 1835008 | bytes 5504 | tf_op jit(solution)/shard_map/input_part/pallas_call | solution.py:297
  151.9 2.8 %collective-permute-done.29 = bf16[128,2048]{1,0:T(8,128)(2,1)S(1)} collective-permute-done((bf16[128,2048]{1,0:T(8,128)(2,1)S(1)}, bf16[128,2048]{1,0:T(8,128)(2,1)S(1)}, u32[]{:S(2)}, u32[]{:S(2)}) %collective-permute-start.29) | collective-permute-done | bytes 524320 | tf_op jit(solution)/shard_map/ppermute | solution.py:423
  155.0 1.6 collective-permute-start.35
  157.1 11.2 %weight_grad.4 = bf16[2048,1792]{1,0:T(8,128)(2,1)} custom-call(s32[16,14]{1,0:T(8,128)S(1)} %copy-done.8, s32[13]{0:T(128)S(1)} %compare_select_fusion.14.at_ref.i_ref.p_ref, bf16[2048,128]{1,0:T(8,128)(2,1)S(1)} %collective-permute-done.18.refs_0_, bf16[2048,128]{1,0:T(8,128)(2,1)S(1)} %copy-done.3, bf16[2048,128]{1,0:T(8,128)(2,1)} %collective-permute-done.21.refs_2_, ...), custom_call_target="tpu_custom_call" | custom-call | flops 1835008 | bytes 3712 | tf_op jit(solution)/shard_map/weight_grad/pallas_call | solution.py:366
  170.4 1.6 collective-permute-start.38
  172.1 11.2 %weight_grad.5 = bf16[2048,1792]{1,0:T(8,128)(2,1)} custom-call(s32[16,14]{1,0:T(8,128)S(1)} %copy-done.9, s32[13]{0:T(128)S(1)} %compare_select_fusion.14.at_ref.i_ref.p_ref, bf16[2048,128]{1,0:T(8,128)(2,1)S(1)} %collective-permute-done.18.refs_0_, bf16[2048,128]{1,0:T(8,128)(2,1)S(1)} %copy-done.3, bf16[2048,128]{1,0:T(8,128)(2,1)} %collective-permute-done.21.refs_2_, ...), custom_call_target="tpu_custom_call" | custom-call | flops 1835008 | bytes 3712 | tf_op jit(solution)/shard_map/weight_grad/pallas_call | solution.py:366
  (126 shorter events, 25.2 us)
Async XLA Ops:
  0.6 26.1 %collective-permute-start.4 = (bf16[256,1792]{1,0:T(8,128)(2,1)}, bf16[256,1792]{1,0:T(8,128)(2,1)S(1)}, u32[]{:S(2)}, u32[]{:S(2)}) collective-permute-start(bf16[256,1792]{1,0:T(8,128)(2,1)} %refs_0_.9), channel_id=1, source_target_pairs={{0,16},{8,24},{16,0},{24,8},{1,17},{9,25},{17,1},{25,9},{2,18},{10... | collective-permute-start | bytes 2752520 | tf_op jit(solution)/shard_map/ppermute | solution.py:429
  3.7 14.8 %collective-permute-start = (bf16[128,2048]{1,0:T(8,128)(2,1)}, bf16[128,2048]{1,0:T(8,128)(2,1)S(1)}, u32[]{:S(2)}, u32[]{:S(2)}) collective-permute-start(bf16[128,2048]{1,0:T(8,128)(2,1)} %refs_7_.1), channel_id=1, source_target_pairs={{0,2},{1,0},{3,1},{5,3},{7,5},{6,7},{4,6},{2,4},{8,9},{9,11},{11,1... | collective-permute-start | bytes 1572872 | tf_op jit(solution)/shard_map/ppermute | solution.py:420
  5.2 13.2 %collective-permute-start.1 = (bf16[128,2048]{1,0:T(8,128)(2,1)}, bf16[128,2048]{1,0:T(8,128)(2,1)S(1)}, u32[]{:S(2)}, u32[]{:S(2)}) collective-permute-start(bf16[128,2048]{1,0:T(8,128)(2,1)} %refs_7_.1), channel_id=1, source_target_pairs={{0,1},{1,3},{3,5},{5,7},{7,6},{6,4},{4,2},{2,0},{8,10},{9,8},{11,9... | collective-permute-start | bytes 1572872 | tf_op jit(solution)/shard_map/ppermute | solution.py:423
  5.7 38.2 %collective-permute-start.5 = (bf16[256,1792]{1,0:T(8,128)(2,1)}, bf16[256,1792]{1,0:T(8,128)(2,1)S(1)}, u32[]{:S(2)}, u32[]{:S(2)}) collective-permute-start(bf16[256,1792]{1,0:T(8,128)(2,1)} %refs_1_.9), channel_id=1, source_target_pairs={{0,16},{8,24},{16,0},{24,8},{1,17},{9,25},{17,1},{25,9},{2,18},{10... | collective-permute-start | bytes 2752520 | tf_op jit(solution)/shard_map/ppermute | solution.py:429
  18.5 25.4 %collective-permute-start.2 = (bf16[128,2048]{1,0:T(8,128)(2,1)S(1)}, bf16[128,2048]{1,0:T(8,128)(2,1)S(1)}, u32[]{:S(2)}, u32[]{:S(2)}) collective-permute-start(bf16[128,2048]{1,0:T(8,128)(2,1)S(1)} %collective-permute-done.a_ref.refs_1_), channel_id=1, source_target_pairs={{0,2},{1,0},{3,1},{5,3},{7,5},{6,7},{4,6},{2,4},{8,9},{9,11},{11,1... | collective-permute-start | bytes 1572872 | tf_op jit(solution)/shard_map/ppermute | solution.py:420
  19.9 24.0 %collective-permute-start.3 = (bf16[128,2048]{1,0:T(8,128)(2,1)S(1)}, bf16[128,2048]{1,0:T(8,128)(2,1)S(1)}, u32[]{:S(2)}, u32[]{:S(2)}) collective-permute-start(bf16[128,2048]{1,0:T(8,128)(2,1)S(1)} %collective-permute-done.1.b_ref.refs_2_), channel_id=1, source_target_pairs={{0,1},{1,3},{3,5},{5,7},{7,6},{6,4},{4,2},{2,0},{8,10},{9,8},{11,9... | collective-permute-start | bytes 1572872 | tf_op jit(solution)/shard_map/ppermute | solution.py:423
  26.6 17.3 %collective-permute-start.6 = (bf16[128,1792]{1,0:T(8,128)(2,1)S(1)}, bf16[128,1792]{1,0:T(8,128)(2,1)S(1)}, u32[]{:S(2)}, u32[]{:S(2)}) collective-permute-start(bf16[128,1792]{1,0:T(8,128)(2,1)S(1)} %get-tuple-element.87), channel_id=1, source_target_pairs={{0,8},{8,0},{16,24},{24,16},{1,9},{9,1},{17,25},{25,17},{2,10},{10... | collective-permute-start | bytes 1376264 | tf_op jit(solution)/shard_map/ppermute | solution.py:426
  26.7 27.4 %collective-permute-start.10 = (bf16[256,1792]{1,0:T(8,128)(2,1)S(1)}, bf16[256,1792]{1,0:T(8,128)(2,1)S(1)}, u32[]{:S(2)}, u32[]{:S(2)}) collective-permute-start(bf16[256,1792]{1,0:T(8,128)(2,1)S(1)} %copy-done.10), channel_id=1, source_target_pairs={{0,8},{8,0},{16,24},{24,16},{1,9},{9,1},{17,25},{25,17},{2,10},{10... | collective-permute-start | bytes 2752520 | tf_op jit(solution)/shard_map/ppermute | solution.py:426
  43.9 14.3 %collective-permute-start.8 = (bf16[128,2048]{1,0:T(8,128)(2,1)S(1)}, bf16[128,2048]{1,0:T(8,128)(2,1)S(1)}, u32[]{:S(2)}, u32[]{:S(2)}) collective-permute-start(bf16[128,2048]{1,0:T(8,128)(2,1)S(1)} %collective-permute-done.2.a_ref.refs_3_), channel_id=1, source_target_pairs={{0,2},{1,0},{3,1},{5,3},{7,5},{6,7},{4,6},{2,4},{8,9},{9,11},{11,1... | collective-permute-start | bytes 1572872 | tf_op jit(solution)/shard_map/ppermute | solution.py:420
  45.8 12.4 %collective-permute-start.9 = (bf16[128,2048]{1,0:T(8,128)(2,1)S(1)}, bf16[128,2048]{1,0:T(8,128)(2,1)S(1)}, u32[]{:S(2)}, u32[]{:S(2)}) collective-permute-start(bf16[128,2048]{1,0:T(8,128)(2,1)S(1)} %collective-permute-done.3.b_ref.refs_4_), channel_id=1, source_target_pairs={{0,1},{1,3},{3,5},{5,7},{7,6},{6,4},{4,2},{2,0},{8,10},{9,8},{11,9... | collective-permute-start | bytes 1572872 | tf_op jit(solution)/shard_map/ppermute | solution.py:423
  54.1 13.3 %collective-permute-start.14 = (bf16[256,1792]{1,0:T(8,128)(2,1)S(1)}, bf16[256,1792]{1,0:T(8,128)(2,1)S(1)}, u32[]{:S(2)}, u32[]{:S(2)}) collective-permute-start(bf16[256,1792]{1,0:T(8,128)(2,1)S(1)} %copy-done.11), channel_id=1, source_target_pairs={{0,8},{8,0},{16,24},{24,16},{1,9},{9,1},{17,25},{25,17},{2,10},{10... | collective-permute-start | bytes 2752520 | tf_op jit(solution)/shard_map/ppermute | solution.py:426
  58.2 16.7 %collective-permute-start.13 = (bf16[128,2048]{1,0:T(8,128)(2,1)S(1)}, bf16[128,2048]{1,0:T(8,128)(2,1)S(1)}, u32[]{:S(2)}, u32[]{:S(2)}) collective-permute-start(bf16[128,2048]{1,0:T(8,128)(2,1)S(1)} %collective-permute-done.8.a_ref.refs_5_), channel_id=1, source_target_pairs={{0,2},{1,0},{3,1},{5,3},{7,5},{6,7},{4,6},{2,4},{8,9},{9,11},{11,1... | collective-permute-start | bytes 1572872 | tf_op jit(solution)/shard_map/ppermute | solution.py:420
  59.7 15.1 %collective-permute-start.12 = (bf16[128,1920]{1,0:T(8,128)(2,1)S(1)}, bf16[128,1920]{1,0:T(8,128)(2,1)S(1)}, u32[]{:S(2)}, u32[]{:S(2)}) collective-permute-start(bf16[128,1920]{1,0:T(8,128)(2,1)S(1)} %pad.14), channel_id=1, source_target_pairs={{0,16},{8,24},{16,0},{24,8},{1,17},{9,25},{17,1},{25,9},{2,18},{10... | collective-permute-start | bytes 1474568 | tf_op jit(solution)/shard_map/ppermute | solution.py:429
  74.9 15.1 %collective-permute-start.18 = (bf16[2048,128]{1,0:T(8,128)(2,1)S(1)}, bf16[2048,128]{1,0:T(8,128)(2,1)S(1)}, u32[]{:S(2)}, u32[]{:S(2)}) collective-permute-start(bf16[2048,128]{1,0:T(8,128)(2,1)S(1)} %bitcast.31), channel_id=1, source_target_pairs={{0,2},{1,0},{3,1},{5,3},{7,5},{6,7},{4,6},{2,4},{8,9},{9,11},{11,1... | collective-permute-start | bytes 1572872 | tf_op jit(solution)/shard_map/ppermute | solution.py:420
  76.5 13.5 %collective-permute-start.19 = (bf16[2048,128]{1,0:T(8,128)(2,1)S(1)}, bf16[2048,128]{1,0:T(8,128)(2,1)S(1)}, u32[]{:S(2)}, u32[]{:S(2)}) collective-permute-start(bf16[2048,128]{1,0:T(8,128)(2,1)S(1)} %bitcast.32), channel_id=1, source_target_pairs={{0,1},{1,3},{3,5},{5,7},{7,6},{6,4},{4,2},{2,0},{8,10},{9,8},{11,9... | collective-permute-start | bytes 1572872 | tf_op jit(solution)/shard_map/ppermute | solution.py:423
  77.1 12.9 %collective-permute-start.20 = (bf16[128,1920]{1,0:T(8,128)(2,1)S(1)}, bf16[128,1920]{1,0:T(8,128)(2,1)S(1)}, u32[]{:S(2)}, u32[]{:S(2)}) collective-permute-start(bf16[128,1920]{1,0:T(8,128)(2,1)S(1)} %pad.15), channel_id=1, source_target_pairs={{0,16},{8,24},{16,0},{24,8},{1,17},{9,25},{17,1},{25,9},{2,18},{10... | collective-permute-start | bytes 1474568 | tf_op jit(solution)/shard_map/ppermute | solution.py:429
  90.0 14.6 %collective-permute-start.21 = (bf16[2048,128]{1,0:T(8,128)(2,1)S(1)}, bf16[2048,128]{1,0:T(8,128)(2,1)}, u32[]{:S(2)}, u32[]{:S(2)}) collective-permute-start(bf16[2048,128]{1,0:T(8,128)(2,1)S(1)} %collective-permute-done.18.refs_0_), channel_id=1, source_target_pairs={{0,2},{1,0},{3,1},{5,3},{7,5},{6,7},{4,6},{2,4},{8,9},{9,11},{11,1... | collective-permute-start | bytes 1572872 | tf_op jit(solution)/shard_map/ppermute | solution.py:420
  91.6 13.0 %collective-permute-start.22 = (bf16[2048,128]{1,0:T(8,128)(2,1)S(1)}, bf16[2048,128]{1,0:T(8,128)(2,1)S(1)}, u32[]{:S(2)}, u32[]{:S(2)}) collective-permute-start(bf16[2048,128]{1,0:T(8,128)(2,1)S(1)} %collective-permute-done.19.refs_1_), channel_id=1, source_target_pairs={{0,1},{1,3},{3,5},{5,7},{7,6},{6,4},{4,2},{2,0},{8,10},{9,8},{11,9... | collective-permute-start | bytes 1572872 | tf_op jit(solution)/shard_map/ppermute | solution.py:423
  92.2 12.4 %collective-permute-start.24 = (bf16[128,1920]{1,0:T(8,128)(2,1)S(1)}, bf16[128,1920]{1,0:T(8,128)(2,1)S(1)}, u32[]{:S(2)}, u32[]{:S(2)}) collective-permute-start(bf16[128,1920]{1,0:T(8,128)(2,1)S(1)} %pad.16), channel_id=1, source_target_pairs={{0,16},{8,24},{16,0},{24,8},{1,17},{9,25},{17,1},{25,9},{2,18},{10... | collective-permute-start | bytes 1474568 | tf_op jit(solution)/shard_map/ppermute | solution.py:429
  107.1 15.8 %collective-permute-start.26 = (bf16[2048,128]{1,0:T(8,128)(2,1)}, bf16[2048,128]{1,0:T(8,128)(2,1)}, u32[]{:S(2)}, u32[]{:S(2)}) collective-permute-start(bf16[2048,128]{1,0:T(8,128)(2,1)} %collective-permute-done.21.refs_2_), channel_id=1, source_target_pairs={{0,2},{1,0},{3,1},{5,3},{7,5},{6,7},{4,6},{2,4},{8,9},{9,11},{11,1... | collective-permute-start | bytes 1572872 | tf_op jit(solution)/shard_map/ppermute | solution.py:420
  111.1 15.6 %collective-permute-start.28 = (bf16[2,128,1792]{2,1,0:T(8,128)(2,1)S(1)}, bf16[2,128,1792]{2,1,0:T(8,128)(2,1)S(1)}, u32[]{:S(2)}, u32[]{:S(2)}) collective-permute-start(bf16[2,128,1792]{2,1,0:T(8,128)(2,1)S(1)} %swiglu_grads.7.refs_0_.refs_12_), channel_id=1, source_target_pairs={{0,8},{8,0},{16,24},{24,16},{1,9},{9,1},{17,25},{25,17},{2,10},{10... | collective-permute-start | bytes 2752520 | tf_op jit(solution)/shard_map/ppermute | solution.py:426
  123.0 12.8 %collective-permute-start.27 = (bf16[128,2048]{1,0:T(8,128)(2,1)S(1)}, bf16[128,2048]{1,0:T(8,128)(2,1)S(1)}, u32[]{:S(2)}, u32[]{:S(2)}) collective-permute-start(bf16[128,2048]{1,0:T(8,128)(2,1)S(1)} %fusion.7), channel_id=1, source_target_pairs={{0,1},{1,3},{3,5},{5,7},{7,6},{6,4},{4,2},{2,0},{8,10},{9,8},{11,9... | collective-permute-start | bytes 1572872 | tf_op jit(solution)/shard_map/ppermute | solution.py:423
  124.6 13.5 %collective-permute-start.31 = (bf16[2,128,1792]{2,1,0:T(8,128)(2,1)S(1)}, bf16[2,128,1792]{2,1,0:T(8,128)(2,1)S(1)}, u32[]{:S(2)}, u32[]{:S(2)}) collective-permute-start(bf16[2,128,1792]{2,1,0:T(8,128)(2,1)S(1)} %swiglu_grads.4.refs_0_.refs_8_), channel_id=1, source_target_pairs={{0,8},{8,0},{16,24},{24,16},{1,9},{9,1},{17,25},{25,17},{2,10},{10... | collective-permute-start | bytes 2752520 | tf_op jit(solution)/shard_map/ppermute | solution.py:426
  124.6 13.4 %collective-permute-start.32 = (bf16[2,128,1792]{2,1,0:T(8,128)(2,1)S(1)}, bf16[2,128,1792]{2,1,0:T(8,128)(2,1)S(1)}, u32[]{:S(2)}, u32[]{:S(2)}) collective-permute-start(bf16[2,128,1792]{2,1,0:T(8,128)(2,1)S(1)} %swiglu_grads.5.refs_2_.refs_10_), channel_id=1, source_target_pairs={{0,8},{8,0},{16,24},{24,16},{1,9},{9,1},{17,25},{25,17},{2,10},{10... | collective-permute-start | bytes 2752520 | tf_op jit(solution)/shard_map/ppermute | solution.py:426
  125.1 26.7 %collective-permute-start.33 = (bf16[2048,128]{1,0:T(8,128)(2,1)S(1)}, bf16[2048,128]{1,0:T(8,128)(2,1)S(1)}, u32[]{:S(2)}, u32[]{:S(2)}) collective-permute-start(bf16[2048,128]{1,0:T(8,128)(2,1)S(1)} %copy-done.5), channel_id=1, source_target_pairs={{0,1},{1,3},{3,5},{5,7},{7,6},{6,4},{4,2},{2,0},{8,10},{9,8},{11,9... | collective-permute-start | bytes 1572872 | tf_op jit(solution)/shard_map/ppermute | solution.py:423
  126.7 25.0 %collective-permute-start.34 = (bf16[2048,128]{1,0:T(8,128)(2,1)}, bf16[2048,128]{1,0:T(8,128)(2,1)S(1)}, u32[]{:S(2)}, u32[]{:S(2)}) collective-permute-start(bf16[2048,128]{1,0:T(8,128)(2,1)} %collective-permute-done.26.refs_4_), channel_id=1, source_target_pairs={{0,2},{1,0},{3,1},{5,3},{7,5},{6,7},{4,6},{2,4},{8,9},{9,11},{11,1... | collective-permute-start | bytes 1572872 | tf_op jit(solution)/shard_map/ppermute | solution.py:420
  136.0 18.7 %collective-permute-start.29 = (bf16[128,2048]{1,0:T(8,128)(2,1)S(1)}, bf16[128,2048]{1,0:T(8,128)(2,1)S(1)}, u32[]{:S(2)}, u32[]{:S(2)}) collective-permute-start(bf16[128,2048]{1,0:T(8,128)(2,1)S(1)} %fusion.4), channel_id=1, source_target_pairs={{0,1},{1,3},{3,5},{5,7},{7,6},{6,4},{4,2},{2,0},{8,10},{9,8},{11,9... | collective-permute-start | bytes 1572872 | tf_op jit(solution)/shard_map/ppermute | solution.py:423
  138.1 16.6 %collective-permute-start.30 = (bf16[128,2048]{1,0:T(8,128)(2,1)S(1)}, bf16[128,2048]{1,0:T(8,128)(2,1)S(1)}, u32[]{:S(2)}, u32[]{:S(2)}) collective-permute-start(bf16[128,2048]{1,0:T(8,128)(2,1)S(1)} %fusion.8), channel_id=1, source_target_pairs={{0,2},{1,0},{3,1},{5,3},{7,5},{6,7},{4,6},{2,4},{8,9},{9,11},{11,1... | collective-permute-start | bytes 1572872 | tf_op jit(solution)/shard_map/ppermute | solution.py:420
  155.0 14.7 %collective-permute-start.35 = (bf16[128,2048]{1,0:T(8,128)(2,1)S(1)}, bf16[128,2048]{1,0:T(8,128)(2,1)S(1)}, u32[]{:S(2)}, u32[]{:S(2)}) collective-permute-start(bf16[128,2048]{1,0:T(8,128)(2,1)S(1)} %get-tuple-element.163), channel_id=1, source_target_pairs={{0,1},{1,3},{3,5},{5,7},{7,6},{6,4},{4,2},{2,0},{8,10},{9,8},{11,9... | collective-permute-start | bytes 1572872 | tf_op jit(solution)/shard_map/ppermute | solution.py:423
  156.6 13.0 %collective-permute-start.36 = (bf16[128,2048]{1,0:T(8,128)(2,1)S(1)}, bf16[128,2048]{1,0:T(8,128)(2,1)S(1)}, u32[]{:S(2)}, u32[]{:S(2)}) collective-permute-start(bf16[128,2048]{1,0:T(8,128)(2,1)S(1)} %get-tuple-element.162), channel_id=1, source_target_pairs={{0,2},{1,0},{3,1},{5,3},{7,5},{6,7},{4,6},{2,4},{8,9},{9,11},{11,1... | collective-permute-start | bytes 1572872 | tf_op jit(solution)/shard_map/ppermute | solution.py:420
  170.0 14.6 %collective-permute-start.37 = (bf16[128,2048]{1,0:T(8,128)(2,1)S(1)}, bf16[128,2048]{1,0:T(8,128)(2,1)S(1)}, u32[]{:S(2)}, u32[]{:S(2)}) collective-permute-start(bf16[128,2048]{1,0:T(8,128)(2,1)S(1)} %get-tuple-element.160), channel_id=1, source_target_pairs={{0,1},{1,3},{3,5},{5,7},{7,6},{6,4},{4,2},{2,0},{8,10},{9,8},{11,9... | collective-permute-start | bytes 1572872 | tf_op jit(solution)/shard_map/ppermute | solution.py:423
  170.4 14.1 %collective-permute-start.38 = (bf16[128,2048]{1,0:T(8,128)(2,1)S(1)}, bf16[128,2048]{1,0:T(8,128)(2,1)S(1)}, u32[]{:S(2)}, u32[]{:S(2)}) collective-permute-start(bf16[128,2048]{1,0:T(8,128)(2,1)S(1)} %get-tuple-element.161), channel_id=1, source_target_pairs={{0,2},{1,0},{3,1},{5,3},{7,5},{6,7},{4,6},{2,4},{8,9},{9,11},{11,1... | collective-permute-start | bytes 1572872 | tf_op jit(solution)/shard_map/ppermute | solution.py:420
  (30 other events, 249.3 us)

commit v2 on v1

--- a/solution.py
+++ b/solution.py
@@ -61,21 +61,14 @@
     m = first.shape[0]
     tile = 2 * blk
 
-    def body(at_ref, m_ref, w_ref, a_ref, b_ref, keep_ref, send_ref, rows_ref, eff_ref, all_ref, sem_ref, row_sem):
+    def body(at_ref, m_ref, w_ref, a_ref, b_ref, keep_ref, send_ref, rows_ref, eff_ref, all_ref, sem_ref):
         j = pl.program_id(0)
 
         @pl.when(j == 0)
         def _():
-            rows = [
-                pltpu.make_async_copy(x, rows_ref.at[pl.ds(i * m, m)], row_sem.at[i])
-                for i, x in enumerate((a_ref, b_ref))
-            ]
-            for copy in rows:
-                copy.start()
             for t in range(h // tile):
                 tile_copy(w_ref, all_ref, sem_ref, t).start()
-            for copy in rows:
-                copy.wait()
+            stack_rows(rows_ref, (a_ref, b_ref))
 
         tile_copy(w_ref, all_ref, sem_ref, j).wait()
         apply_mask(eff_ref, all_ref.at[j], m_ref, j, blk)
@@ -94,8 +87,10 @@
         in_specs=[
             smem_spec(),
             smem_spec(),
-        ]
-        + [pl.BlockSpec(memory_space=pl.ANY)] * 3,
+            pl.BlockSpec(memory_space=pl.ANY),
+            whole_spec(first),
+            whole_spec(second),
+        ],
         out_specs=[out_spec, out_spec],
         out_shape=[jax.ShapeDtypeStruct((m, h), F32), jax.ShapeDtypeStruct((m, h), BF16)],
         scratch_shapes=[
@@ -103,7 +98,6 @@
             pltpu.VMEM((tile, d), BF16),
             pltpu.VMEM((h // tile, tile, d), BF16),
             pltpu.SemaphoreType.DMA((h // tile,)),
-            pltpu.SemaphoreType.DMA((2,)),
         ],
         compiler_params=params(16),
         cost_estimate=cost(4 * m * d * h, 2 * d * (m + h) + 6 * m * h),
@@ -262,7 +256,7 @@
     d = tiles * tile
 
     def body(at_ref, wg_ref, wu_ref, *refs):
-        o_ref, g_ref, u_ref, wg_all, wu_all, g_sem, u_sem, row_sem = refs[n:]
+        o_ref, g_ref, u_ref, wg_all, wu_all, g_sem, u_sem = refs[n:]
         i = pl.program_id(0)
 
         def copies(t):
@@ -273,18 +267,11 @@
 
         @pl.when(i == 0)
         def _():
-            rows = [
-                pltpu.make_async_copy(r.at[p], dst.at[pl.ds(k * m, m)], row_sem.at[p, k])
-                for p, dst in enumerate((g_ref, u_ref))
-                for k, r in enumerate(refs[:n])
-            ]
-            for copy in rows:
-                copy.start()
             for t in range(tiles):
                 for copy in copies(t):
                     copy.start()
-            for copy in rows:
-                copy.wait()
+            stack_rows(g_ref, [r.at[0] for r in refs[:n]])
+            stack_rows(u_ref, [r.at[1] for r in refs[:n]])
 
         for copy in copies(i):
             copy.wait()
@@ -297,13 +284,12 @@
     return pl.pallas_call(
         body,
         grid=(tiles,),
-        in_specs=[smem_spec()] + [anywhere] * (2 + n),
+        in_specs=[smem_spec(), anywhere, anywhere] + [whole_spec(x) for x in grads],
         out_specs=pl.BlockSpec((n, m, tile), lambda j: (0, 0, j)),
         out_shape=jax.ShapeDtypeStruct((n, m, d), F32),
         scratch_shapes=[pltpu.VMEM((n * m, h), BF16)] * 2
         + [pltpu.VMEM((tiles, h, tile), BF16)] * 2
-        + [pltpu.SemaphoreType.DMA((tiles,))] * 2
-        + [pltpu.SemaphoreType.DMA((2, n))],
+        + [pltpu.SemaphoreType.DMA((tiles,))] * 2,
         compiler_params=params(28),
         cost_estimate=cost(4 * n * m * d * h, 4 * n * m * h + 4 * d * h + 4 * n * m * d),
         name="input_part",
@@ -532,8 +518,10 @@
     for n in range(half - 2):
         got[n] = swap_core(own[n])
     grad_down = weight_grad(act_t, go_rows, mask_down, after, places=half)
-    ia, ib, where, grad_down, *rest = join(ia, ib, where, grad_down, *others[last])
-    others[last] = rest
+    ia, ib, where, grad_down, *rest = join(
+        ia, ib, where, grad_down, *others[last], *got[: half - 2]
+    )
+    others[last], got[: half - 2] = rest[: ny - 1], rest[ny - 1 :]
     in_pairs.append((ia, ib))
 
     for _ in range(2, half - 1):
@@ -551,7 +539,10 @@
     both = part([last], following(own[half - 2]))
     to_self = jnp.where(first, both[0], both[1])
     to_far = jnp.where(first, both[1], both[0]).astype(BF16)
-    to_far, ia, where = join(to_far, ia, where)
+    to_far, where, *early = join(to_far, where, *in_pairs[-1], *got[: half - 2])
+    in_pairs[-1] = tuple(early[:2])
+    got[: half - 2] = early[2:]
+    ia = in_pairs[-1][0]
 
     run_a, run_b, in_far = from_behind(to_far), None, from_ahead(ia)
     parts[half - 2] = part([half - 2], where)

time: 186 us -> 181 us (0.973)
  Pallas kernels: 125 us -> 118 us
  waiting for transfers between devices: 19.2 us -> 21.1 us
    pallas_call x3, Pallas kernels: 33.6 us -> 27 us  [input_part(): pl.pallas_call(body, grid=(tiles,), in_specs=[smem_spec(), anywhere, anyw...]
    ppermute x10, starting transfers between devices: 9.63 us -> 7.3 us  [from_behind(): return lax.ppermute(x, ('row', 'col'), ahead)]
    unnamed x47 -> x51, local copies, waits for them, and re-layouts: 4.89 us -> 4.89 us
  transfers between devices with their start and end apart: 39 -> 39, of which waited for: 10 -> 9; matrix products, arithmetic and copies ran while one was open for 2% -> 2% of each run, Pallas kernels for 66% -> 64%
where the time goes in v2:
time: 181 us; the launch traced here: 180 us
  Pallas kernels  118 us (65%)
  starting transfers between devices  32.1 us (18%)
  waiting for transfers between devices  21.1 us (12%)
  local copies, waits for them, and re-layouts  5.09 us (3%)
  other arithmetic  2.43 us (1%)
    pallas_call x3, Pallas kernels, weight_grad(): pl.pallas_call(body, grid=(rows // tile,), in_specs=[smem_spec(), smem_sp...  33.8 us
    pallas_call x3, Pallas kernels, input_part(): pl.pallas_call(body, grid=(tiles,), in_specs=[smem_spec(), anywhere, anyw...  27 us
    pallas_call x4, Pallas kernels, hidden_part(): pl.pallas_call(body, grid=(h // tile,), in_specs=[smem_spec(), smem_spec(...  23.9 us
    pallas_call x2, Pallas kernels, turned_weight(): pl.pallas_call(body, grid=(d // tile,), in_specs=[smem_spec(), smem_spec(...  18.5 us
    ppermute x11, starting transfers between devices, from_ahead(): return lax.ppermute(x, ('row', 'col'), back)  14.8 us
    ppermute x6, waiting for transfers between devices, shift_y(): lax.ppermute(x, 'row', [(r, (r // 2 + s) % ny * 2 + r % 2) for r in range...  12.3 us
    pallas_call x4, Pallas kernels, swiglu_grads(): pl.pallas_call(body, in_specs=[smem_spec()] + [anywhere] * (2 * ns + nt),...  9.94 us
    ppermute x6, starting transfers between devices, shift_y(): lax.ppermute(x, 'row', [(r, (r // 2 + s) % ny * 2 + r % 2) for r in range...  7.75 us
  transfers between devices with their start and end apart: 39, of which 9 were waited for; matrix products, arithmetic and copies ran while one was open for 2% of the time, Pallas kernels for 64%

profile of v2, /device:TPU:0, one launch (start us, length us, event | category | flops | bytes accessed | tf_op | source)
XLA Modules:
  0.0 180.3 jit_solution(13810632166374937357)
XLA Ops:
  0.6 3.0 %collective-permute-start.4 = (bf16[256,1792]{1,0:T(8,128)(2,1)}, bf16[256,1792]{1,0:T(8,128)(2,1)S(1)}, u32[]{:S(2)}, u32[]{:S(2)}) collective-permute-start(bf16[256,1792]{1,0:T(8,128)(2,1)} %refs_0_.9), channel_id=1, source_target_pairs={{0,16},{8,24},{16,0},{24,8},{1,17},{9,25},{17,1},{25,9},{2,18},{10... | collective-permute-start | bytes 2752520 | tf_op jit(solution)/shard_map/ppermute | solution.py:415
  6.5 9.2 %turned_weight.2.wg_ref = bf16[8,1792,256]{2,1,0:T(8,128)(2,1)} custom-call(s32[13]{0:T(128)S(1)} %compare_select_fusion.14.at_ref.i_ref.p_ref, s32[16,14]{1,0:T(8,128)S(1)} %copy-done.9, bf16[2048,1792]{1,0:T(8,128)(2,1)} %w_ref.6), custom_call_target="tpu_custom_call" | custom-call | flops 896 | bytes 3584 | tf_op jit(solution)/shard_map/turned_weight/pallas_call | solution.py:240
  15.8 2.0 %copy.14 = bf16[128,2048]{0,1:T(8,128)(2,1)} copy(bf16[128,2048]{1,0:T(8,128)(2,1)} %param.10) | data formatting | bytes 1048576 | tf_op args[0]
  18.6 1.6 collective-permute-start.2
  20.6 5.9 %hidden_part.4 = (f32[128,1792]{1,0:T(8,128)S(1)}, bf16[128,1792]{1,0:T(8,128)(2,1)S(1)}) custom-call(s32[13]{0:T(128)S(1)} %compare_select_fusion.14.at_ref.i_ref.p_ref, s32[14,16]{1,0:T(8,128)S(1)} %copy-done.8, bf16[1792,2048]{1,0:T(8,128)(2,1)} %w_ref.11, bf16[128,2048]{1,0:T(8,128)(2,1)S(1)} %collective-permute-done.a_ref.refs_1_, ...), custom_call_target="tpu_custom_call" | custom-call | flops 458752 | bytes 2256 | tf_op jit(solution)/shard_map/hidden_part/pallas_call | solution.py:84
  27.2 9.2 %turned_weight.3.wu_ref = bf16[8,1792,256]{2,1,0:T(8,128)(2,1)} custom-call(s32[13]{0:T(128)S(1)} %compare_select_fusion.14.at_ref.i_ref.p_ref, s32[16,14]{1,0:T(8,128)S(1)} %copy-done.11, bf16[2048,1792]{1,0:T(8,128)(2,1)} %w_ref.8), custom_call_target="tpu_custom_call" | custom-call | flops 896 | bytes 3584 | tf_op jit(solution)/shard_map/turned_weight/pallas_call | solution.py:240
  36.5 7.4 %collective-permute-done.5.refs_5_ = bf16[256,1792]{1,0:T(8,128)(2,1)S(1)} collective-permute-done((bf16[256,1792]{1,0:T(8,128)(2,1)}, bf16[256,1792]{1,0:T(8,128)(2,1)S(1)}, u32[]{:S(2)}, u32[]{:S(2)}) %collective-permute-start.5) | collective-permute-done | bytes 917536 | tf_op jit(solution)/shard_map/ppermute | solution.py:415
  43.9 1.8 %collective-permute-start.8 = (bf16[128,2048]{1,0:T(8,128)(2,1)S(1)}, bf16[128,2048]{1,0:T(8,128)(2,1)S(1)}, u32[]{:S(2)}, u32[]{:S(2)}) collective-permute-start(bf16[128,2048]{1,0:T(8,128)(2,1)S(1)} %collective-permute-done.2.a_ref.refs_3_), channel_id=1, source_target_pairs={{0,2},{1,0},{3,1},{5,3},{7,5},{6,7},{4,6},{2,4},{8,9},{9,11},{11,1... | collective-permute-start | bytes 1572872 | tf_op jit(solution)/shard_map/ppermute | solution.py:406
  46.2 1.8 collective-permute-start.7
  47.9 5.9 %hidden_part.5 = (f32[128,1792]{1,0:T(8,128)S(1)}, bf16[128,1792]{1,0:T(8,128)(2,1)S(1)}) custom-call(s32[13]{0:T(128)S(1)} %compare_select_fusion.14.at_ref.i_ref.p_ref, s32[14,16]{1,0:T(8,128)S(1)} %copy-done.8, bf16[1792,2048]{1,0:T(8,128)(2,1)} %w_ref.11, bf16[128,2048]{1,0:T(8,128)(2,1)S(1)} %collective-permute-done.2.a_ref.refs_3_, ...), custom_call_target="tpu_custom_call" | custom-call | flops 458752 | bytes 2256 | tf_op jit(solution)/shard_map/hidden_part/pallas_call | solution.py:84
  55.9 2.1 %collective-permute-done.7.refs_10_ = bf16[128,1920]{1,0:T(8,128)(2,1)S(1)} collective-permute-done((bf16[128,1920]{1,0:T(8,128)(2,1)S(1)}, bf16[128,1920]{1,0:T(8,128)(2,1)S(1)}, u32[]{:S(2)}, u32[]{:S(2)}) %collective-permute-start.7) | collective-permute-done | bytes 491552 | tf_op jit(solution)/shard_map/ppermute | solution.py:415
  59.7 1.6 collective-permute-start.12
  61.3 5.9 %hidden_part.6 = (f32[128,1792]{1,0:T(8,128)S(1)}, bf16[128,1792]{1,0:T(8,128)(2,1)S(1)}) custom-call(s32[13]{0:T(128)S(1)} %compare_select_fusion.14.at_ref.i_ref.p_ref, s32[14,16]{1,0:T(8,128)S(1)} %copy-done.8, bf16[1792,2048]{1,0:T(8,128)(2,1)} %w_ref.11, bf16[128,2048]{1,0:T(8,128)(2,1)S(1)} %collective-permute-done.8.a_ref.refs_5_, ...), custom_call_target="tpu_custom_call" | custom-call | flops 458752 | bytes 2256 | tf_op jit(solution)/shard_map/hidden_part/pallas_call | solution.py:84
  69.5 5.2 %activation.1.refs_0_ = bf16[1792,1024]{1,0:T(8,128)(2,1)S(1)} custom-call(s32[13]{0:T(128)S(1)} %compare_select_fusion.14.at_ref.i_ref.p_ref, bf16[256,1792]{1,0:T(8,128)(2,1)} %refs_0_.9, bf16[256,1792]{1,0:T(8,128)(2,1)} %refs_1_.9, bf16[256,1792]{1,0:T(8,128)(2,1)} %copy-done.17, bf16[256,1792]{1,0:T(8,128)(2,1)} %copy-done.18, ...), custom_call_target="tpu_custom_call" | custom-call | flops 4480 | bytes 2688 | tf_op jit(solution)/shard_map/activation/pallas_call | solution.py:135
  77.6 6.0 %hidden_part.7 = (f32[128,1792]{1,0:T(8,128)S(1)}, bf16[128,1792]{1,0:T(8,128)(2,1)S(1)}) custom-call(s32[13]{0:T(128)S(1)} %compare_select_fusion.14.at_ref.i_ref.p_ref, s32[14,16]{1,0:T(8,128)S(1)} %copy-done.8, bf16[1792,2048]{1,0:T(8,128)(2,1)} %w_ref.11, bf16[128,2048]{1,0:T(8,128)(2,1)S(1)} %copy-done.5, ...), custom_call_target="tpu_custom_call" | custom-call | flops 458752 | bytes 2256 | tf_op jit(solution)/shard_map/hidden_part/pallas_call | solution.py:84
  83.7 2.4 %swiglu_grads.4.refs_0_.refs_8_ = bf16[2,128,1792]{2,1,0:T(8,128)(2,1)S(1)} custom-call(s32[13]{0:T(128)S(1)} %compare_select_fusion.14.at_ref.i_ref.p_ref, bf16[256,1792]{1,0:T(8,128)(2,1)} %refs_0_.9, bf16[256,1792]{1,0:T(8,128)(2,1)} %refs_1_.9, bf16[256,1792]{1,0:T(8,128)(2,1)} %copy-done.17, bf16[256,1792]{1,0:T(8,128)(2,1)} %copy-done.18, ...), custom_call_target="tpu_custom_call" | custom-call | flops 1120 | bytes 784 | tf_op jit(solution)/shard_map/swiglu_grads/pallas_call | solution.py:205
  86.6 2.4 %swiglu_grads.5.refs_2_.refs_10_ = bf16[2,128,1792]{2,1,0:T(8,128)(2,1)S(1)} custom-call(s32[13]{0:T(128)S(1)} %compare_select_fusion.14.at_ref.i_ref.p_ref, bf16[256,1792]{1,0:T(8,128)(2,1)} %refs_0_.9, bf16[256,1792]{1,0:T(8,128)(2,1)} %refs_1_.9, bf16[256,1792]{1,0:T(8,128)(2,1)} %copy-done.17, bf16[256,1792]{1,0:T(8,128)(2,1)} %copy-done.18, ...), custom_call_target="tpu_custom_call" | custom-call | flops 1120 | bytes 784 | tf_op jit(solution)/shard_map/swiglu_grads/pallas_call | solution.py:205
  89.9 1.6 collective-permute-start.21
  92.9 11.1 %weight_grad.3 = bf16[1792,2048]{1,0:T(8,128)(2,1)} custom-call(s32[14,16]{1,0:T(8,128)S(1)} %copy-done.8, s32[13]{0:T(128)S(1)} %compare_select_fusion.14.at_ref.i_ref.p_ref, bf16[1792,1024]{1,0:T(8,128)(2,1)S(1)} %activation.1.refs_0_, bf16[128,2048]{1,0:T(8,128)(2,1)S(1)} %collective-permute-done.a_ref.refs_1_, ...), custom_call_target="tpu_custom_call" | custom-call | flops 1835008 | bytes 3712 | tf_op jit(solution)/shard_map/weight_grad/pallas_call | solution.py:352
  104.0 1.9 %collective-permute-done.24.refs_10_ = bf16[128,1920]{1,0:T(8,128)(2,1)S(1)} collective-permute-done((bf16[128,1920]{1,0:T(8,128)(2,1)S(1)}, bf16[128,1920]{1,0:T(8,128)(2,1)S(1)}, u32[]{:S(2)}, u32[]{:S(2)}) %collective-permute-start.24) | collective-permute-done | bytes 491552 | tf_op jit(solution)/shard_map/ppermute | solution.py:415
  105.9 2.4 %swiglu_grads.6.refs_0_.refs_14_ = bf16[2,128,1792]{2,1,0:T(8,128)(2,1)S(1)} custom-call(s32[13]{0:T(128)S(1)} %compare_select_fusion.14.at_ref.i_ref.p_ref, bf16[256,1792]{1,0:T(8,128)(2,1)} %refs_0_.9, bf16[256,1792]{1,0:T(8,128)(2,1)} %refs_1_.9, bf16[256,1792]{1,0:T(8,128)(2,1)} %copy-done.17, bf16[256,1792]{1,0:T(8,128)(2,1)} %copy-done.18, ...), custom_call_target="tpu_custom_call" | custom-call | flops 1120 | bytes 784 | tf_op jit(solution)/shard_map/swiglu_grads/pallas_call | solution.py:205
  108.4 1.6 collective-permute-start.28
  110.5 2.8 %swiglu_grads.7.refs_0_.refs_12_ = bf16[2,128,1792]{2,1,0:T(8,128)(2,1)S(1)} custom-call(s32[13]{0:T(128)S(1)} %compare_select_fusion.14.at_ref.i_ref.p_ref, bf16[256,1792]{1,0:T(8,128)(2,1)} %refs_0_.9, bf16[256,1792]{1,0:T(8,128)(2,1)} %refs_1_.9, bf16[256,1792]{1,0:T(8,128)(2,1)} %copy-done.17, bf16[256,1792]{1,0:T(8,128)(2,1)} %copy-done.18, ...), custom_call_target="tpu_custom_call" | custom-call | flops 1120 | bytes 784 | tf_op jit(solution)/shard_map/swiglu_grads/pallas_call | solution.py:205
  113.3 8.2 %input_part.3 = f32[2,128,2048]{2,1,0:T(8,128)S(1)} custom-call(s32[13]{0:T(128)S(1)} %compare_select_fusion.14.at_ref.i_ref.p_ref, bf16[8,1792,256]{2,1,0:T(8,128)(2,1)} %turned_weight.2.wg_ref, bf16[8,1792,256]{2,1,0:T(8,128)(2,1)} %turned_weight.3.wu_ref, bf16[2,128,1792]{2,1,0:T(8,128)(2,1)S(1)} %swiglu_grads.6.refs_0_.refs_14_, ...), custom_call_target="tpu_custom_call" | custom-call | flops 917504 | bytes 4544 | tf_op jit(solution)/shard_map/input_part/pallas_call | solution.py:284
  121.6 1.6 collective-permute-done.28.refs_4_
  125.2 7.5 %input_part.4 = f32[2,128,2048]{2,1,0:T(8,128)S(1)} custom-call(s32[13]{0:T(128)S(1)} %compare_select_fusion.14.at_ref.i_ref.p_ref, bf16[8,1792,256]{2,1,0:T(8,128)(2,1)} %turned_weight.2.wg_ref, bf16[8,1792,256]{2,1,0:T(8,128)(2,1)} %turned_weight.3.wu_ref, bf16[2,128,1792]{2,1,0:T(8,128)(2,1)S(1)} %swiglu_grads.7.refs_0_.refs_12_, ...), custom_call_target="tpu_custom_call" | custom-call | flops 917504 | bytes 4544 | tf_op jit(solution)/shard_map/input_part/pallas_call | solution.py:284
  132.7 5.0 %collective-permute-done.30 = bf16[128,2048]{1,0:T(8,128)(2,1)S(1)} collective-permute-done((bf16[128,2048]{1,0:T(8,128)(2,1)S(1)}, bf16[128,2048]{1,0:T(8,128)(2,1)S(1)}, u32[]{:S(2)}, u32[]{:S(2)}) %collective-permute-start.30) | collective-permute-done | bytes 524320 | tf_op jit(solution)/shard_map/ppermute | solution.py:409
  138.0 1.6 collective-permute-start.33
  140.0 11.4 %input_part.5 = f32[4,128,2048]{2,1,0:T(8,128)S(1)} custom-call(s32[13]{0:T(128)S(1)} %compare_select_fusion.14.at_ref.i_ref.p_ref, bf16[8,1792,256]{2,1,0:T(8,128)(2,1)} %turned_weight.2.wg_ref, bf16[8,1792,256]{2,1,0:T(8,128)(2,1)} %turned_weight.3.wu_ref, bf16[2,128,1792]{2,1,0:T(8,128)(2,1)S(1)} %swiglu_grads.4.refs_0_.refs_8_, ...), custom_call_target="tpu_custom_call" | custom-call | flops 1835008 | bytes 5504 | tf_op jit(solution)/shard_map/input_part/pallas_call | solution.py:284
  151.9 1.6 collective-permute-start.36
  154.0 11.4 %weight_grad.4 = bf16[2048,1792]{1,0:T(8,128)(2,1)} custom-call(s32[16,14]{1,0:T(8,128)S(1)} %copy-done.10, s32[13]{0:T(128)S(1)} %compare_select_fusion.14.at_ref.i_ref.p_ref, bf16[2048,128]{1,0:T(8,128)(2,1)S(1)} %copy-done.7, bf16[2048,128]{1,0:T(8,128)(2,1)S(1)} %collective-permute-done.19.refs_1_, bf16[2048,128]{1,0:T(8,128)(2,1)} %collective-permute-done.21.refs_2_, ...), custom_call_target="tpu_custom_call" | custom-call | flops 1835008 | bytes 3712 | tf_op jit(solution)/shard_map/weight_grad/pallas_call | solution.py:352
  167.8 11.4 %weight_grad.5 = bf16[2048,1792]{1,0:T(8,128)(2,1)} custom-call(s32[16,14]{1,0:T(8,128)S(1)} %copy-done.11, s32[13]{0:T(128)S(1)} %compare_select_fusion.14.at_ref.i_ref.p_ref, bf16[2048,128]{1,0:T(8,128)(2,1)S(1)} %copy-done.7, bf16[2048,128]{1,0:T(8,128)(2,1)S(1)} %collective-permute-done.19.refs_1_, bf16[2048,128]{1,0:T(8,128)(2,1)} %collective-permute-done.21.refs_2_, ...), custom_call_target="tpu_custom_call" | custom-call | flops 1835008 | bytes 3712 | tf_op jit(solution)/shard_map/weight_grad/pallas_call | solution.py:352
  (130 shorter events, 24.4 us)
Async XLA Ops:
  0.6 26.0 %collective-permute-start.4 = (bf16[256,1792]{1,0:T(8,128)(2,1)}, bf16[256,1792]{1,0:T(8,128)(2,1)S(1)}, u32[]{:S(2)}, u32[]{:S(2)}) collective-permute-start(bf16[256,1792]{1,0:T(8,128)(2,1)} %refs_0_.9), channel_id=1, source_target_pairs={{0,16},{8,24},{16,0},{24,8},{1,17},{9,25},{17,1},{25,9},{2,18},{10... | collective-permute-start | bytes 2752520 | tf_op jit(solution)/shard_map/ppermute | solution.py:415
  3.7 14.9 %collective-permute-start.1 = (bf16[128,2048]{1,0:T(8,128)(2,1)}, bf16[128,2048]{1,0:T(8,128)(2,1)S(1)}, u32[]{:S(2)}, u32[]{:S(2)}) collective-permute-start(bf16[128,2048]{1,0:T(8,128)(2,1)} %refs_7_.1), channel_id=1, source_target_pairs={{0,1},{1,3},{3,5},{5,7},{7,6},{6,4},{4,2},{2,0},{8,10},{9,8},{11,9... | collective-permute-start | bytes 1572872 | tf_op jit(solution)/shard_map/ppermute | solution.py:409
  5.2 13.4 %collective-permute-start = (bf16[128,2048]{1,0:T(8,128)(2,1)}, bf16[128,2048]{1,0:T(8,128)(2,1)S(1)}, u32[]{:S(2)}, u32[]{:S(2)}) collective-permute-start(bf16[128,2048]{1,0:T(8,128)(2,1)} %refs_7_.1), channel_id=1, source_target_pairs={{0,2},{1,0},{3,1},{5,3},{7,5},{6,7},{4,6},{2,4},{8,9},{9,11},{11,1... | collective-permute-start | bytes 1572872 | tf_op jit(solution)/shard_map/ppermute | solution.py:406
  5.7 38.2 %collective-permute-start.5 = (bf16[256,1792]{1,0:T(8,128)(2,1)}, bf16[256,1792]{1,0:T(8,128)(2,1)S(1)}, u32[]{:S(2)}, u32[]{:S(2)}) collective-permute-start(bf16[256,1792]{1,0:T(8,128)(2,1)} %refs_1_.9), channel_id=1, source_target_pairs={{0,16},{8,24},{16,0},{24,8},{1,17},{9,25},{17,1},{25,9},{2,18},{10... | collective-permute-start | bytes 2752520 | tf_op jit(solution)/shard_map/ppermute | solution.py:415
  18.6 25.3 %collective-permute-start.2 = (bf16[128,2048]{1,0:T(8,128)(2,1)S(1)}, bf16[128,2048]{1,0:T(8,128)(2,1)S(1)}, u32[]{:S(2)}, u32[]{:S(2)}) collective-permute-start(bf16[128,2048]{1,0:T(8,128)(2,1)S(1)} %collective-permute-done.a_ref.refs_1_), channel_id=1, source_target_pairs={{0,2},{1,0},{3,1},{5,3},{7,5},{6,7},{4,6},{2,4},{8,9},{9,11},{11,1... | collective-permute-start | bytes 1572872 | tf_op jit(solution)/shard_map/ppermute | solution.py:406
  20.2 23.7 %collective-permute-start.3 = (bf16[128,2048]{1,0:T(8,128)(2,1)S(1)}, bf16[128,2048]{1,0:T(8,128)(2,1)S(1)}, u32[]{:S(2)}, u32[]{:S(2)}) collective-permute-start(bf16[128,2048]{1,0:T(8,128)(2,1)S(1)} %collective-permute-done.1.b_ref.refs_2_), channel_id=1, source_target_pairs={{0,1},{1,3},{3,5},{5,7},{7,6},{6,4},{4,2},{2,0},{8,10},{9,8},{11,9... | collective-permute-start | bytes 1572872 | tf_op jit(solution)/shard_map/ppermute | solution.py:409
  26.6 17.3 %collective-permute-start.6 = (bf16[128,1792]{1,0:T(8,128)(2,1)S(1)}, bf16[128,1792]{1,0:T(8,128)(2,1)S(1)}, u32[]{:S(2)}, u32[]{:S(2)}) collective-permute-start(bf16[128,1792]{1,0:T(8,128)(2,1)S(1)} %get-tuple-element.92), channel_id=1, source_target_pairs={{0,8},{8,0},{16,24},{24,16},{1,9},{9,1},{17,25},{25,17},{2,10},{10... | collective-permute-start | bytes 1376264 | tf_op jit(solution)/shard_map/ppermute | solution.py:412
  26.7 27.3 %collective-permute-start.10 = (bf16[256,1792]{1,0:T(8,128)(2,1)S(1)}, bf16[256,1792]{1,0:T(8,128)(2,1)S(1)}, u32[]{:S(2)}, u32[]{:S(2)}) collective-permute-start(bf16[256,1792]{1,0:T(8,128)(2,1)S(1)} %copy-done.12), channel_id=1, source_target_pairs={{0,8},{8,0},{16,24},{24,16},{1,9},{9,1},{17,25},{25,17},{2,10},{10... | collective-permute-start | bytes 2752520 | tf_op jit(solution)/shard_map/ppermute | solution.py:412
  43.9 14.3 %collective-permute-start.8 = (bf16[128,2048]{1,0:T(8,128)(2,1)S(1)}, bf16[128,2048]{1,0:T(8,128)(2,1)S(1)}, u32[]{:S(2)}, u32[]{:S(2)}) collective-permute-start(bf16[128,2048]{1,0:T(8,128)(2,1)S(1)} %collective-permute-done.2.a_ref.refs_3_), channel_id=1, source_target_pairs={{0,2},{1,0},{3,1},{5,3},{7,5},{6,7},{4,6},{2,4},{8,9},{9,11},{11,1... | collective-permute-start | bytes 1572872 | tf_op jit(solution)/shard_map/ppermute | solution.py:406
  45.8 12.4 %collective-permute-start.9 = (bf16[128,2048]{1,0:T(8,128)(2,1)S(1)}, bf16[128,2048]{1,0:T(8,128)(2,1)S(1)}, u32[]{:S(2)}, u32[]{:S(2)}) collective-permute-start(bf16[128,2048]{1,0:T(8,128)(2,1)S(1)} %collective-permute-done.3.b_ref.refs_4_), channel_id=1, source_target_pairs={{0,1},{1,3},{3,5},{5,7},{7,6},{6,4},{4,2},{2,0},{8,10},{9,8},{11,9... | collective-permute-start | bytes 1572872 | tf_op jit(solution)/shard_map/ppermute | solution.py:409
  54.0 13.3 %collective-permute-start.14 = (bf16[256,1792]{1,0:T(8,128)(2,1)S(1)}, bf16[256,1792]{1,0:T(8,128)(2,1)S(1)}, u32[]{:S(2)}, u32[]{:S(2)}) collective-permute-start(bf16[256,1792]{1,0:T(8,128)(2,1)S(1)} %copy-done.13), channel_id=1, source_target_pairs={{0,8},{8,0},{16,24},{24,16},{1,9},{9,1},{17,25},{25,17},{2,10},{10... | collective-permute-start | bytes 2752520 | tf_op jit(solution)/shard_map/ppermute | solution.py:412
  58.2 16.5 %collective-permute-start.13 = (bf16[128,2048]{1,0:T(8,128)(2,1)S(1)}, bf16[128,2048]{1,0:T(8,128)(2,1)S(1)}, u32[]{:S(2)}, u32[]{:S(2)}) collective-permute-start(bf16[128,2048]{1,0:T(8,128)(2,1)S(1)} %collective-permute-done.8.a_ref.refs_5_), channel_id=1, source_target_pairs={{0,2},{1,0},{3,1},{5,3},{7,5},{6,7},{4,6},{2,4},{8,9},{9,11},{11,1... | collective-permute-start | bytes 1572872 | tf_op jit(solution)/shard_map/ppermute | solution.py:406
  59.7 15.0 %collective-permute-start.12 = (bf16[128,1920]{1,0:T(8,128)(2,1)S(1)}, bf16[128,1920]{1,0:T(8,128)(2,1)S(1)}, u32[]{:S(2)}, u32[]{:S(2)}) collective-permute-start(bf16[128,1920]{1,0:T(8,128)(2,1)S(1)} %pad.14), channel_id=1, source_target_pairs={{0,16},{8,24},{16,0},{24,8},{1,17},{9,25},{17,1},{25,9},{2,18},{10... | collective-permute-start | bytes 1474568 | tf_op jit(solution)/shard_map/ppermute | solution.py:415
  74.8 15.2 %collective-permute-start.19 = (bf16[2048,128]{1,0:T(8,128)(2,1)S(1)}, bf16[2048,128]{1,0:T(8,128)(2,1)S(1)}, u32[]{:S(2)}, u32[]{:S(2)}) collective-permute-start(bf16[2048,128]{1,0:T(8,128)(2,1)S(1)} %bitcast.31), channel_id=1, source_target_pairs={{0,1},{1,3},{3,5},{5,7},{7,6},{6,4},{4,2},{2,0},{8,10},{9,8},{11,9... | collective-permute-start | bytes 1572872 | tf_op jit(solution)/shard_map/ppermute | solution.py:409
  76.0 13.9 %collective-permute-start.18 = (bf16[2048,128]{1,0:T(8,128)(2,1)S(1)}, bf16[2048,128]{1,0:T(8,128)(2,1)S(1)}, u32[]{:S(2)}, u32[]{:S(2)}) collective-permute-start(bf16[2048,128]{1,0:T(8,128)(2,1)S(1)} %bitcast.32), channel_id=1, source_target_pairs={{0,2},{1,0},{3,1},{5,3},{7,5},{6,7},{4,6},{2,4},{8,9},{9,11},{11,1... | collective-permute-start | bytes 1572872 | tf_op jit(solution)/shard_map/ppermute | solution.py:406
  77.0 12.9 %collective-permute-start.20 = (bf16[128,1920]{1,0:T(8,128)(2,1)S(1)}, bf16[128,1920]{1,0:T(8,128)(2,1)S(1)}, u32[]{:S(2)}, u32[]{:S(2)}) collective-permute-start(bf16[128,1920]{1,0:T(8,128)(2,1)S(1)} %pad.15), channel_id=1, source_target_pairs={{0,16},{8,24},{16,0},{24,8},{1,17},{9,25},{17,1},{25,9},{2,18},{10... | collective-permute-start | bytes 1474568 | tf_op jit(solution)/shard_map/ppermute | solution.py:415
  86.1 17.9 %collective-permute-start.25 = (bf16[2,128,1792]{2,1,0:T(8,128)(2,1)S(1)}, bf16[2,128,1792]{2,1,0:T(8,128)(2,1)S(1)}, u32[]{:S(2)}, u32[]{:S(2)}) collective-permute-start(bf16[2,128,1792]{2,1,0:T(8,128)(2,1)S(1)} %swiglu_grads.4.refs_0_.refs_8_), channel_id=1, source_target_pairs={{0,8},{8,0},{16,24},{24,16},{1,9},{9,1},{17,25},{25,17},{2,10},{10... | collective-permute-start | bytes 2752520 | tf_op jit(solution)/shard_map/ppermute | solution.py:412
  89.9 15.9 %collective-permute-start.21 = (bf16[2048,128]{1,0:T(8,128)(2,1)S(1)}, bf16[2048,128]{1,0:T(8,128)(2,1)}, u32[]{:S(2)}, u32[]{:S(2)}) collective-permute-start(bf16[2048,128]{1,0:T(8,128)(2,1)S(1)} %collective-permute-done.18.refs_0_), channel_id=1, source_target_pairs={{0,2},{1,0},{3,1},{5,3},{7,5},{6,7},{4,6},{2,4},{8,9},{9,11},{11,1... | collective-permute-start | bytes 1572872 | tf_op jit(solution)/shard_map/ppermute | solution.py:406
  91.6 14.3 %collective-permute-start.22 = (bf16[2048,128]{1,0:T(8,128)(2,1)S(1)}, bf16[2048,128]{1,0:T(8,128)(2,1)}, u32[]{:S(2)}, u32[]{:S(2)}) collective-permute-start(bf16[2048,128]{1,0:T(8,128)(2,1)S(1)} %collective-permute-done.19.refs_1_), channel_id=1, source_target_pairs={{0,1},{1,3},{3,5},{5,7},{7,6},{6,4},{4,2},{2,0},{8,10},{9,8},{11,9... | collective-permute-start | bytes 1572872 | tf_op jit(solution)/shard_map/ppermute | solution.py:409
  92.0 13.9 %collective-permute-start.26 = (bf16[2,128,1792]{2,1,0:T(8,128)(2,1)S(1)}, bf16[2,128,1792]{2,1,0:T(8,128)(2,1)S(1)}, u32[]{:S(2)}, u32[]{:S(2)}) collective-permute-start(bf16[2,128,1792]{2,1,0:T(8,128)(2,1)S(1)} %swiglu_grads.5.refs_2_.refs_10_), channel_id=1, source_target_pairs={{0,8},{8,0},{16,24},{24,16},{1,9},{9,1},{17,25},{25,17},{2,10},{10... | collective-permute-start | bytes 2752520 | tf_op jit(solution)/shard_map/ppermute | solution.py:412
  92.2 13.7 %collective-permute-start.24 = (bf16[128,1920]{1,0:T(8,128)(2,1)S(1)}, bf16[128,1920]{1,0:T(8,128)(2,1)S(1)}, u32[]{:S(2)}, u32[]{:S(2)}) collective-permute-start(bf16[128,1920]{1,0:T(8,128)(2,1)S(1)} %pad.16), channel_id=1, source_target_pairs={{0,16},{8,24},{16,0},{24,8},{1,17},{9,25},{17,1},{25,9},{2,18},{10... | collective-permute-start | bytes 1474568 | tf_op jit(solution)/shard_map/ppermute | solution.py:415
  108.4 14.8 %collective-permute-start.28 = (bf16[2048,128]{1,0:T(8,128)(2,1)}, bf16[2048,128]{1,0:T(8,128)(2,1)}, u32[]{:S(2)}, u32[]{:S(2)}) collective-permute-start(bf16[2048,128]{1,0:T(8,128)(2,1)} %collective-permute-done.21.refs_2_), channel_id=1, source_target_pairs={{0,2},{1,0},{3,1},{5,3},{7,5},{6,7},{4,6},{2,4},{8,9},{9,11},{11,1... | collective-permute-start | bytes 1572872 | tf_op jit(solution)/shard_map/ppermute | solution.py:406
  110.0 13.2 %collective-permute-start.29 = (bf16[2048,128]{1,0:T(8,128)(2,1)}, bf16[2048,128]{1,0:T(8,128)(2,1)}, u32[]{:S(2)}, u32[]{:S(2)}) collective-permute-start(bf16[2048,128]{1,0:T(8,128)(2,1)} %collective-permute-done.22.refs_3_), channel_id=1, source_target_pairs={{0,1},{1,3},{3,5},{5,7},{7,6},{6,4},{4,2},{2,0},{8,10},{9,8},{11,9... | collective-permute-start | bytes 1572872 | tf_op jit(solution)/shard_map/ppermute | solution.py:409
  113.2 12.0 %collective-permute-start.31 = (bf16[2,128,1792]{2,1,0:T(8,128)(2,1)S(1)}, bf16[2,128,1792]{2,1,0:T(8,128)(2,1)S(1)}, u32[]{:S(2)}, u32[]{:S(2)}) collective-permute-start(bf16[2,128,1792]{2,1,0:T(8,128)(2,1)S(1)} %swiglu_grads.7.refs_0_.refs_12_), channel_id=1, source_target_pairs={{0,8},{8,0},{16,24},{24,16},{1,9},{9,1},{17,25},{25,17},{2,10},{10... | collective-permute-start | bytes 2752520 | tf_op jit(solution)/shard_map/ppermute | solution.py:412
  123.2 14.5 %collective-permute-start.30 = (bf16[128,2048]{1,0:T(8,128)(2,1)S(1)}, bf16[128,2048]{1,0:T(8,128)(2,1)S(1)}, u32[]{:S(2)}, u32[]{:S(2)}) collective-permute-start(bf16[128,2048]{1,0:T(8,128)(2,1)S(1)} %fusion.7), channel_id=1, source_target_pairs={{0,1},{1,3},{3,5},{5,7},{7,6},{6,4},{4,2},{2,0},{8,10},{9,8},{11,9... | collective-permute-start | bytes 1572872 | tf_op jit(solution)/shard_map/ppermute | solution.py:409
  124.1 27.3 %collective-permute-start.34 = (bf16[2048,128]{1,0:T(8,128)(2,1)}, bf16[2048,128]{1,0:T(8,128)(2,1)S(1)}, u32[]{:S(2)}, u32[]{:S(2)}) collective-permute-start(bf16[2048,128]{1,0:T(8,128)(2,1)} %collective-permute-done.28.refs_4_), channel_id=1, source_target_pairs={{0,2},{1,0},{3,1},{5,3},{7,5},{6,7},{4,6},{2,4},{8,9},{9,11},{11,1... | collective-permute-start | bytes 1572872 | tf_op jit(solution)/shard_map/ppermute | solution.py:406
  138.0 13.6 %collective-permute-start.33 = (bf16[128,2048]{1,0:T(8,128)(2,1)S(1)}, bf16[128,2048]{1,0:T(8,128)(2,1)S(1)}, u32[]{:S(2)}, u32[]{:S(2)}) collective-permute-start(bf16[128,2048]{1,0:T(8,128)(2,1)S(1)} %fusion.8), channel_id=1, source_target_pairs={{0,2},{1,0},{3,1},{5,3},{7,5},{6,7},{4,6},{2,4},{8,9},{9,11},{11,1... | collective-permute-start | bytes 1572872 | tf_op jit(solution)/shard_map/ppermute | solution.py:406
  139.5 12.1 %collective-permute-start.32 = (bf16[128,2048]{1,0:T(8,128)(2,1)S(1)}, bf16[128,2048]{1,0:T(8,128)(2,1)S(1)}, u32[]{:S(2)}, u32[]{:S(2)}) collective-permute-start(bf16[128,2048]{1,0:T(8,128)(2,1)S(1)} %fusion.4), channel_id=1, source_target_pairs={{0,1},{1,3},{3,5},{5,7},{7,6},{6,4},{4,2},{2,0},{8,10},{9,8},{11,9... | collective-permute-start | bytes 1572872 | tf_op jit(solution)/shard_map/ppermute | solution.py:409
  151.9 13.5 %collective-permute-start.36 = (bf16[128,2048]{1,0:T(8,128)(2,1)S(1)}, bf16[128,2048]{1,0:T(8,128)(2,1)S(1)}, u32[]{:S(2)}, u32[]{:S(2)}) collective-permute-start(bf16[128,2048]{1,0:T(8,128)(2,1)S(1)} %get-tuple-element.172), channel_id=1, source_target_pairs={{0,2},{1,0},{3,1},{5,3},{7,5},{6,7},{4,6},{2,4},{8,9},{9,11},{11,1... | collective-permute-start | bytes 1572872 | tf_op jit(solution)/shard_map/ppermute | solution.py:406
  153.5 11.9 %collective-permute-start.35 = (bf16[128,2048]{1,0:T(8,128)(2,1)S(1)}, bf16[128,2048]{1,0:T(8,128)(2,1)S(1)}, u32[]{:S(2)}, u32[]{:S(2)}) collective-permute-start(bf16[128,2048]{1,0:T(8,128)(2,1)S(1)} %get-tuple-element.173), channel_id=1, source_target_pairs={{0,1},{1,3},{3,5},{5,7},{7,6},{6,4},{4,2},{2,0},{8,10},{9,8},{11,9... | collective-permute-start | bytes 1572872 | tf_op jit(solution)/shard_map/ppermute | solution.py:409
  165.8 13.5 %collective-permute-start.37 = (bf16[128,2048]{1,0:T(8,128)(2,1)S(1)}, bf16[128,2048]{1,0:T(8,128)(2,1)S(1)}, u32[]{:S(2)}, u32[]{:S(2)}) collective-permute-start(bf16[128,2048]{1,0:T(8,128)(2,1)S(1)} %get-tuple-element.170), channel_id=1, source_target_pairs={{0,1},{1,3},{3,5},{5,7},{7,6},{6,4},{4,2},{2,0},{8,10},{9,8},{11,9... | collective-permute-start | bytes 1572872 | tf_op jit(solution)/shard_map/ppermute | solution.py:409
  166.8 12.4 %collective-permute-start.38 = (bf16[128,2048]{1,0:T(8,128)(2,1)S(1)}, bf16[128,2048]{1,0:T(8,128)(2,1)S(1)}, u32[]{:S(2)}, u32[]{:S(2)}) collective-permute-start(bf16[128,2048]{1,0:T(8,128)(2,1)S(1)} %get-tuple-element.171), channel_id=1, source_target_pairs={{0,2},{1,0},{3,1},{5,3},{7,5},{6,7},{4,6},{2,4},{8,9},{9,11},{11,1... | collective-permute-start | bytes 1572872 | tf_op jit(solution)/shard_map/ppermute | solution.py:406
  (32 other events, 262.5 us)

commit v3 on v2

--- a/solution.py
+++ b/solution.py
@@ -147,8 +147,8 @@
 
 def swiglu_grads(sums, saved, where, n, q):
     m, h = sums[0].shape
-    cuts = 2 if (h // 2) % 128 == 0 else 1
-    wide = h // cuts
+    wide = 256 if h % 256 == 0 else 128
+    cuts = h // wide
     ns, nt = len(saved), len(sums)
 
     def body(i_ref, *refs):
@@ -305,32 +305,58 @@
     blk = rows // nr
     per = 4 if nr % 4 == 0 else 2
     tile = per * blk
+    tiles = rows // tile
     wide = 2 * blk
     nl, n = len(lhs), len(rhs)
 
     def body(m_ref, p_ref, *refs):
         lefts, rights = refs[:nl], refs[nl : nl + n]
-        o_ref, r_ref, l_ref = refs[nl + n :]
+        o_ref, r_ref, l_ref, l_sem, r_sem = refs[nl + n :]
         i = pl.program_id(0)
+
+        def left_copies(t):
+            at, out = 0, []
+            src = pl.ds(pl.multiple_of(t * tile, tile), tile)
+            for j, x in enumerate(lefts):
+                dst = l_ref.at[t, :, at : at + x.shape[1]]
+                out.append(pltpu.make_async_copy(x.at[src], dst, l_sem.at[t, j]))
+                at += x.shape[1]
+            return out
+
+        def right_copies():
+            at, out = 0, []
+            for t, x in enumerate(rights):
+                x = x if pick is None else x.at[pick]
+                m = x.shape[0]
+                if places is None:
+                    dst = r_ref.at[at : at + m]
+                else:
+                    dst = r_ref.at[pl.ds(pl.multiple_of(p_ref[places + t] * m, m), m)]
+                out.append(pltpu.make_async_copy(x, dst, r_sem.at[t]))
+                at += m
+            return out
 
         @pl.when(i == 0)
         def _():
-            if places is None:
-                stack_rows(r_ref, [r if pick is None else r.at[0] for r in rights])
-            else:
-                for t, r in enumerate(rights):
-                    m = r.shape[0]
-                    r_ref[pl.ds(pl.multiple_of(p_ref[places + t] * m, m), m)] = r[...]
-
-        if nl > 1:
-            at = 0
-            for r in lefts:
-                l_ref[:, at : at + r.shape[1]] = r[...]
-                at += r.shape[1]
-        left = l_ref if nl > 1 else lefts[0]
+            first = left_copies(0) + right_copies()
+            for copy in first:
+                copy.start()
+            for copy in first:
+                copy.wait()
+
+        @pl.when(i > 0)
+        def _():
+            for copy in left_copies(i):
+                copy.wait()
+
+        @pl.when(i + 1 < tiles)
+        def _():
+            for copy in left_copies(i + 1):
+                copy.start()
+
         for c in range(cols // wide):
             out = lax.dot_general(
-                left[...], r_ref[:, c * wide : (c + 1) * wide], NN, preferred_element_type=F32
+                l_ref[i], r_ref[:, c * wide : (c + 1) * wide], NN, preferred_element_type=F32
             )
             for a in range(per):
                 for s in range(2):
@@ -339,25 +365,17 @@
                     at = slice((2 * c + s) * blk, (2 * c + s + 1) * blk)
                     o_ref[ra, at] = (out[ra, cs] * keep).astype(BF16)
 
-    specs = [pl.BlockSpec((tile, x.shape[1]), lambda i: (i, 0)) for x in lhs]
-    for r in rhs:
-        if pick is None:
-            specs.append(whole_spec(r))
-        else:
-            specs.append(
-                pl.BlockSpec(
-                    (1,) + r.shape[1:], lambda i: (pick, 0, 0), pipeline_mode=pl.Buffered(1)
-                )
-            )
     return pl.pallas_call(
         body,
-        grid=(rows // tile,),
-        in_specs=[smem_spec(), smem_spec()] + specs,
+        grid=(tiles,),
+        in_specs=[smem_spec(), smem_spec()] + [pl.BlockSpec(memory_space=pl.ANY)] * (nl + n),
         out_specs=pl.BlockSpec((tile, cols), lambda i: (i, 0)),
         out_shape=jax.ShapeDtypeStruct((rows, cols), BF16),
         scratch_shapes=[
             pltpu.VMEM((k, cols), BF16),
-            pltpu.VMEM((tile, k) if nl > 1 else (16, 128), BF16),
+            pltpu.VMEM((tiles, tile, k), BF16),
+            pltpu.SemaphoreType.DMA((tiles, nl)),
+            pltpu.SemaphoreType.DMA((n,)),
         ],
         compiler_params=params(20),
         cost_estimate=cost(2 * rows * cols * k, 2 * (rows * k + cols * k + rows * cols)),
@@ -446,7 +464,7 @@
 
     def chip_sum(n):
         chip = (terms[n][0] + terms[n][1].astype(F32)).astype(BF16)
-        return jnp.pad(chip, ((0, 0), (0, 128)))
+        return chip if n == last else jnp.pad(chip, ((0, 0), (0, 128)))
 
     def grads(n, after):
         sums = terms[n] + others[n]

time: 181 us -> 187 us (1.033)
  Pallas kernels: 118 us -> 126 us
  waiting for transfers between devices: 21.1 us -> 19.2 us
    pallas_call x3, Pallas kernels: 33.8 us -> 40.4 us  [weight_grad(): pl.pallas_call(body, grid=(tiles,), in_specs=[smem_spec(), smem_spec()] +...]
  transfers between devices with their start and end apart: 39 -> 39, of which waited for: 9 -> 9; matrix products, arithmetic and copies ran while one was open for 2% -> 2% of each run, Pallas kernels for 64% -> 66%
where the time goes in v3:
time: 187 us; the launch traced here: 186 us
  Pallas kernels  126 us (67%)
  starting transfers between devices  32.4 us (17%)
  waiting for transfers between devices  19.2 us (10%)
  local copies, waits for them, and re-layouts  5.05 us (3%)
  other arithmetic  2.43 us (1%)
    pallas_call x3, Pallas kernels, weight_grad(): pl.pallas_call(body, grid=(tiles,), in_specs=[smem_spec(), smem_spec()] +...  40.4 us
    pallas_call x3, Pallas kernels, input_part(): pl.pallas_call(body, grid=(tiles,), in_specs=[smem_spec(), anywhere, anyw...  27 us
    pallas_call x4, Pallas kernels, hidden_part(): pl.pallas_call(body, grid=(h // tile,), in_specs=[smem_spec(), smem_spec(...  23.9 us
    pallas_call x2, Pallas kernels, turned_weight(): pl.pallas_call(body, grid=(d // tile,), in_specs=[smem_spec(), smem_spec(...  18.5 us
    ppermute x11, starting transfers between devices, from_ahead(): return lax.ppermute(x, ('row', 'col'), back)  14.8 us
    pallas_call x4, Pallas kernels, swiglu_grads(): pl.pallas_call(body, in_specs=[smem_spec()] + [anywhere] * (2 * ns + nt),...  10.6 us
    ppermute x6, waiting for transfers between devices, shift_y(): lax.ppermute(x, 'row', [(r, (r // 2 + s) % ny * 2 + r % 2) for r in range...  10.5 us
    ppermute x6, starting transfers between devices, shift_y(): lax.ppermute(x, 'row', [(r, (r // 2 + s) % ny * 2 + r % 2) for r in range...  8.1 us
  transfers between devices with their start and end apart: 39, of which 9 were waited for; matrix products, arithmetic and copies ran while one was open for 2% of the time, Pallas kernels for 66%

profile of v3, /device:TPU:0, one launch (start us, length us, event | category | flops | bytes accessed | tf_op | source)
XLA Modules:
  0.0 186.0 jit_solution(17904854277224842875)
XLA Ops:
  0.6 3.0 %collective-permute-start.4 = (bf16[256,1792]{1,0:T(8,128)(2,1)}, bf16[256,1792]{1,0:T(8,128)(2,1)S(1)}, u32[]{:S(2)}, u32[]{:S(2)}) collective-permute-start(bf16[256,1792]{1,0:T(8,128)(2,1)} %refs_0_.9), channel_id=1, source_target_pairs={{0,16},{8,24},{16,0},{24,8},{1,17},{9,25},{17,1},{25,9},{2,18},{10... | collective-permute-start | bytes 2752520 | tf_op jit(solution)/shard_map/ppermute | solution.py:433
  3.7 1.5 collective-permute-start.1
  6.5 9.2 %turned_weight.2.wg_ref = bf16[8,1792,256]{2,1,0:T(8,128)(2,1)} custom-call(s32[13]{0:T(128)S(1)} %compare_select_fusion.14.at_ref.i_ref.p_ref, s32[16,14]{1,0:T(8,128)S(1)} %copy-done.9, bf16[2048,1792]{1,0:T(8,128)(2,1)} %w_ref.6), custom_call_target="tpu_custom_call" | custom-call | flops 896 | bytes 3584 | tf_op jit(solution)/shard_map/turned_weight/pallas_call | solution.py:240
  15.8 2.0 %copy.14 = bf16[128,2048]{0,1:T(8,128)(2,1)} copy(bf16[128,2048]{1,0:T(8,128)(2,1)} %param.10) | data formatting | bytes 1048576 | tf_op args[0]
  18.6 1.6 collective-permute-start.2
  20.6 5.9 %hidden_part.4 = (f32[128,1792]{1,0:T(8,128)S(1)}, bf16[128,1792]{1,0:T(8,128)(2,1)S(1)}) custom-call(s32[13]{0:T(128)S(1)} %compare_select_fusion.14.at_ref.i_ref.p_ref, s32[14,16]{1,0:T(8,128)S(1)} %copy-done.8, bf16[1792,2048]{1,0:T(8,128)(2,1)} %w_ref.11, bf16[128,2048]{1,0:T(8,128)(2,1)S(1)} %collective-permute-done.a_ref.refs_1_, ...), custom_call_target="tpu_custom_call" | custom-call | flops 458752 | bytes 2256 | tf_op jit(solution)/shard_map/hidden_part/pallas_call | solution.py:84
  27.2 9.2 %turned_weight.3.wu_ref = bf16[8,1792,256]{2,1,0:T(8,128)(2,1)} custom-call(s32[13]{0:T(128)S(1)} %compare_select_fusion.14.at_ref.i_ref.p_ref, s32[16,14]{1,0:T(8,128)S(1)} %copy-done.11, bf16[2048,1792]{1,0:T(8,128)(2,1)} %w_ref.8), custom_call_target="tpu_custom_call" | custom-call | flops 896 | bytes 3584 | tf_op jit(solution)/shard_map/turned_weight/pallas_call | solution.py:240
  36.5 7.4 %collective-permute-done.5.refs_5_ = bf16[256,1792]{1,0:T(8,128)(2,1)S(1)} collective-permute-done((bf16[256,1792]{1,0:T(8,128)(2,1)}, bf16[256,1792]{1,0:T(8,128)(2,1)S(1)}, u32[]{:S(2)}, u32[]{:S(2)}) %collective-permute-start.5) | collective-permute-done | bytes 917536 | tf_op jit(solution)/shard_map/ppermute | solution.py:433
  43.9 1.8 collective-permute-start.8
  46.2 1.8 collective-permute-start.7
  47.9 5.9 %hidden_part.5 = (f32[128,1792]{1,0:T(8,128)S(1)}, bf16[128,1792]{1,0:T(8,128)(2,1)S(1)}) custom-call(s32[13]{0:T(128)S(1)} %compare_select_fusion.14.at_ref.i_ref.p_ref, s32[14,16]{1,0:T(8,128)S(1)} %copy-done.8, bf16[1792,2048]{1,0:T(8,128)(2,1)} %w_ref.11, bf16[128,2048]{1,0:T(8,128)(2,1)S(1)} %collective-permute-done.2.a_ref.refs_3_, ...), custom_call_target="tpu_custom_call" | custom-call | flops 458752 | bytes 2256 | tf_op jit(solution)/shard_map/hidden_part/pallas_call | solution.py:84
  55.9 2.1 %collective-permute-done.7.refs_10_ = bf16[128,1920]{1,0:T(8,128)(2,1)S(1)} collective-permute-done((bf16[128,1920]{1,0:T(8,128)(2,1)S(1)}, bf16[128,1920]{1,0:T(8,128)(2,1)S(1)}, u32[]{:S(2)}, u32[]{:S(2)}) %collective-permute-start.7) | collective-permute-done | bytes 491552 | tf_op jit(solution)/shard_map/ppermute | solution.py:433
  59.7 1.6 collective-permute-start.12
  61.3 5.9 %hidden_part.6 = (f32[128,1792]{1,0:T(8,128)S(1)}, bf16[128,1792]{1,0:T(8,128)(2,1)S(1)}) custom-call(s32[13]{0:T(128)S(1)} %compare_select_fusion.14.at_ref.i_ref.p_ref, s32[14,16]{1,0:T(8,128)S(1)} %copy-done.8, bf16[1792,2048]{1,0:T(8,128)(2,1)} %w_ref.11, bf16[128,2048]{1,0:T(8,128)(2,1)S(1)} %collective-permute-done.8.a_ref.refs_5_, ...), custom_call_target="tpu_custom_call" | custom-call | flops 458752 | bytes 2256 | tf_op jit(solution)/shard_map/hidden_part/pallas_call | solution.py:84
  69.5 5.2 %activation.1.refs_0_ = bf16[1792,1024]{1,0:T(8,128)(2,1)S(1)} custom-call(s32[13]{0:T(128)S(1)} %compare_select_fusion.14.at_ref.i_ref.p_ref, bf16[256,1792]{1,0:T(8,128)(2,1)} %refs_0_.9, bf16[256,1792]{1,0:T(8,128)(2,1)} %refs_1_.9, bf16[256,1792]{1,0:T(8,128)(2,1)} %copy-done.17, bf16[256,1792]{1,0:T(8,128)(2,1)} %copy-done.18, ...), custom_call_target="tpu_custom_call" | custom-call | flops 4480 | bytes 2688 | tf_op jit(solution)/shard_map/activation/pallas_call | solution.py:135
  77.6 6.0 %hidden_part.7 = (f32[128,1792]{1,0:T(8,128)S(1)}, bf16[128,1792]{1,0:T(8,128)(2,1)S(1)}) custom-call(s32[13]{0:T(128)S(1)} %compare_select_fusion.14.at_ref.i_ref.p_ref, s32[14,16]{1,0:T(8,128)S(1)} %copy-done.8, bf16[1792,2048]{1,0:T(8,128)(2,1)} %w_ref.11, bf16[128,2048]{1,0:T(8,128)(2,1)S(1)} %copy-done.5, ...), custom_call_target="tpu_custom_call" | custom-call | flops 458752 | bytes 2256 | tf_op jit(solution)/shard_map/hidden_part/pallas_call | solution.py:84
  83.7 2.6 %swiglu_grads.4.refs_0_.refs_8_ = bf16[2,128,1792]{2,1,0:T(8,128)(2,1)S(1)} custom-call(s32[13]{0:T(128)S(1)} %compare_select_fusion.14.at_ref.i_ref.p_ref, bf16[256,1792]{1,0:T(8,128)(2,1)} %refs_0_.9, bf16[256,1792]{1,0:T(8,128)(2,1)} %refs_1_.9, bf16[256,1792]{1,0:T(8,128)(2,1)} %copy-done.17, bf16[256,1792]{1,0:T(8,128)(2,1)} %copy-done.18, ...), custom_call_target="tpu_custom_call" | custom-call | flops 1120 | bytes 784 | tf_op jit(solution)/shard_map/swiglu_grads/pallas_call | solution.py:205
  86.8 2.6 %swiglu_grads.5.refs_2_.refs_10_ = bf16[2,128,1792]{2,1,0:T(8,128)(2,1)S(1)} custom-call(s32[13]{0:T(128)S(1)} %compare_select_fusion.14.at_ref.i_ref.p_ref, bf16[256,1792]{1,0:T(8,128)(2,1)} %refs_0_.9, bf16[256,1792]{1,0:T(8,128)(2,1)} %refs_1_.9, bf16[256,1792]{1,0:T(8,128)(2,1)} %copy-done.17, bf16[256,1792]{1,0:T(8,128)(2,1)} %copy-done.18, ...), custom_call_target="tpu_custom_call" | custom-call | flops 1120 | bytes 784 | tf_op jit(solution)/shard_map/swiglu_grads/pallas_call | solution.py:205
  89.9 1.6 collective-permute-start.21
  93.2 11.4 %weight_grad.3 = bf16[1792,2048]{1,0:T(8,128)(2,1)} custom-call(s32[14,16]{1,0:T(8,128)S(1)} %copy-done.8, s32[13]{0:T(128)S(1)} %compare_select_fusion.14.at_ref.i_ref.p_ref, bf16[1792,1024]{1,0:T(8,128)(2,1)S(1)} %activation.1.refs_0_, bf16[128,2048]{1,0:T(8,128)(2,1)S(1)} %collective-permute-done.a_ref.refs_1_, ...), custom_call_target="tpu_custom_call" | custom-call | flops 1835008 | bytes 3712 | tf_op jit(solution)/shard_map/weight_grad/pallas_call | solution.py:368
  105.1 2.6 %swiglu_grads.6.refs_0_.refs_14_ = bf16[2,128,1792]{2,1,0:T(8,128)(2,1)S(1)} custom-call(s32[13]{0:T(128)S(1)} %compare_select_fusion.14.at_ref.i_ref.p_ref, bf16[256,1792]{1,0:T(8,128)(2,1)} %refs_0_.9, bf16[256,1792]{1,0:T(8,128)(2,1)} %refs_1_.9, bf16[256,1792]{1,0:T(8,128)(2,1)} %copy-done.17, bf16[256,1792]{1,0:T(8,128)(2,1)} %copy-done.18, ...), custom_call_target="tpu_custom_call" | custom-call | flops 1120 | bytes 784 | tf_op jit(solution)/shard_map/swiglu_grads/pallas_call | solution.py:205
  107.9 1.6 collective-permute-start.28
  109.9 2.9 %swiglu_grads.7.refs_0_.refs_12_ = bf16[2,128,1792]{2,1,0:T(8,128)(2,1)S(1)} custom-call(s32[13]{0:T(128)S(1)} %compare_select_fusion.14.at_ref.i_ref.p_ref, bf16[256,1792]{1,0:T(8,128)(2,1)} %refs_0_.9, bf16[256,1792]{1,0:T(8,128)(2,1)} %refs_1_.9, bf16[256,1792]{1,0:T(8,128)(2,1)} %copy-done.17, bf16[256,1792]{1,0:T(8,128)(2,1)} %copy-done.18, ...), custom_call_target="tpu_custom_call" | custom-call | flops 1120 | bytes 784 | tf_op jit(solution)/shard_map/swiglu_grads/pallas_call | solution.py:205
  112.9 8.2 %input_part.3 = f32[2,128,2048]{2,1,0:T(8,128)S(1)} custom-call(s32[13]{0:T(128)S(1)} %compare_select_fusion.14.at_ref.i_ref.p_ref, bf16[8,1792,256]{2,1,0:T(8,128)(2,1)} %turned_weight.2.wg_ref, bf16[8,1792,256]{2,1,0:T(8,128)(2,1)} %turned_weight.3.wu_ref, bf16[2,128,1792]{2,1,0:T(8,128)(2,1)S(1)} %swiglu_grads.6.refs_0_.refs_14_, ...), custom_call_target="tpu_custom_call" | custom-call | flops 917504 | bytes 4544 | tf_op jit(solution)/shard_map/input_part/pallas_call | solution.py:284
  121.2 1.5 collective-permute-done.28.refs_4_
  124.7 7.5 %input_part.4 = f32[2,128,2048]{2,1,0:T(8,128)S(1)} custom-call(s32[13]{0:T(128)S(1)} %compare_select_fusion.14.at_ref.i_ref.p_ref, bf16[8,1792,256]{2,1,0:T(8,128)(2,1)} %turned_weight.2.wg_ref, bf16[8,1792,256]{2,1,0:T(8,128)(2,1)} %turned_weight.3.wu_ref, bf16[2,128,1792]{2,1,0:T(8,128)(2,1)S(1)} %swiglu_grads.7.refs_0_.refs_12_, ...), custom_call_target="tpu_custom_call" | custom-call | flops 917504 | bytes 4544 | tf_op jit(solution)/shard_map/input_part/pallas_call | solution.py:284
  132.2 5.0 %collective-permute-done.30 = bf16[128,2048]{1,0:T(8,128)(2,1)S(1)} collective-permute-done((bf16[128,2048]{1,0:T(8,128)(2,1)S(1)}, bf16[128,2048]{1,0:T(8,128)(2,1)S(1)}, u32[]{:S(2)}, u32[]{:S(2)}) %collective-permute-start.30) | collective-permute-done | bytes 524320 | tf_op jit(solution)/shard_map/ppermute | solution.py:427
  137.4 1.6 collective-permute-start.33
  139.5 11.4 %input_part.5 = f32[4,128,2048]{2,1,0:T(8,128)S(1)} custom-call(s32[13]{0:T(128)S(1)} %compare_select_fusion.14.at_ref.i_ref.p_ref, bf16[8,1792,256]{2,1,0:T(8,128)(2,1)} %turned_weight.2.wg_ref, bf16[8,1792,256]{2,1,0:T(8,128)(2,1)} %turned_weight.3.wu_ref, bf16[2,128,1792]{2,1,0:T(8,128)(2,1)S(1)} %swiglu_grads.4.refs_0_.refs_8_, ...), custom_call_target="tpu_custom_call" | custom-call | flops 1835008 | bytes 5504 | tf_op jit(solution)/shard_map/input_part/pallas_call | solution.py:284
  151.4 1.6 collective-permute-start.36
  153.5 14.5 %weight_grad.4 = bf16[2048,1792]{1,0:T(8,128)(2,1)} custom-call(s32[16,14]{1,0:T(8,128)S(1)} %copy-done.10, s32[13]{0:T(128)S(1)} %compare_select_fusion.14.at_ref.i_ref.p_ref, bf16[2048,128]{1,0:T(8,128)(2,1)S(1)} %copy-done.7, bf16[2048,128]{1,0:T(8,128)(2,1)S(1)} %collective-permute-done.19.refs_1_, bf16[2048,128]{1,0:T(8,128)(2,1)} %collective-permute-done.21.refs_2_, ...), custom_call_target="tpu_custom_call" | custom-call | flops 1835008 | bytes 3712 | tf_op jit(solution)/shard_map/weight_grad/pallas_call | solution.py:368
  170.4 14.5 %weight_grad.5 = bf16[2048,1792]{1,0:T(8,128)(2,1)} custom-call(s32[16,14]{1,0:T(8,128)S(1)} %copy-done.11, s32[13]{0:T(128)S(1)} %compare_select_fusion.14.at_ref.i_ref.p_ref, bf16[2048,128]{1,0:T(8,128)(2,1)S(1)} %copy-done.7, bf16[2048,128]{1,0:T(8,128)(2,1)S(1)} %collective-permute-done.19.refs_1_, bf16[2048,128]{1,0:T(8,128)(2,1)} %collective-permute-done.21.refs_2_, ...), custom_call_target="tpu_custom_call" | custom-call | flops 1835008 | bytes 3712 | tf_op jit(solution)/shard_map/weight_grad/pallas_call | solution.py:368
  (129 shorter events, 23.3 us)
Async XLA Ops:
  0.6 26.0 %collective-permute-start.4 = (bf16[256,1792]{1,0:T(8,128)(2,1)}, bf16[256,1792]{1,0:T(8,128)(2,1)S(1)}, u32[]{:S(2)}, u32[]{:S(2)}) collective-permute-start(bf16[256,1792]{1,0:T(8,128)(2,1)} %refs_0_.9), channel_id=1, source_target_pairs={{0,16},{8,24},{16,0},{24,8},{1,17},{9,25},{17,1},{25,9},{2,18},{10... | collective-permute-start | bytes 2752520 | tf_op jit(solution)/shard_map/ppermute | solution.py:433
  3.7 14.9 %collective-permute-start.1 = (bf16[128,2048]{1,0:T(8,128)(2,1)}, bf16[128,2048]{1,0:T(8,128)(2,1)S(1)}, u32[]{:S(2)}, u32[]{:S(2)}) collective-permute-start(bf16[128,2048]{1,0:T(8,128)(2,1)} %refs_7_.1), channel_id=1, source_target_pairs={{0,1},{1,3},{3,5},{5,7},{7,6},{6,4},{4,2},{2,0},{8,10},{9,8},{11,9... | collective-permute-start | bytes 1572872 | tf_op jit(solution)/shard_map/ppermute | solution.py:427
  5.2 13.4 %collective-permute-start = (bf16[128,2048]{1,0:T(8,128)(2,1)}, bf16[128,2048]{1,0:T(8,128)(2,1)S(1)}, u32[]{:S(2)}, u32[]{:S(2)}) collective-permute-start(bf16[128,2048]{1,0:T(8,128)(2,1)} %refs_7_.1), channel_id=1, source_target_pairs={{0,2},{1,0},{3,1},{5,3},{7,5},{6,7},{4,6},{2,4},{8,9},{9,11},{11,1... | collective-permute-start | bytes 1572872 | tf_op jit(solution)/shard_map/ppermute | solution.py:424
  5.7 38.2 %collective-permute-start.5 = (bf16[256,1792]{1,0:T(8,128)(2,1)}, bf16[256,1792]{1,0:T(8,128)(2,1)S(1)}, u32[]{:S(2)}, u32[]{:S(2)}) collective-permute-start(bf16[256,1792]{1,0:T(8,128)(2,1)} %refs_1_.9), channel_id=1, source_target_pairs={{0,16},{8,24},{16,0},{24,8},{1,17},{9,25},{17,1},{25,9},{2,18},{10... | collective-permute-start | bytes 2752520 | tf_op jit(solution)/shard_map/ppermute | solution.py:433
  18.6 25.3 %collective-permute-start.2 = (bf16[128,2048]{1,0:T(8,128)(2,1)S(1)}, bf16[128,2048]{1,0:T(8,128)(2,1)S(1)}, u32[]{:S(2)}, u32[]{:S(2)}) collective-permute-start(bf16[128,2048]{1,0:T(8,128)(2,1)S(1)} %collective-permute-done.a_ref.refs_1_), channel_id=1, source_target_pairs={{0,2},{1,0},{3,1},{5,3},{7,5},{6,7},{4,6},{2,4},{8,9},{9,11},{11,1... | collective-permute-start | bytes 1572872 | tf_op jit(solution)/shard_map/ppermute | solution.py:424
  20.2 23.7 %collective-permute-start.3 = (bf16[128,2048]{1,0:T(8,128)(2,1)S(1)}, bf16[128,2048]{1,0:T(8,128)(2,1)S(1)}, u32[]{:S(2)}, u32[]{:S(2)}) collective-permute-start(bf16[128,2048]{1,0:T(8,128)(2,1)S(1)} %collective-permute-done.1.b_ref.refs_2_), channel_id=1, source_target_pairs={{0,1},{1,3},{3,5},{5,7},{7,6},{6,4},{4,2},{2,0},{8,10},{9,8},{11,9... | collective-permute-start | bytes 1572872 | tf_op jit(solution)/shard_map/ppermute | solution.py:427
  26.6 17.3 %collective-permute-start.6 = (bf16[128,1792]{1,0:T(8,128)(2,1)S(1)}, bf16[128,1792]{1,0:T(8,128)(2,1)S(1)}, u32[]{:S(2)}, u32[]{:S(2)}) collective-permute-start(bf16[128,1792]{1,0:T(8,128)(2,1)S(1)} %get-tuple-element.92), channel_id=1, source_target_pairs={{0,8},{8,0},{16,24},{24,16},{1,9},{9,1},{17,25},{25,17},{2,10},{10... | collective-permute-start | bytes 1376264 | tf_op jit(solution)/shard_map/ppermute | solution.py:430
  26.7 27.3 %collective-permute-start.10 = (bf16[256,1792]{1,0:T(8,128)(2,1)S(1)}, bf16[256,1792]{1,0:T(8,128)(2,1)S(1)}, u32[]{:S(2)}, u32[]{:S(2)}) collective-permute-start(bf16[256,1792]{1,0:T(8,128)(2,1)S(1)} %copy-done.12), channel_id=1, source_target_pairs={{0,8},{8,0},{16,24},{24,16},{1,9},{9,1},{17,25},{25,17},{2,10},{10... | collective-permute-start | bytes 2752520 | tf_op jit(solution)/shard_map/ppermute | solution.py:430
  43.9 14.3 %collective-permute-start.8 = (bf16[128,2048]{1,0:T(8,128)(2,1)S(1)}, bf16[128,2048]{1,0:T(8,128)(2,1)S(1)}, u32[]{:S(2)}, u32[]{:S(2)}) collective-permute-start(bf16[128,2048]{1,0:T(8,128)(2,1)S(1)} %collective-permute-done.2.a_ref.refs_3_), channel_id=1, source_target_pairs={{0,2},{1,0},{3,1},{5,3},{7,5},{6,7},{4,6},{2,4},{8,9},{9,11},{11,1... | collective-permute-start | bytes 1572872 | tf_op jit(solution)/shard_map/ppermute | solution.py:424
  45.8 12.4 %collective-permute-start.9 = (bf16[128,2048]{1,0:T(8,128)(2,1)S(1)}, bf16[128,2048]{1,0:T(8,128)(2,1)S(1)}, u32[]{:S(2)}, u32[]{:S(2)}) collective-permute-start(bf16[128,2048]{1,0:T(8,128)(2,1)S(1)} %collective-permute-done.3.b_ref.refs_4_), channel_id=1, source_target_pairs={{0,1},{1,3},{3,5},{5,7},{7,6},{6,4},{4,2},{2,0},{8,10},{9,8},{11,9... | collective-permute-start | bytes 1572872 | tf_op jit(solution)/shard_map/ppermute | solution.py:427
  54.0 13.3 %collective-permute-start.14 = (bf16[256,1792]{1,0:T(8,128)(2,1)S(1)}, bf16[256,1792]{1,0:T(8,128)(2,1)S(1)}, u32[]{:S(2)}, u32[]{:S(2)}) collective-permute-start(bf16[256,1792]{1,0:T(8,128)(2,1)S(1)} %copy-done.13), channel_id=1, source_target_pairs={{0,8},{8,0},{16,24},{24,16},{1,9},{9,1},{17,25},{25,17},{2,10},{10... | collective-permute-start | bytes 2752520 | tf_op jit(solution)/shard_map/ppermute | solution.py:430
  58.2 16.5 %collective-permute-start.13 = (bf16[128,2048]{1,0:T(8,128)(2,1)S(1)}, bf16[128,2048]{1,0:T(8,128)(2,1)S(1)}, u32[]{:S(2)}, u32[]{:S(2)}) collective-permute-start(bf16[128,2048]{1,0:T(8,128)(2,1)S(1)} %collective-permute-done.8.a_ref.refs_5_), channel_id=1, source_target_pairs={{0,2},{1,0},{3,1},{5,3},{7,5},{6,7},{4,6},{2,4},{8,9},{9,11},{11,1... | collective-permute-start | bytes 1572872 | tf_op jit(solution)/shard_map/ppermute | solution.py:424
  59.7 15.0 %collective-permute-start.12 = (bf16[128,1920]{1,0:T(8,128)(2,1)S(1)}, bf16[128,1920]{1,0:T(8,128)(2,1)S(1)}, u32[]{:S(2)}, u32[]{:S(2)}) collective-permute-start(bf16[128,1920]{1,0:T(8,128)(2,1)S(1)} %pad.11), channel_id=1, source_target_pairs={{0,16},{8,24},{16,0},{24,8},{1,17},{9,25},{17,1},{25,9},{2,18},{10... | collective-permute-start | bytes 1474568 | tf_op jit(solution)/shard_map/ppermute | solution.py:433
  74.8 15.2 %collective-permute-start.19 = (bf16[2048,128]{1,0:T(8,128)(2,1)S(1)}, bf16[2048,128]{1,0:T(8,128)(2,1)S(1)}, u32[]{:S(2)}, u32[]{:S(2)}) collective-permute-start(bf16[2048,128]{1,0:T(8,128)(2,1)S(1)} %bitcast.31), channel_id=1, source_target_pairs={{0,1},{1,3},{3,5},{5,7},{7,6},{6,4},{4,2},{2,0},{8,10},{9,8},{11,9... | collective-permute-start | bytes 1572872 | tf_op jit(solution)/shard_map/ppermute | solution.py:427
  76.0 13.9 %collective-permute-start.18 = (bf16[2048,128]{1,0:T(8,128)(2,1)S(1)}, bf16[2048,128]{1,0:T(8,128)(2,1)S(1)}, u32[]{:S(2)}, u32[]{:S(2)}) collective-permute-start(bf16[2048,128]{1,0:T(8,128)(2,1)S(1)} %bitcast.32), channel_id=1, source_target_pairs={{0,2},{1,0},{3,1},{5,3},{7,5},{6,7},{4,6},{2,4},{8,9},{9,11},{11,1... | collective-permute-start | bytes 1572872 | tf_op jit(solution)/shard_map/ppermute | solution.py:424
  77.0 12.9 %collective-permute-start.20 = (bf16[128,1920]{1,0:T(8,128)(2,1)S(1)}, bf16[128,1920]{1,0:T(8,128)(2,1)S(1)}, u32[]{:S(2)}, u32[]{:S(2)}) collective-permute-start(bf16[128,1920]{1,0:T(8,128)(2,1)S(1)} %pad.12), channel_id=1, source_target_pairs={{0,16},{8,24},{16,0},{24,8},{1,17},{9,25},{17,1},{25,9},{2,18},{10... | collective-permute-start | bytes 1474568 | tf_op jit(solution)/shard_map/ppermute | solution.py:433
  86.2 18.9 %collective-permute-start.25 = (bf16[2,128,1792]{2,1,0:T(8,128)(2,1)S(1)}, bf16[2,128,1792]{2,1,0:T(8,128)(2,1)S(1)}, u32[]{:S(2)}, u32[]{:S(2)}) collective-permute-start(bf16[2,128,1792]{2,1,0:T(8,128)(2,1)S(1)} %swiglu_grads.4.refs_0_.refs_8_), channel_id=1, source_target_pairs={{0,8},{8,0},{16,24},{24,16},{1,9},{9,1},{17,25},{25,17},{2,10},{10... | collective-permute-start | bytes 2752520 | tf_op jit(solution)/shard_map/ppermute | solution.py:430
  89.9 15.2 %collective-permute-start.21 = (bf16[2048,128]{1,0:T(8,128)(2,1)S(1)}, bf16[2048,128]{1,0:T(8,128)(2,1)}, u32[]{:S(2)}, u32[]{:S(2)}) collective-permute-start(bf16[2048,128]{1,0:T(8,128)(2,1)S(1)} %collective-permute-done.18.refs_0_), channel_id=1, source_target_pairs={{0,2},{1,0},{3,1},{5,3},{7,5},{6,7},{4,6},{2,4},{8,9},{9,11},{11,1... | collective-permute-start | bytes 1572872 | tf_op jit(solution)/shard_map/ppermute | solution.py:424
  91.6 13.6 %collective-permute-start.22 = (bf16[2048,128]{1,0:T(8,128)(2,1)S(1)}, bf16[2048,128]{1,0:T(8,128)(2,1)}, u32[]{:S(2)}, u32[]{:S(2)}) collective-permute-start(bf16[2048,128]{1,0:T(8,128)(2,1)S(1)} %collective-permute-done.19.refs_1_), channel_id=1, source_target_pairs={{0,1},{1,3},{3,5},{5,7},{7,6},{6,4},{4,2},{2,0},{8,10},{9,8},{11,9... | collective-permute-start | bytes 1572872 | tf_op jit(solution)/shard_map/ppermute | solution.py:427
  92.0 13.1 %collective-permute-start.26 = (bf16[2,128,1792]{2,1,0:T(8,128)(2,1)S(1)}, bf16[2,128,1792]{2,1,0:T(8,128)(2,1)S(1)}, u32[]{:S(2)}, u32[]{:S(2)}) collective-permute-start(bf16[2,128,1792]{2,1,0:T(8,128)(2,1)S(1)} %swiglu_grads.5.refs_2_.refs_10_), channel_id=1, source_target_pairs={{0,8},{8,0},{16,24},{24,16},{1,9},{9,1},{17,25},{25,17},{2,10},{10... | collective-permute-start | bytes 2752520 | tf_op jit(solution)/shard_map/ppermute | solution.py:430
  92.1 13.0 %collective-permute-start.24 = (bf16[128,1792]{1,0:T(8,128)(2,1)S(1)}, bf16[128,1792]{1,0:T(8,128)(2,1)S(1)}, u32[]{:S(2)}, u32[]{:S(2)}) collective-permute-start(bf16[128,1792]{1,0:T(8,128)(2,1)S(1)} %add_convert_fusion), channel_id=1, source_target_pairs={{0,16},{8,24},{16,0},{24,8},{1,17},{9,25},{17,1},{25,9},{2,18},{10... | collective-permute-start | bytes 1376264 | tf_op jit(solution)/shard_map/ppermute | solution.py:433
  107.9 14.8 %collective-permute-start.28 = (bf16[2048,128]{1,0:T(8,128)(2,1)}, bf16[2048,128]{1,0:T(8,128)(2,1)}, u32[]{:S(2)}, u32[]{:S(2)}) collective-permute-start(bf16[2048,128]{1,0:T(8,128)(2,1)} %collective-permute-done.21.refs_2_), channel_id=1, source_target_pairs={{0,2},{1,0},{3,1},{5,3},{7,5},{6,7},{4,6},{2,4},{8,9},{9,11},{11,1... | collective-permute-start | bytes 1572872 | tf_op jit(solution)/shard_map/ppermute | solution.py:424
  109.5 13.2 %collective-permute-start.29 = (bf16[2048,128]{1,0:T(8,128)(2,1)}, bf16[2048,128]{1,0:T(8,128)(2,1)}, u32[]{:S(2)}, u32[]{:S(2)}) collective-permute-start(bf16[2048,128]{1,0:T(8,128)(2,1)} %collective-permute-done.22.refs_3_), channel_id=1, source_target_pairs={{0,1},{1,3},{3,5},{5,7},{7,6},{6,4},{4,2},{2,0},{8,10},{9,8},{11,9... | collective-permute-start | bytes 1572872 | tf_op jit(solution)/shard_map/ppermute | solution.py:427
  112.8 11.9 %collective-permute-start.31 = (bf16[2,128,1792]{2,1,0:T(8,128)(2,1)S(1)}, bf16[2,128,1792]{2,1,0:T(8,128)(2,1)S(1)}, u32[]{:S(2)}, u32[]{:S(2)}) collective-permute-start(bf16[2,128,1792]{2,1,0:T(8,128)(2,1)S(1)} %swiglu_grads.7.refs_0_.refs_12_), channel_id=1, source_target_pairs={{0,8},{8,0},{16,24},{24,16},{1,9},{9,1},{17,25},{25,17},{2,10},{10... | collective-permute-start | bytes 2752520 | tf_op jit(solution)/shard_map/ppermute | solution.py:430
  122.7 14.5 %collective-permute-start.30 = (bf16[128,2048]{1,0:T(8,128)(2,1)S(1)}, bf16[128,2048]{1,0:T(8,128)(2,1)S(1)}, u32[]{:S(2)}, u32[]{:S(2)}) collective-permute-start(bf16[128,2048]{1,0:T(8,128)(2,1)S(1)} %fusion.7), channel_id=1, source_target_pairs={{0,1},{1,3},{3,5},{5,7},{7,6},{6,4},{4,2},{2,0},{8,10},{9,8},{11,9... | collective-permute-start | bytes 1572872 | tf_op jit(solution)/shard_map/ppermute | solution.py:427
  123.6 27.3 %collective-permute-start.34 = (bf16[2048,128]{1,0:T(8,128)(2,1)}, bf16[2048,128]{1,0:T(8,128)(2,1)S(1)}, u32[]{:S(2)}, u32[]{:S(2)}) collective-permute-start(bf16[2048,128]{1,0:T(8,128)(2,1)} %collective-permute-done.28.refs_4_), channel_id=1, source_target_pairs={{0,2},{1,0},{3,1},{5,3},{7,5},{6,7},{4,6},{2,4},{8,9},{9,11},{11,1... | collective-permute-start | bytes 1572872 | tf_op jit(solution)/shard_map/ppermute | solution.py:424
  137.4 13.6 %collective-permute-start.33 = (bf16[128,2048]{1,0:T(8,128)(2,1)S(1)}, bf16[128,2048]{1,0:T(8,128)(2,1)S(1)}, u32[]{:S(2)}, u32[]{:S(2)}) collective-permute-start(bf16[128,2048]{1,0:T(8,128)(2,1)S(1)} %fusion.8), channel_id=1, source_target_pairs={{0,2},{1,0},{3,1},{5,3},{7,5},{6,7},{4,6},{2,4},{8,9},{9,11},{11,1... | collective-permute-start | bytes 1572872 | tf_op jit(solution)/shard_map/ppermute | solution.py:424
  139.0 12.1 %collective-permute-start.32 = (bf16[128,2048]{1,0:T(8,128)(2,1)S(1)}, bf16[128,2048]{1,0:T(8,128)(2,1)S(1)}, u32[]{:S(2)}, u32[]{:S(2)}) collective-permute-start(bf16[128,2048]{1,0:T(8,128)(2,1)S(1)} %fusion.4), channel_id=1, source_target_pairs={{0,1},{1,3},{3,5},{5,7},{7,6},{6,4},{4,2},{2,0},{8,10},{9,8},{11,9... | collective-permute-start | bytes 1572872 | tf_op jit(solution)/shard_map/ppermute | solution.py:427
  151.4 16.5 %collective-permute-start.36 = (bf16[128,2048]{1,0:T(8,128)(2,1)S(1)}, bf16[128,2048]{1,0:T(8,128)(2,1)S(1)}, u32[]{:S(2)}, u32[]{:S(2)}) collective-permute-start(bf16[128,2048]{1,0:T(8,128)(2,1)S(1)} %get-tuple-element.172), channel_id=1, source_target_pairs={{0,2},{1,0},{3,1},{5,3},{7,5},{6,7},{4,6},{2,4},{8,9},{9,11},{11,1... | collective-permute-start | bytes 1572872 | tf_op jit(solution)/shard_map/ppermute | solution.py:424
  153.0 15.0 %collective-permute-start.35 = (bf16[128,2048]{1,0:T(8,128)(2,1)S(1)}, bf16[128,2048]{1,0:T(8,128)(2,1)S(1)}, u32[]{:S(2)}, u32[]{:S(2)}) collective-permute-start(bf16[128,2048]{1,0:T(8,128)(2,1)S(1)} %get-tuple-element.173), channel_id=1, source_target_pairs={{0,1},{1,3},{3,5},{5,7},{7,6},{6,4},{4,2},{2,0},{8,10},{9,8},{11,9... | collective-permute-start | bytes 1572872 | tf_op jit(solution)/shard_map/ppermute | solution.py:427
  168.3 16.5 %collective-permute-start.37 = (bf16[128,2048]{1,0:T(8,128)(2,1)S(1)}, bf16[128,2048]{1,0:T(8,128)(2,1)S(1)}, u32[]{:S(2)}, u32[]{:S(2)}) collective-permute-start(bf16[128,2048]{1,0:T(8,128)(2,1)S(1)} %get-tuple-element.170), channel_id=1, source_target_pairs={{0,1},{1,3},{3,5},{5,7},{7,6},{6,4},{4,2},{2,0},{8,10},{9,8},{11,9... | collective-permute-start | bytes 1572872 | tf_op jit(solution)/shard_map/ppermute | solution.py:427
  169.3 15.5 %collective-permute-start.38 = (bf16[128,2048]{1,0:T(8,128)(2,1)S(1)}, bf16[128,2048]{1,0:T(8,128)(2,1)S(1)}, u32[]{:S(2)}, u32[]{:S(2)}) collective-permute-start(bf16[128,2048]{1,0:T(8,128)(2,1)S(1)} %get-tuple-element.171), channel_id=1, source_target_pairs={{0,2},{1,0},{3,1},{5,3},{7,5},{6,7},{4,6},{2,4},{8,9},{9,11},{11,1... | collective-permute-start | bytes 1572872 | tf_op jit(solution)/shard_map/ppermute | solution.py:424
  (32 other events, 261.5 us)

commit v4 on v2

--- a/solution.py
+++ b/solution.py
@@ -142,7 +142,7 @@
         compiler_params=params(16),
         cost_estimate=cost(10 * h * n * m, 6 * h * n * m),
         name="activation",
-    )(where, *[in_hbm(x) for pair in saved for x in pair])
+    )(where, *[in_hbm(x) for x in saved[0]], *[x for pair in saved[1:] for x in pair])
 
 
 def swiglu_grads(sums, saved, where, n, q):
@@ -446,7 +446,7 @@
 
     def chip_sum(n):
         chip = (terms[n][0] + terms[n][1].astype(F32)).astype(BF16)
-        return jnp.pad(chip, ((0, 0), (0, 128)))
+        return chip if n == last else jnp.pad(chip, ((0, 0), (0, 128)))
 
     def grads(n, after):
         sums = terms[n] + others[n]

time: 181 us -> 180 us (level)
  local copies, waits for them, and re-layouts: 5.09 us -> 1.97 us
  Pallas kernels: 118 us -> 120 us
    unnamed x51 -> x55, local copies, waits for them, and re-layouts: 4.89 us -> 1.8 us
    ppermute x6, waiting for transfers between devices: 12.3 us -> 9.76 us  [shift_y(): lax.ppermute(x, 'row', [(r, (r // 2 + s) % ny * 2 + r % 2) for r in range...]
  transfers between devices with their start and end apart: 39 -> 39, of which waited for: 9 -> 13; matrix products, arithmetic and copies ran while one was open for 2% -> 1% of each run, Pallas kernels for 64% -> 66%
where the time goes in v4:
time: 180 us; the launch traced here: 179 us
  Pallas kernels  120 us (67%)
  starting transfers between devices  32.7 us (18%)
  waiting for transfers between devices  20.4 us (11%)
  other arithmetic  2.41 us (1%)
  local copies, waits for them, and re-layouts  1.97 us (1%)
    pallas_call x3, Pallas kernels, weight_grad(): pl.pallas_call(body, grid=(rows // tile,), in_specs=[smem_spec(), smem_sp...  34.2 us
    pallas_call x3, Pallas kernels, input_part(): pl.pallas_call(body, grid=(tiles,), in_specs=[smem_spec(), anywhere, anyw...  27 us
    pallas_call x4, Pallas kernels, hidden_part(): pl.pallas_call(body, grid=(h // tile,), in_specs=[smem_spec(), smem_spec(...  24.3 us
    pallas_call x2, Pallas kernels, turned_weight(): pl.pallas_call(body, grid=(d // tile,), in_specs=[smem_spec(), smem_spec(...  18.5 us
    ppermute x11, starting transfers between devices, from_ahead(): return lax.ppermute(x, ('row', 'col'), back)  14.3 us
    pallas_call x4, Pallas kernels, swiglu_grads(): pl.pallas_call(body, in_specs=[smem_spec()] + [anywhere] * (2 * ns + nt),...  9.98 us
    ppermute x6, waiting for transfers between devices, shift_y(): lax.ppermute(x, 'row', [(r, (r // 2 + s) % ny * 2 + r % 2) for r in range...  9.76 us
    ppermute x6, starting transfers between devices, shift_y(): lax.ppermute(x, 'row', [(r, (r // 2 + s) % ny * 2 + r % 2) for r in range...  8.46 us
  transfers between devices with their start and end apart: 39, of which 13 were waited for; matrix products, arithmetic and copies ran while one was open for 1% of the time, Pallas kernels for 66%

profile of v4, /device:TPU:0, one launch (start us, length us, event | category | flops | bytes accessed | tf_op | source)
XLA Modules:
  0.0 178.8 jit_solution(12829133009791621886)
XLA Ops:
  0.6 3.0 %collective-permute-start.4 = (bf16[256,1792]{1,0:T(8,128)(2,1)}, bf16[256,1792]{1,0:T(8,128)(2,1)S(1)}, u32[]{:S(2)}, u32[]{:S(2)}) collective-permute-start(bf16[256,1792]{1,0:T(8,128)(2,1)} %refs_0_.9), channel_id=1, source_target_pairs={{0,16},{8,24},{16,0},{24,8},{1,17},{9,25},{17,1},{25,9},{2,18},{10... | collective-permute-start | bytes 2752520 | tf_op jit(solution)/shard_map/ppermute | solution.py:415
  3.7 1.5 collective-permute-start.1
  6.5 9.3 %turned_weight.2.wg_ref = bf16[8,1792,256]{2,1,0:T(8,128)(2,1)} custom-call(s32[13]{0:T(128)S(1)} %compare_select_fusion.14.at_ref.i_ref.p_ref, s32[16,14]{1,0:T(8,128)S(1)} %copy-done.17, bf16[2048,1792]{1,0:T(8,128)(2,1)} %w_ref.6), custom_call_target="tpu_custom_call" | custom-call | flops 896 | bytes 3584 | tf_op jit(solution)/shard_map/turned_weight/pallas_call | solution.py:240
  16.8 1.7 collective-permute-done.1.b_ref.refs_2_
  18.6 1.6 collective-permute-start.2
  20.6 6.3 %hidden_part.4 = (f32[128,1792]{1,0:T(8,128)S(1)}, bf16[128,1792]{1,0:T(8,128)(2,1)S(1)}) custom-call(s32[13]{0:T(128)S(1)} %compare_select_fusion.14.at_ref.i_ref.p_ref, s32[14,16]{1,0:T(8,128)S(1)} %copy-done.16, bf16[1792,2048]{1,0:T(8,128)(2,1)} %w_ref.11, bf16[128,2048]{1,0:T(8,128)(2,1)} %collective-permute-done.a_ref.refs_1_, ...), custom_call_target="tpu_custom_call" | custom-call | flops 458752 | bytes 2256 | tf_op jit(solution)/shard_map/hidden_part/pallas_call | solution.py:84
  27.6 9.2 %turned_weight.3.wu_ref = bf16[8,1792,256]{2,1,0:T(8,128)(2,1)} custom-call(s32[13]{0:T(128)S(1)} %compare_select_fusion.14.at_ref.i_ref.p_ref, s32[16,14]{1,0:T(8,128)S(1)} %copy-done.19, bf16[2048,1792]{1,0:T(8,128)(2,1)} %w_ref.8), custom_call_target="tpu_custom_call" | custom-call | flops 896 | bytes 3584 | tf_op jit(solution)/shard_map/turned_weight/pallas_call | solution.py:240
  36.9 7.0 %collective-permute-done.5.refs_5_ = bf16[256,1792]{1,0:T(8,128)(2,1)S(1)} collective-permute-done((bf16[256,1792]{1,0:T(8,128)(2,1)}, bf16[256,1792]{1,0:T(8,128)(2,1)S(1)}, u32[]{:S(2)}, u32[]{:S(2)}) %collective-permute-start.5) | collective-permute-done | bytes 917536 | tf_op jit(solution)/shard_map/ppermute | solution.py:415
  43.9 1.8 %collective-permute-start.8 = (bf16[128,2048]{1,0:T(8,128)(2,1)S(1)}, bf16[128,2048]{1,0:T(8,128)(2,1)S(1)}, u32[]{:S(2)}, u32[]{:S(2)}) collective-permute-start(bf16[128,2048]{1,0:T(8,128)(2,1)S(1)} %collective-permute-done.2.a_ref.refs_3_), channel_id=1, source_target_pairs={{0,2},{1,0},{3,1},{5,3},{7,5},{6,7},{4,6},{2,4},{8,9},{9,11},{11,1... | collective-permute-start | bytes 1572872 | tf_op jit(solution)/shard_map/ppermute | solution.py:406
  46.2 1.8 collective-permute-start.7
  47.9 6.0 %hidden_part.5 = (f32[128,1792]{1,0:T(8,128)S(1)}, bf16[128,1792]{1,0:T(8,128)(2,1)S(1)}) custom-call(s32[13]{0:T(128)S(1)} %compare_select_fusion.14.at_ref.i_ref.p_ref, s32[14,16]{1,0:T(8,128)S(1)} %copy-done.16, bf16[1792,2048]{1,0:T(8,128)(2,1)} %w_ref.11, bf16[128,2048]{1,0:T(8,128)(2,1)S(1)} %collective-permute-done.2.a_ref.refs_3_, ...), custom_call_target="tpu_custom_call" | custom-call | flops 458752 | bytes 2256 | tf_op jit(solution)/shard_map/hidden_part/pallas_call | solution.py:84
  55.9 2.1 %collective-permute-done.7.refs_10_ = bf16[128,1920]{1,0:T(8,128)(2,1)S(1)} collective-permute-done((bf16[128,1920]{1,0:T(8,128)(2,1)S(1)}, bf16[128,1920]{1,0:T(8,128)(2,1)S(1)}, u32[]{:S(2)}, u32[]{:S(2)}) %collective-permute-start.7) | collective-permute-done | bytes 491552 | tf_op jit(solution)/shard_map/ppermute | solution.py:415
  59.7 1.6 collective-permute-start.12
  61.3 6.0 %hidden_part.6 = (f32[128,1792]{1,0:T(8,128)S(1)}, bf16[128,1792]{1,0:T(8,128)(2,1)S(1)}) custom-call(s32[13]{0:T(128)S(1)} %compare_select_fusion.14.at_ref.i_ref.p_ref, s32[14,16]{1,0:T(8,128)S(1)} %copy-done.16, bf16[1792,2048]{1,0:T(8,128)(2,1)} %w_ref.11, bf16[128,2048]{1,0:T(8,128)(2,1)S(1)} %collective-permute-done.8.a_ref.refs_5_, ...), custom_call_target="tpu_custom_call" | custom-call | flops 458752 | bytes 2256 | tf_op jit(solution)/shard_map/hidden_part/pallas_call | solution.py:84
  67.5 6.1 %activation.1.refs_0_ = bf16[1792,1024]{1,0:T(8,128)(2,1)S(1)} custom-call(s32[13]{0:T(128)S(1)} %compare_select_fusion.14.at_ref.i_ref.p_ref, bf16[256,1792]{1,0:T(8,128)(2,1)} %refs_0_.9, bf16[256,1792]{1,0:T(8,128)(2,1)} %refs_1_.9, bf16[256,1792]{1,0:T(8,128)(2,1)S(1)} %collective-permute-done.10.refs_2_, ...), custom_call_target="tpu_custom_call" | custom-call | flops 4480 | bytes 2688 | tf_op jit(solution)/shard_map/activation/pallas_call | solution.py:135
  76.7 6.0 %hidden_part.7 = (f32[128,1792]{1,0:T(8,128)S(1)}, bf16[128,1792]{1,0:T(8,128)(2,1)S(1)}) custom-call(s32[13]{0:T(128)S(1)} %compare_select_fusion.14.at_ref.i_ref.p_ref, s32[14,16]{1,0:T(8,128)S(1)} %copy-done.16, bf16[1792,2048]{1,0:T(8,128)(2,1)} %w_ref.11, bf16[128,2048]{1,0:T(8,128)(2,1)S(1)} %copy-done.11, ...), custom_call_target="tpu_custom_call" | custom-call | flops 458752 | bytes 2256 | tf_op jit(solution)/shard_map/hidden_part/pallas_call | solution.py:84
  82.8 2.4 %swiglu_grads.4.refs_0_.refs_8_ = bf16[2,128,1792]{2,1,0:T(8,128)(2,1)S(1)} custom-call(s32[13]{0:T(128)S(1)} %compare_select_fusion.14.at_ref.i_ref.p_ref, bf16[256,1792]{1,0:T(8,128)(2,1)} %refs_0_.9, bf16[256,1792]{1,0:T(8,128)(2,1)} %refs_1_.9, bf16[256,1792]{1,0:T(8,128)(2,1)} %copy-done.2, bf16[256,1792]{1,0:T(8,128)(2,1)} %copy-done.3, ...), custom_call_target="tpu_custom_call" | custom-call | flops 1120 | bytes 784 | tf_op jit(solution)/shard_map/swiglu_grads/pallas_call | solution.py:205
  85.8 2.4 %swiglu_grads.5.refs_2_.refs_10_ = bf16[2,128,1792]{2,1,0:T(8,128)(2,1)S(1)} custom-call(s32[13]{0:T(128)S(1)} %compare_select_fusion.14.at_ref.i_ref.p_ref, bf16[256,1792]{1,0:T(8,128)(2,1)} %refs_0_.9, bf16[256,1792]{1,0:T(8,128)(2,1)} %refs_1_.9, bf16[256,1792]{1,0:T(8,128)(2,1)} %copy-done.2, bf16[256,1792]{1,0:T(8,128)(2,1)} %copy-done.3, ...), custom_call_target="tpu_custom_call" | custom-call | flops 1120 | bytes 784 | tf_op jit(solution)/shard_map/swiglu_grads/pallas_call | solution.py:205
  88.4 1.6 collective-permute-start.21
  91.7 11.5 %weight_grad.3 = bf16[1792,2048]{1,0:T(8,128)(2,1)} custom-call(s32[14,16]{1,0:T(8,128)S(1)} %copy-done.16, s32[13]{0:T(128)S(1)} %compare_select_fusion.14.at_ref.i_ref.p_ref, bf16[1792,1024]{1,0:T(8,128)(2,1)S(1)} %activation.1.refs_0_, bf16[128,2048]{1,0:T(8,128)(2,1)} %collective-permute-done.a_ref.refs_1_, ...), custom_call_target="tpu_custom_call" | custom-call | flops 1835008 | bytes 3712 | tf_op jit(solution)/shard_map/weight_grad/pallas_call | solution.py:352
  103.6 2.4 %swiglu_grads.6.refs_0_.refs_14_ = bf16[2,128,1792]{2,1,0:T(8,128)(2,1)S(1)} custom-call(s32[13]{0:T(128)S(1)} %compare_select_fusion.14.at_ref.i_ref.p_ref, bf16[256,1792]{1,0:T(8,128)(2,1)} %refs_0_.9, bf16[256,1792]{1,0:T(8,128)(2,1)} %refs_1_.9, bf16[256,1792]{1,0:T(8,128)(2,1)} %copy-done.2, bf16[256,1792]{1,0:T(8,128)(2,1)} %copy-done.3, ...), custom_call_target="tpu_custom_call" | custom-call | flops 1120 | bytes 784 | tf_op jit(solution)/shard_map/swiglu_grads/pallas_call | solution.py:205
  106.2 1.6 collective-permute-start.28
  108.2 2.8 %swiglu_grads.7.refs_0_.refs_12_ = bf16[2,128,1792]{2,1,0:T(8,128)(2,1)S(1)} custom-call(s32[13]{0:T(128)S(1)} %compare_select_fusion.14.at_ref.i_ref.p_ref, bf16[256,1792]{1,0:T(8,128)(2,1)} %refs_0_.9, bf16[256,1792]{1,0:T(8,128)(2,1)} %refs_1_.9, bf16[256,1792]{1,0:T(8,128)(2,1)} %copy-done.2, bf16[256,1792]{1,0:T(8,128)(2,1)} %copy-done.3, ...), custom_call_target="tpu_custom_call" | custom-call | flops 1120 | bytes 784 | tf_op jit(solution)/shard_map/swiglu_grads/pallas_call | solution.py:205
  111.1 8.2 %input_part.3 = f32[2,128,2048]{2,1,0:T(8,128)S(1)} custom-call(s32[13]{0:T(128)S(1)} %compare_select_fusion.14.at_ref.i_ref.p_ref, bf16[8,1792,256]{2,1,0:T(8,128)(2,1)} %turned_weight.2.wg_ref, bf16[8,1792,256]{2,1,0:T(8,128)(2,1)} %turned_weight.3.wu_ref, bf16[2,128,1792]{2,1,0:T(8,128)(2,1)S(1)} %swiglu_grads.6.refs_0_.refs_14_, ...), custom_call_target="tpu_custom_call" | custom-call | flops 917504 | bytes 4544 | tf_op jit(solution)/shard_map/input_part/pallas_call | solution.py:284
  122.8 7.5 %input_part.4 = f32[2,128,2048]{2,1,0:T(8,128)S(1)} custom-call(s32[13]{0:T(128)S(1)} %compare_select_fusion.14.at_ref.i_ref.p_ref, bf16[8,1792,256]{2,1,0:T(8,128)(2,1)} %turned_weight.2.wg_ref, bf16[8,1792,256]{2,1,0:T(8,128)(2,1)} %turned_weight.3.wu_ref, bf16[2,128,1792]{2,1,0:T(8,128)(2,1)S(1)} %swiglu_grads.7.refs_0_.refs_12_, ...), custom_call_target="tpu_custom_call" | custom-call | flops 917504 | bytes 4544 | tf_op jit(solution)/shard_map/input_part/pallas_call | solution.py:284
  130.3 4.9 %collective-permute-done.30 = bf16[128,2048]{1,0:T(8,128)(2,1)S(1)} collective-permute-done((bf16[128,2048]{1,0:T(8,128)(2,1)S(1)}, bf16[128,2048]{1,0:T(8,128)(2,1)S(1)}, u32[]{:S(2)}, u32[]{:S(2)}) %collective-permute-start.30) | collective-permute-done | bytes 524320 | tf_op jit(solution)/shard_map/ppermute | solution.py:409
  135.4 1.8 collective-permute-start.33
  137.5 11.4 %input_part.5 = f32[4,128,2048]{2,1,0:T(8,128)S(1)} custom-call(s32[13]{0:T(128)S(1)} %compare_select_fusion.14.at_ref.i_ref.p_ref, bf16[8,1792,256]{2,1,0:T(8,128)(2,1)} %turned_weight.2.wg_ref, bf16[8,1792,256]{2,1,0:T(8,128)(2,1)} %turned_weight.3.wu_ref, bf16[2,128,1792]{2,1,0:T(8,128)(2,1)S(1)} %swiglu_grads.4.refs_0_.refs_8_, ...), custom_call_target="tpu_custom_call" | custom-call | flops 1835008 | bytes 5504 | tf_op jit(solution)/shard_map/input_part/pallas_call | solution.py:284
  149.4 1.8 collective-permute-start.36
  151.5 11.4 %weight_grad.4 = bf16[2048,1792]{1,0:T(8,128)(2,1)} custom-call(s32[16,14]{1,0:T(8,128)S(1)} %copy-done.18, s32[13]{0:T(128)S(1)} %compare_select_fusion.14.at_ref.i_ref.p_ref, bf16[2048,128]{1,0:T(8,128)(2,1)S(1)} %copy-done.15, bf16[2048,128]{1,0:T(8,128)(2,1)S(1)} %copy-done.13, bf16[2048,128]{1,0:T(8,128)(2,1)} %collective-permute-done.21.refs_2_, ...), custom_call_target="tpu_custom_call" | custom-call | flops 1835008 | bytes 3712 | tf_op jit(solution)/shard_map/weight_grad/pallas_call | solution.py:352
  164.0 1.8 %collective-permute-start.37 = (bf16[128,2048]{1,0:T(8,128)(2,1)S(1)}, bf16[128,2048]{1,0:T(8,128)(2,1)S(1)}, u32[]{:S(2)}, u32[]{:S(2)}) collective-permute-start(bf16[128,2048]{1,0:T(8,128)(2,1)S(1)} %get-tuple-element.170), channel_id=1, source_target_pairs={{0,1},{1,3},{3,5},{5,7},{7,6},{6,4},{4,2},{2,0},{8,10},{9,8},{11,9... | collective-permute-start | bytes 1572872 | tf_op jit(solution)/shard_map/ppermute | solution.py:409
  166.1 11.3 %weight_grad.5 = bf16[2048,1792]{1,0:T(8,128)(2,1)} custom-call(s32[16,14]{1,0:T(8,128)S(1)} %copy-done.19, s32[13]{0:T(128)S(1)} %compare_select_fusion.14.at_ref.i_ref.p_ref, bf16[2048,128]{1,0:T(8,128)(2,1)S(1)} %copy-done.15, bf16[2048,128]{1,0:T(8,128)(2,1)S(1)} %copy-done.13, bf16[2048,128]{1,0:T(8,128)(2,1)} %collective-permute-done.21.refs_2_, ...), custom_call_target="tpu_custom_call" | custom-call | flops 1835008 | bytes 3712 | tf_op jit(solution)/shard_map/weight_grad/pallas_call | solution.py:352
  (133 shorter events, 21.7 us)
Async XLA Ops:
  0.6 26.4 %collective-permute-start.4 = (bf16[256,1792]{1,0:T(8,128)(2,1)}, bf16[256,1792]{1,0:T(8,128)(2,1)S(1)}, u32[]{:S(2)}, u32[]{:S(2)}) collective-permute-start(bf16[256,1792]{1,0:T(8,128)(2,1)} %refs_0_.9), channel_id=1, source_target_pairs={{0,16},{8,24},{16,0},{24,8},{1,17},{9,25},{17,1},{25,9},{2,18},{10... | collective-permute-start | bytes 2752520 | tf_op jit(solution)/shard_map/ppermute | solution.py:415
  3.7 14.9 %collective-permute-start.1 = (bf16[128,2048]{1,0:T(8,128)(2,1)}, bf16[128,2048]{1,0:T(8,128)(2,1)S(1)}, u32[]{:S(2)}, u32[]{:S(2)}) collective-permute-start(bf16[128,2048]{1,0:T(8,128)(2,1)} %refs_7_.1), channel_id=1, source_target_pairs={{0,1},{1,3},{3,5},{5,7},{7,6},{6,4},{4,2},{2,0},{8,10},{9,8},{11,9... | collective-permute-start | bytes 1572872 | tf_op jit(solution)/shard_map/ppermute | solution.py:409
  5.2 13.4 %collective-permute-start = (bf16[128,2048]{1,0:T(8,128)(2,1)}, bf16[128,2048]{1,0:T(8,128)(2,1)}, u32[]{:S(2)}, u32[]{:S(2)}) collective-permute-start(bf16[128,2048]{1,0:T(8,128)(2,1)} %refs_7_.1), channel_id=1, source_target_pairs={{0,2},{1,0},{3,1},{5,3},{7,5},{6,7},{4,6},{2,4},{8,9},{9,11},{11,1... | collective-permute-start | bytes 1572872 | tf_op jit(solution)/shard_map/ppermute | solution.py:406
  5.7 38.2 %collective-permute-start.5 = (bf16[256,1792]{1,0:T(8,128)(2,1)}, bf16[256,1792]{1,0:T(8,128)(2,1)S(1)}, u32[]{:S(2)}, u32[]{:S(2)}) collective-permute-start(bf16[256,1792]{1,0:T(8,128)(2,1)} %refs_1_.9), channel_id=1, source_target_pairs={{0,16},{8,24},{16,0},{24,8},{1,17},{9,25},{17,1},{25,9},{2,18},{10... | collective-permute-start | bytes 2752520 | tf_op jit(solution)/shard_map/ppermute | solution.py:415
  18.6 25.3 %collective-permute-start.2 = (bf16[128,2048]{1,0:T(8,128)(2,1)}, bf16[128,2048]{1,0:T(8,128)(2,1)S(1)}, u32[]{:S(2)}, u32[]{:S(2)}) collective-permute-start(bf16[128,2048]{1,0:T(8,128)(2,1)} %collective-permute-done.a_ref.refs_1_), channel_id=1, source_target_pairs={{0,2},{1,0},{3,1},{5,3},{7,5},{6,7},{4,6},{2,4},{8,9},{9,11},{11,1... | collective-permute-start | bytes 1572872 | tf_op jit(solution)/shard_map/ppermute | solution.py:406
  20.2 23.7 %collective-permute-start.3 = (bf16[128,2048]{1,0:T(8,128)(2,1)S(1)}, bf16[128,2048]{1,0:T(8,128)(2,1)S(1)}, u32[]{:S(2)}, u32[]{:S(2)}) collective-permute-start(bf16[128,2048]{1,0:T(8,128)(2,1)S(1)} %collective-permute-done.1.b_ref.refs_2_), channel_id=1, source_target_pairs={{0,1},{1,3},{3,5},{5,7},{7,6},{6,4},{4,2},{2,0},{8,10},{9,8},{11,9... | collective-permute-start | bytes 1572872 | tf_op jit(solution)/shard_map/ppermute | solution.py:409
  27.0 16.9 %collective-permute-start.6 = (bf16[128,1792]{1,0:T(8,128)(2,1)S(1)}, bf16[128,1792]{1,0:T(8,128)(2,1)S(1)}, u32[]{:S(2)}, u32[]{:S(2)}) collective-permute-start(bf16[128,1792]{1,0:T(8,128)(2,1)S(1)} %get-tuple-element.92), channel_id=1, source_target_pairs={{0,8},{8,0},{16,24},{24,16},{1,9},{9,1},{17,25},{25,17},{2,10},{10... | collective-permute-start | bytes 1376264 | tf_op jit(solution)/shard_map/ppermute | solution.py:412
  27.1 26.9 %collective-permute-start.10 = (bf16[256,1792]{1,0:T(8,128)(2,1)S(1)}, bf16[256,1792]{1,0:T(8,128)(2,1)S(1)}, u32[]{:S(2)}, u32[]{:S(2)}) collective-permute-start(bf16[256,1792]{1,0:T(8,128)(2,1)S(1)} %copy-done.20), channel_id=1, source_target_pairs={{0,8},{8,0},{16,24},{24,16},{1,9},{9,1},{17,25},{25,17},{2,10},{10... | collective-permute-start | bytes 2752520 | tf_op jit(solution)/shard_map/ppermute | solution.py:412
  43.9 14.3 %collective-permute-start.8 = (bf16[128,2048]{1,0:T(8,128)(2,1)S(1)}, bf16[128,2048]{1,0:T(8,128)(2,1)S(1)}, u32[]{:S(2)}, u32[]{:S(2)}) collective-permute-start(bf16[128,2048]{1,0:T(8,128)(2,1)S(1)} %collective-permute-done.2.a_ref.refs_3_), channel_id=1, source_target_pairs={{0,2},{1,0},{3,1},{5,3},{7,5},{6,7},{4,6},{2,4},{8,9},{9,11},{11,1... | collective-permute-start | bytes 1572872 | tf_op jit(solution)/shard_map/ppermute | solution.py:406
  45.8 12.4 %collective-permute-start.9 = (bf16[128,2048]{1,0:T(8,128)(2,1)S(1)}, bf16[128,2048]{1,0:T(8,128)(2,1)S(1)}, u32[]{:S(2)}, u32[]{:S(2)}) collective-permute-start(bf16[128,2048]{1,0:T(8,128)(2,1)S(1)} %collective-permute-done.3.b_ref.refs_4_), channel_id=1, source_target_pairs={{0,1},{1,3},{3,5},{5,7},{7,6},{6,4},{4,2},{2,0},{8,10},{9,8},{11,9... | collective-permute-start | bytes 1572872 | tf_op jit(solution)/shard_map/ppermute | solution.py:409
  46.2 11.9 %collective-permute-start.7 = (bf16[128,1920]{1,0:T(8,128)(2,1)S(1)}, bf16[128,1920]{1,0:T(8,128)(2,1)S(1)}, u32[]{:S(2)}, u32[]{:S(2)}) collective-permute-start(bf16[128,1920]{1,0:T(8,128)(2,1)S(1)} %pad.10), channel_id=1, source_target_pairs={{0,16},{8,24},{16,0},{24,8},{1,17},{9,25},{17,1},{25,9},{2,18},{10... | collective-permute-start | bytes 1474568 | tf_op jit(solution)/shard_map/ppermute | solution.py:415
  54.0 13.3 %collective-permute-start.14 = (bf16[256,1792]{1,0:T(8,128)(2,1)S(1)}, bf16[256,1792]{1,0:T(8,128)(2,1)S(1)}, u32[]{:S(2)}, u32[]{:S(2)}) collective-permute-start(bf16[256,1792]{1,0:T(8,128)(2,1)S(1)} %copy-done.21), channel_id=1, source_target_pairs={{0,8},{8,0},{16,24},{24,16},{1,9},{9,1},{17,25},{25,17},{2,10},{10... | collective-permute-start | bytes 2752520 | tf_op jit(solution)/shard_map/ppermute | solution.py:412
  58.2 15.4 %collective-permute-start.13 = (bf16[128,2048]{1,0:T(8,128)(2,1)S(1)}, bf16[128,2048]{1,0:T(8,128)(2,1)S(1)}, u32[]{:S(2)}, u32[]{:S(2)}) collective-permute-start(bf16[128,2048]{1,0:T(8,128)(2,1)S(1)} %collective-permute-done.8.a_ref.refs_5_), channel_id=1, source_target_pairs={{0,2},{1,0},{3,1},{5,3},{7,5},{6,7},{4,6},{2,4},{8,9},{9,11},{11,1... | collective-permute-start | bytes 1572872 | tf_op jit(solution)/shard_map/ppermute | solution.py:406
  59.7 13.9 %collective-permute-start.12 = (bf16[128,1920]{1,0:T(8,128)(2,1)S(1)}, bf16[128,1920]{1,0:T(8,128)(2,1)S(1)}, u32[]{:S(2)}, u32[]{:S(2)}) collective-permute-start(bf16[128,1920]{1,0:T(8,128)(2,1)S(1)} %pad.11), channel_id=1, source_target_pairs={{0,16},{8,24},{16,0},{24,8},{1,17},{9,25},{17,1},{25,9},{2,18},{10... | collective-permute-start | bytes 1474568 | tf_op jit(solution)/shard_map/ppermute | solution.py:415
  73.6 14.8 %collective-permute-start.19 = (bf16[2048,128]{1,0:T(8,128)(2,1)S(1)}, bf16[2048,128]{1,0:T(8,128)(2,1)S(1)}, u32[]{:S(2)}, u32[]{:S(2)}) collective-permute-start(bf16[2048,128]{1,0:T(8,128)(2,1)S(1)} %bitcast.31), channel_id=1, source_target_pairs={{0,1},{1,3},{3,5},{5,7},{7,6},{6,4},{4,2},{2,0},{8,10},{9,8},{11,9... | collective-permute-start | bytes 1572872 | tf_op jit(solution)/shard_map/ppermute | solution.py:409
  74.5 13.9 %collective-permute-start.18 = (bf16[2048,128]{1,0:T(8,128)(2,1)S(1)}, bf16[2048,128]{1,0:T(8,128)(2,1)S(1)}, u32[]{:S(2)}, u32[]{:S(2)}) collective-permute-start(bf16[2048,128]{1,0:T(8,128)(2,1)S(1)} %bitcast.32), channel_id=1, source_target_pairs={{0,2},{1,0},{3,1},{5,3},{7,5},{6,7},{4,6},{2,4},{8,9},{9,11},{11,1... | collective-permute-start | bytes 1572872 | tf_op jit(solution)/shard_map/ppermute | solution.py:406
  75.8 12.6 %collective-permute-start.20 = (bf16[128,1920]{1,0:T(8,128)(2,1)S(1)}, bf16[128,1920]{1,0:T(8,128)(2,1)S(1)}, u32[]{:S(2)}, u32[]{:S(2)}) collective-permute-start(bf16[128,1920]{1,0:T(8,128)(2,1)S(1)} %pad.12), channel_id=1, source_target_pairs={{0,16},{8,24},{16,0},{24,8},{1,17},{9,25},{17,1},{25,9},{2,18},{10... | collective-permute-start | bytes 1474568 | tf_op jit(solution)/shard_map/ppermute | solution.py:415
  85.2 18.3 %collective-permute-start.25 = (bf16[2,128,1792]{2,1,0:T(8,128)(2,1)S(1)}, bf16[2,128,1792]{2,1,0:T(8,128)(2,1)S(1)}, u32[]{:S(2)}, u32[]{:S(2)}) collective-permute-start(bf16[2,128,1792]{2,1,0:T(8,128)(2,1)S(1)} %swiglu_grads.4.refs_0_.refs_8_), channel_id=1, source_target_pairs={{0,8},{8,0},{16,24},{24,16},{1,9},{9,1},{17,25},{25,17},{2,10},{10... | collective-permute-start | bytes 2752520 | tf_op jit(solution)/shard_map/ppermute | solution.py:412
  88.4 15.2 %collective-permute-start.21 = (bf16[2048,128]{1,0:T(8,128)(2,1)S(1)}, bf16[2048,128]{1,0:T(8,128)(2,1)}, u32[]{:S(2)}, u32[]{:S(2)}) collective-permute-start(bf16[2048,128]{1,0:T(8,128)(2,1)S(1)} %collective-permute-done.18.refs_0_), channel_id=1, source_target_pairs={{0,2},{1,0},{3,1},{5,3},{7,5},{6,7},{4,6},{2,4},{8,9},{9,11},{11,1... | collective-permute-start | bytes 1572872 | tf_op jit(solution)/shard_map/ppermute | solution.py:406
  90.0 13.6 %collective-permute-start.22 = (bf16[2048,128]{1,0:T(8,128)(2,1)S(1)}, bf16[2048,128]{1,0:T(8,128)(2,1)}, u32[]{:S(2)}, u32[]{:S(2)}) collective-permute-start(bf16[2048,128]{1,0:T(8,128)(2,1)S(1)} %collective-permute-done.19.refs_1_), channel_id=1, source_target_pairs={{0,1},{1,3},{3,5},{5,7},{7,6},{6,4},{4,2},{2,0},{8,10},{9,8},{11,9... | collective-permute-start | bytes 1572872 | tf_op jit(solution)/shard_map/ppermute | solution.py:409
  90.5 13.1 %collective-permute-start.26 = (bf16[2,128,1792]{2,1,0:T(8,128)(2,1)S(1)}, bf16[2,128,1792]{2,1,0:T(8,128)(2,1)S(1)}, u32[]{:S(2)}, u32[]{:S(2)}) collective-permute-start(bf16[2,128,1792]{2,1,0:T(8,128)(2,1)S(1)} %swiglu_grads.5.refs_2_.refs_10_), channel_id=1, source_target_pairs={{0,8},{8,0},{16,24},{24,16},{1,9},{9,1},{17,25},{25,17},{2,10},{10... | collective-permute-start | bytes 2752520 | tf_op jit(solution)/shard_map/ppermute | solution.py:412
  90.6 13.0 %collective-permute-start.24 = (bf16[128,1792]{1,0:T(8,128)(2,1)S(1)}, bf16[128,1792]{1,0:T(8,128)(2,1)S(1)}, u32[]{:S(2)}, u32[]{:S(2)}) collective-permute-start(bf16[128,1792]{1,0:T(8,128)(2,1)S(1)} %add_convert_fusion), channel_id=1, source_target_pairs={{0,16},{8,24},{16,0},{24,8},{1,17},{9,25},{17,1},{25,9},{2,18},{10... | collective-permute-start | bytes 1376264 | tf_op jit(solution)/shard_map/ppermute | solution.py:415
  106.2 14.5 %collective-permute-start.28 = (bf16[2048,128]{1,0:T(8,128)(2,1)}, bf16[2048,128]{1,0:T(8,128)(2,1)S(1)}, u32[]{:S(2)}, u32[]{:S(2)}) collective-permute-start(bf16[2048,128]{1,0:T(8,128)(2,1)} %collective-permute-done.21.refs_2_), channel_id=1, source_target_pairs={{0,2},{1,0},{3,1},{5,3},{7,5},{6,7},{4,6},{2,4},{8,9},{9,11},{11,1... | collective-permute-start | bytes 1572872 | tf_op jit(solution)/shard_map/ppermute | solution.py:406
  107.8 13.0 %collective-permute-start.29 = (bf16[2048,128]{1,0:T(8,128)(2,1)}, bf16[2048,128]{1,0:T(8,128)(2,1)}, u32[]{:S(2)}, u32[]{:S(2)}) collective-permute-start(bf16[2048,128]{1,0:T(8,128)(2,1)} %collective-permute-done.22.refs_3_), channel_id=1, source_target_pairs={{0,1},{1,3},{3,5},{5,7},{7,6},{6,4},{4,2},{2,0},{8,10},{9,8},{11,9... | collective-permute-start | bytes 1572872 | tf_op jit(solution)/shard_map/ppermute | solution.py:409
  120.8 14.5 %collective-permute-start.30 = (bf16[128,2048]{1,0:T(8,128)(2,1)S(1)}, bf16[128,2048]{1,0:T(8,128)(2,1)S(1)}, u32[]{:S(2)}, u32[]{:S(2)}) collective-permute-start(bf16[128,2048]{1,0:T(8,128)(2,1)S(1)} %fusion.7), channel_id=1, source_target_pairs={{0,1},{1,3},{3,5},{5,7},{7,6},{6,4},{4,2},{2,0},{8,10},{9,8},{11,9... | collective-permute-start | bytes 1572872 | tf_op jit(solution)/shard_map/ppermute | solution.py:409
  122.2 26.7 %collective-permute-start.34 = (bf16[2048,128]{1,0:T(8,128)(2,1)S(1)}, bf16[2048,128]{1,0:T(8,128)(2,1)S(1)}, u32[]{:S(2)}, u32[]{:S(2)}) collective-permute-start(bf16[2048,128]{1,0:T(8,128)(2,1)S(1)} %collective-permute-done.28.refs_4_), channel_id=1, source_target_pairs={{0,2},{1,0},{3,1},{5,3},{7,5},{6,7},{4,6},{2,4},{8,9},{9,11},{11,1... | collective-permute-start | bytes 1572872 | tf_op jit(solution)/shard_map/ppermute | solution.py:406
  135.4 13.6 %collective-permute-start.33 = (bf16[128,2048]{1,0:T(8,128)(2,1)S(1)}, bf16[128,2048]{1,0:T(8,128)(2,1)S(1)}, u32[]{:S(2)}, u32[]{:S(2)}) collective-permute-start(bf16[128,2048]{1,0:T(8,128)(2,1)S(1)} %fusion.8), channel_id=1, source_target_pairs={{0,2},{1,0},{3,1},{5,3},{7,5},{6,7},{4,6},{2,4},{8,9},{9,11},{11,1... | collective-permute-start | bytes 1572872 | tf_op jit(solution)/shard_map/ppermute | solution.py:406
  137.2 11.9 %collective-permute-start.32 = (bf16[128,2048]{1,0:T(8,128)(2,1)S(1)}, bf16[128,2048]{1,0:T(8,128)(2,1)S(1)}, u32[]{:S(2)}, u32[]{:S(2)}) collective-permute-start(bf16[128,2048]{1,0:T(8,128)(2,1)S(1)} %fusion.4), channel_id=1, source_target_pairs={{0,1},{1,3},{3,5},{5,7},{7,6},{6,4},{4,2},{2,0},{8,10},{9,8},{11,9... | collective-permute-start | bytes 1572872 | tf_op jit(solution)/shard_map/ppermute | solution.py:409
  149.4 14.2 %collective-permute-start.36 = (bf16[128,2048]{1,0:T(8,128)(2,1)S(1)}, bf16[128,2048]{1,0:T(8,128)(2,1)S(1)}, u32[]{:S(2)}, u32[]{:S(2)}) collective-permute-start(bf16[128,2048]{1,0:T(8,128)(2,1)S(1)} %get-tuple-element.172), channel_id=1, source_target_pairs={{0,2},{1,0},{3,1},{5,3},{7,5},{6,7},{4,6},{2,4},{8,9},{9,11},{11,1... | collective-permute-start | bytes 1572872 | tf_op jit(solution)/shard_map/ppermute | solution.py:406
  151.2 12.5 %collective-permute-start.35 = (bf16[128,2048]{1,0:T(8,128)(2,1)S(1)}, bf16[128,2048]{1,0:T(8,128)(2,1)S(1)}, u32[]{:S(2)}, u32[]{:S(2)}) collective-permute-start(bf16[128,2048]{1,0:T(8,128)(2,1)S(1)} %get-tuple-element.173), channel_id=1, source_target_pairs={{0,1},{1,3},{3,5},{5,7},{7,6},{6,4},{4,2},{2,0},{8,10},{9,8},{11,9... | collective-permute-start | bytes 1572872 | tf_op jit(solution)/shard_map/ppermute | solution.py:409
  164.0 13.5 %collective-permute-start.37 = (bf16[128,2048]{1,0:T(8,128)(2,1)S(1)}, bf16[128,2048]{1,0:T(8,128)(2,1)S(1)}, u32[]{:S(2)}, u32[]{:S(2)}) collective-permute-start(bf16[128,2048]{1,0:T(8,128)(2,1)S(1)} %get-tuple-element.170), channel_id=1, source_target_pairs={{0,1},{1,3},{3,5},{5,7},{7,6},{6,4},{4,2},{2,0},{8,10},{9,8},{11,9... | collective-permute-start | bytes 1572872 | tf_op jit(solution)/shard_map/ppermute | solution.py:409
  165.8 11.9 %collective-permute-start.38 = (bf16[128,2048]{1,0:T(8,128)(2,1)S(1)}, bf16[128,2048]{1,0:T(8,128)(2,1)S(1)}, u32[]{:S(2)}, u32[]{:S(2)}) collective-permute-start(bf16[128,2048]{1,0:T(8,128)(2,1)S(1)} %get-tuple-element.171), channel_id=1, source_target_pairs={{0,2},{1,0},{3,1},{5,3},{7,5},{6,7},{4,6},{2,4},{8,9},{9,11},{11,1... | collective-permute-start | bytes 1572872 | tf_op jit(solution)/shard_map/ppermute | solution.py:406
  (34 other events, 326.5 us)
